TPU v7x, 32 devices: a whole 2x2x4 slice. The times are simulated.
32 devices in a mesh: case: 2 (over x), elem: 16 (over z, y, core).
Axes of the slice: x: 2, y: 2, z: 4, core: 2. Of those that a mesh axis runs over, the one named last changes fastest.
Arguments:
- records: bfloat16 [32768, 128], P(('case', 'elem')), parts along dimension 0, may hold values from -6 to 6
- panel_owner: int32 [16384, 1], P('elem'), may hold values from 0 to 15; in each aligned block of 1024 rows (0 to 1023, 1024 to 2047, ...) at most 128 rows name the same one
- panel_slot: int32 [16384], P('elem'), may hold values from 0 to 3071
- stiff_blocks: bfloat16 [512, 3, 96, 96], P('elem'), may hold values from -0.375 to 0.375
- block_cols: int32 [512, 3], P('elem'), may hold values from 0 to 511, as said below
- modes: bfloat16 [49152, 1024], P('elem'), may hold values from -0.02734375 to 0.02734375
- admittance: float32 [2048, 1024], P('case'), parts along dimension 0, may hold values from -3 to 3
Outputs:
- adjoint: bfloat16 [98304, 128], P(('case', 'elem')), parts along dimension 0
- sensitivity: float32 [98304], P(('case', 'elem')), parts along dimension 0
There are 2 independent parts, one for each index of `case`. A program takes and returns all parts, laid end to end along the dimension named above; an argument that names none is the same for every part. Nothing has to cross between parts.
Inputs may be any that keep to these rules, and one draw needn't show every extreme that they name: `panel_owner`: among the 1024 panels of one device no owner appears more than 128 times, and in some device's panels some owner appears exactly 128 times. `block_cols`: each stored block's column block lies within 8 blocks of its row block; column 0 lies exactly 8 blocks away unless the grid's end clips it.
All inputs are finite; a program needn't handle non-finite values.
Results may differ from a plain program's by a relative error of at most 0.0062.
Values may be sent and summed in bfloat16 or wider, within the bound.
No kernel may reach another device: no remote copies, remote signals or barrier semaphores. Data moves between devices by JAX's collectives and lax.ppermute only.
A program may use at most 64 MiB of HBM per device.

v0:
```python
import jax
import jax.numpy as jnp
from jax import lax
from jax.sharding import PartitionSpec as P


def with_halo(array, sides, width):
    for axis, dim in sides:
        size, length = (lax.axis_size(axis), array.shape[dim])
        up = [(i, (i + 1) % size) for i in range(size - 1)]
        down = [(j, i) for i, j in up]
        last = lax.slice_in_dim(array, length - width, length, axis=dim)
        initial = lax.slice_in_dim(array, 0, width, axis=dim)
        before = lax.ppermute(last, axis, up)
        after = lax.ppermute(initial, axis, down)
        array = jnp.concatenate([before, array, after], axis=dim)
    return array


def body(records, panel_owner, panel_slot, stiff_blocks, block_cols, modes, admittance):
    owners = lax.axis_size("elem")
    my_index = lax.axis_index("elem")
    pan_rows, record_width = records.shape
    capacity = 2 * pan_rows // owners
    elem_rows = modes.shape[0]
    blk_rows = stiff_blocks.shape[0]
    blk_size = stiff_blocks.shape[2]
    owner_list = panel_owner[:, 0]
    panel_order = jnp.argsort(owner_list, stable=True)
    sorted_owner = owner_list[panel_order]
    counts = jnp.sum(
        (owner_list[:, None] == jnp.arange(owners, dtype=jnp.int32)[None, :]).astype(jnp.int32),
        axis=0,
    )
    starts = jnp.cumsum(counts) - counts
    slot_rank = jnp.arange(pan_rows, dtype=jnp.int32) - starts[sorted_owner]
    target = sorted_owner * capacity + slot_rank
    send_rec = (
        jnp.zeros((owners * capacity, record_width), records.dtype)
        .at[target]
        .set(records[panel_order])
    )
    send_slot = (
        jnp.full((owners * capacity,), elem_rows, jnp.int32).at[target].set(panel_slot[panel_order])
    )
    got_rec, got_slot = (
        lax.all_to_all(
            send_rec.reshape(owners, capacity, record_width),
            "elem",
            split_axis=0,
            concat_axis=0,
            tiled=True,
        ),
        lax.all_to_all(
            send_slot.reshape(owners, capacity), "elem", split_axis=0, concat_axis=0, tiled=True
        ),
    )
    summed = (
        jnp.zeros((elem_rows + 1, record_width), jnp.float32)
        .at[got_slot.reshape(-1)]
        .add(got_rec.reshape(-1, record_width).astype(jnp.float32))
    )
    elem_load = summed[:elem_rows].astype(jnp.bfloat16)
    extended = with_halo(elem_load, (("elem", 0),), elem_rows)
    ext_blocks = extended.reshape(-1, blk_size, record_width)
    local_cols = block_cols - (my_index * blk_rows - blk_rows)
    picked = ext_blocks[local_cols]
    stiff_out = jnp.einsum(
        "bjrs,bjsc->brc", stiff_blocks, picked, preferred_element_type=jnp.float32
    )
    stiff_out = stiff_out.reshape(elem_rows, record_width).astype(jnp.bfloat16)
    partial_value = lax.dot_general(
        modes, stiff_out, (((0,), (0,)), ((), ())), preferred_element_type=jnp.float32
    )
    modal = lax.psum(partial_value, "elem")
    mode_share = admittance.shape[0] // owners
    admit_rows = lax.dynamic_slice_in_dim(admittance, my_index * mode_share, mode_share, 0)
    adj_rows = jnp.dot(admit_rows, modal, precision=lax.Precision.HIGHEST).astype(jnp.bfloat16)
    adjoint = jnp.dot(
        modes,
        lax.all_gather(adj_rows, "elem", axis=0, tiled=True),
        preferred_element_type=jnp.float32,
    )
    sensitivity = jnp.sum(adjoint * stiff_out.astype(jnp.float32), axis=1)
    return (adjoint.astype(jnp.bfloat16), sensitivity)


def solution(mesh):
    in_specs = (
        P(("case", "elem"), None),
        P("elem", None),
        P("elem"),
        P("elem", None, None, None),
        P("elem", None),
        P("elem", None),
        P("case", None),
    )
    out_specs = (P(("case", "elem"), None), P(("case", "elem")))
    return jax.shard_map(body, mesh=mesh, in_specs=in_specs, out_specs=out_specs, check_vma=False)
```

profile of v0, /device:TPU:0, one launch (start us, length us, event | category | flops | bytes accessed | tf_op | source)
XLA Modules:
  0.0 259.9 jit_solution(5559056118627392330)
XLA Ops:
  8.2 5.1 %sort.17 = (s32[1024]{0:T(1024)}, s32[1024]{0:T(1024)S(1)}) sort(s32[1024]{0:T(1024)} %bitcast.51, s32[1024]{0:T(1024)S(1)} %iota.12), dimensions={0}, to_apply=%region_0.0 | sort | flops 10240 | bytes 16384 | tf_op jit(solution)/shard_map/jit(argsort)/sort | solution.py:29
  13.2 4.5 %gather_fusion = s32[1024]{0:T(1024)S(1)} fusion(s32[1024]{0:T(1024)S(1)} %bitcast.52, s32[1024]{0:T(1024)S(1)} %fusion.7), kind=kCustom, calls=%fused_computation | custom fusion | bytes 12288 | tf_op jit(solution)/shard_map/gather | solution.py:30
  17.8 4.5 %gather_fusion.1 = s32[1024]{0:T(1024)S(1)} fusion(s32[1024]{0:T(1024)S(1)} %copy-done.2, s32[1024]{0:T(1024)S(1)} %fusion.7), kind=kCustom, calls=%fused_computation.1 | custom fusion | bytes 12288 | tf_op jit(solution)/shard_map/gather | solution.py:44
  23.3 4.4 %compare_select_fusion.3 = (s32[1024,1]{0,1:T(1,128)S(1)}, s32[1024,1]{0,1:T(1,128)S(1)}) fusion(s32[]{:T(128)} %bitcast.12, s32[]{:T(128)} %bitcast.13, s32[]{:T(128)} %bitcast.14, s32[]{:T(128)} %bitcast.15, s32[]{:T(128)} %bitcast.16, s32[]{:T(128)} %bitcast.18, s32[]{:T(128)} %bitcast.17, s32[1024,1]{0,1:T(1,128)S(1)} %bitcast.58), kind=kLoop, calls=%fused_computation.35 | loop fusion | flops 15360 | bytes 12316 | tf_op jit(solution)/shard_map/gather | solution.py:36
  27.8 5.7 %select_select_fusion = s32[1024]{0:T(1024)S(1)} fusion(pred[1024]{0:T(1024)(128)(4,1)S(1)} %get-tuple-element.18, pred[1024]{0:T(1024)(128)(4,1)S(1)} %get-tuple-element.17, pred[1024]{0:T(1024)(128)(4,1)S(1)} %get-tuple-element.16, pred[1024]{0:T(1024)(128)(4,1)S(1)} %get-tuple-element.15, pred[1024]{0:T(1024)(128)(4,1)S(1)} %get-tuple-element.14, ...), kind=kLoop, calls=%fused_computation.45 | loop fusion | flops 9216 | bytes 17444 | tf_op jit(solution)/shard_map/gather | solution.py:36
  33.5 4.9 %scatter_custom_fusion = s32[2048]{0:T(1024)} fusion(s32[1024]{0:T(1024)S(1)} %bitcast.63, s32[1024]{0:T(1024)S(1)} %gather_fusion.1, s32[]{:T(128)} %constant.19.clone.1), kind=kCustom, calls=%fused_computation.46 | custom fusion | bytes 8196 | tf_op jit(solution)/shard_map/scatter | solution.py:44
  38.4 7.4 %all-to-all-start = ((s32[16,1,128]{2,1,0:T(1,128)}), s32[16,1,128]{2,1,0:T(1,128)S(1)}, u32[]{:S(2)}, u32[]{:S(2)}) async-start(s32[16,1,128]{2,1,0:T(1,128)} %bitcast.22), calls=%async_computation | async-start | bytes 16384 | tf_op jit(solution)/shard_map/all_to_all | solution.py:54
  45.8 10.4 %scatter_custom_fusion.1 = bf16[2048,128]{1,0:T(8,128)(2,1)} fusion(s32[1024]{0:T(1024)S(1)} %bitcast.64, bf16[1024,128]{1,0:T(8,128)(2,1)} %param.7, s32[1024]{0:T(1024)S(1)} %fusion.7, bf16[]{:T(256)} %constant.8.clone.1), kind=kCustom, calls=%fused_computation.17 | custom fusion | bytes 524800 | tf_op jit(solution)/shard_map/scatter | solution.py:41
  56.2 6.1 %all-to-all-start.1 = ((bf16[16,128,128]{2,1,0:T(8,128)(2,1)}), bf16[16,128,128]{2,1,0:T(8,128)(2,1)S(1)}, u32[]{:S(2)}, u32[]{:S(2)}) async-start(bf16[16,128,128]{2,1,0:T(8,128)(2,1)} %bitcast.25), calls=%async_computation.1 | async-start | bytes 1048576 | tf_op jit(solution)/shard_map/all_to_all | solution.py:47
  62.4 14.4 %all-to-all-done.1 = bf16[16,128,128]{2,1,0:T(8,128)(2,1)S(1)} async-done(((bf16[16,128,128]{2,1,0:T(8,128)(2,1)}), bf16[16,128,128]{2,1,0:T(8,128)(2,1)S(1)}, u32[]{:S(2)}, u32[]{:S(2)}) %all-to-all-start.1) | async-done | bytes 524320 | tf_op jit(solution)/shard_map/all_to_all | solution.py:47
  76.8 14.9 %scatter_custom_fusion.2 = f32[3073,128]{1,0:T(8,128)} fusion(s32[2048]{0:T(1024)S(1)} %bitcast.62, bf16[2048,128]{1,0:T(8,128)(2,1)S(1)} %bitcast.57, f32[]{:T(128)} %constant.18.clone.1), kind=kCustom, calls=%fused_computation.14 | custom fusion | flops 524288 | bytes 2097668 | tf_op jit(solution)/shard_map/scatter-add | solution.py:61
  91.6 1.5 slice.34
  93.1 1.3 collective-permute-start.1
  94.4 3.9 %collective-permute-start = (bf16[3072,128]{1,0:T(8,128)(2,1)S(1)}, bf16[3072,128]{1,0:T(8,128)(2,1)}, u32[]{:S(2)}, u32[]{:S(2)}) collective-permute-start(bf16[3072,128]{1,0:T(8,128)(2,1)S(1)} %slice.34), channel_id=1, source_target_pairs={{0,1},{1,2},{2,3},{3,4},{4,5},{5,6},{6,7},{7,8},{8,9},{9,10},{10,1... | collective-permute-start | bytes 2359304 | tf_op jit(solution)/shard_map/ppermute | solution.py:14
  99.5 7.6 %pad_maximum_fusion = bf16[9216,128]{1,0:T(8,128)(2,1)} fusion(bf16[3072,128]{1,0:T(8,128)(2,1)} %collective-permute-done.1, bf16[3072,128]{1,0:T(8,128)(2,1)S(1)} %slice.34, bf16[3072,128]{1,0:T(8,128)(2,1)} %collective-permute-done), kind=kLoop, calls=%fused_computation.8 | loop fusion | flops 7077888 | bytes 4718592 | tf_op jit(solution)/shard_map/concatenate | solution.py:16
  107.1 4.0 %gather_fusion.2 = bf16[96,96,128]{2,1,0:T(8,128)(2,1)} fusion(bf16[96,96,128]{2,1,0:T(8,128)(2,1)} %bitcast.55, s32[1024]{0:T(1024)S(1)} %pad_clamp_fusion), kind=kCustom, calls=%fused_computation.3 | custom fusion | bytes 4718976 | tf_op jit(solution)/shard_map/gather | solution.py:67
  111.0 2.6 bitcast_convert_fusion
  113.6 4.6 %convolution_bitcast_fusion.1 = f32[1024,128]{0,1:T(8,128)} fusion(bf16[3072,128]{1,0:T(8,128)(2,1)S(1)} %bitcast.53, bf16[3072,1024]{1,0:T(8,128)(2,1)} %param.12), kind=kOutput, calls=%fused_computation.12 | convolution fusion | flops 805306368 | bytes 7602176 | tf_op jit(solution)/shard_map/dot_general | solution.py:72
  118.2 1.2 copy.19
  119.4 103.3 %all-reduce.2.cloned.1.call-done = f32[1024,128]{0,1:T(8,128)} async-done(((f32[1024,128]{0,1:T(8,128)}), f32[1024,128]{0,1:T(8,128)}) %all-reduce.2.cloned.1.call-update) | async-done | bytes 524304 | tf_op jit(solution)/shard_map/psum | solution.py:75
  222.7 1.8 convolution_convert_fusion
  224.5 21.6 %all_gather.3 = bf16[1024,128]{1,0:T(8,128)(2,1)S(1)} all-gather(bf16[64,128]{1,0:T(8,128)(2,1)S(1)} %convolution_convert_fusion), channel_id=1, replica_groups=mesh['case'=2,'elem'=16] {'elem'}, dimensions={0}, use_global_device_ids=true | all-gather | bytes 278528 | tf_op jit(solution)/shard_map/all_gather | solution.py:81
  246.1 5.8 %multiply_reduce_fusion = (f32[3072]{0:T(1024)}, bf16[3072,128]{0,1:T(8,128)(2,1)S(1)}) fusion(bf16[3072,128]{0,1:T(8,128)(2,1)} %copy.19, bf16[1024,128]{1,0:T(8,128)(2,1)S(1)} %all_gather.3, bf16[3072,1024]{1,0:T(8,128)(2,1)} %param.12), kind=kOutput, calls=%fused_computation.11 | convolution fusion | flops 806876160 | bytes 8138752 | tf_op jit(solution)/shard_map/dot_general | solution.py:79
  251.9 1.2 copy.20
  (28 shorter events, 3.3 us)
Async XLA Ops:
  7.2 103.9 %copy-start = (bf16[32,3,96,96]{3,2,1,0:T(8,128)(2,1)S(1)}, bf16[32,3,96,96]{3,2,1,0:T(8,128)(2,1)}, u32[]{:S(2)}) copy-start(bf16[32,3,96,96]{3,2,1,0:T(8,128)(2,1)} %param.10) | copy-start | bytes 5308420
  7.2 6.0 %copy-start.1 = (s32[1024,1]{0,1:T(1,128)S(1)}, s32[1024,1]{0,1:T(1,128)}, u32[]{:S(2)}) copy-start(s32[1024,1]{0,1:T(1,128)} %param.8) | copy-start | bytes 12292
  7.2 10.6 %copy-start.2 = (s32[1024]{0:T(1024)S(1)}, s32[1024]{0:T(1024)}, u32[]{:S(2)}) copy-start(s32[1024]{0:T(1024)} %param.9) | copy-start | bytes 12292
  38.4 17.8 %all-to-all-start = ((s32[16,1,128]{2,1,0:T(1,128)}), s32[16,1,128]{2,1,0:T(1,128)S(1)}, u32[]{:S(2)}, u32[]{:S(2)}) async-start(s32[16,1,128]{2,1,0:T(1,128)} %bitcast.22), calls=%async_computation | async-start | bytes 16384 | tf_op jit(solution)/shard_map/all_to_all | solution.py:54
  56.2 42.2 %copy-start.3 = (s32[32,3]{0,1:T(4,128)S(1)}, s32[32,3]{0,1:T(4,128)}, u32[]{:S(2)}) copy-start(s32[32,3]{0,1:T(4,128)} %param.11) | copy-start | bytes 1156
  56.2 20.6 %all-to-all-start.1 = ((bf16[16,128,128]{2,1,0:T(8,128)(2,1)}), bf16[16,128,128]{2,1,0:T(8,128)(2,1)S(1)}, u32[]{:S(2)}, u32[]{:S(2)}) async-start(bf16[16,128,128]{2,1,0:T(8,128)(2,1)} %bitcast.25), calls=%async_computation.1 | async-start | bytes 1048576 | tf_op jit(solution)/shard_map/all_to_all | solution.py:47
  62.3 160.4 %all-reduce.2.cloned.1.call-start = ((), (), s32[]{:S(2)}) async-start(), calls=%async_computation.2 | async-start | bytes 1048576 | tf_op jit(solution)/shard_map/psum | solution.py:75
  93.1 5.4 %collective-permute-start.1 = (bf16[3072,128]{1,0:T(8,128)(2,1)S(1)}, bf16[3072,128]{1,0:T(8,128)(2,1)}, u32[]{:S(2)}, u32[]{:S(2)}) collective-permute-start(bf16[3072,128]{1,0:T(8,128)(2,1)S(1)} %slice.34), channel_id=1, source_target_pairs={{1,0},{2,1},{3,2},{4,3},{5,4},{6,5},{7,6},{8,7},{9,8},{10,9},{11,1... | collective-permute-start | bytes 2359304 | tf_op jit(solution)/shard_map/ppermute | solution.py:15
  94.4 5.1 %collective-permute-start = (bf16[3072,128]{1,0:T(8,128)(2,1)S(1)}, bf16[3072,128]{1,0:T(8,128)(2,1)}, u32[]{:S(2)}, u32[]{:S(2)}) collective-permute-start(bf16[3072,128]{1,0:T(8,128)(2,1)S(1)} %slice.34), channel_id=1, source_target_pairs={{0,1},{1,2},{2,3},{3,4},{4,5},{5,6},{6,7},{7,8},{8,9},{9,10},{10,1... | collective-permute-start | bytes 2359304 | tf_op jit(solution)/shard_map/ppermute | solution.py:14
Sparse Core Ops, SparseCore 0:
  118.4 104.3 all-reduce.1
where the time goes:
time: 261 us; the launch traced here: 260 us
  waiting for transfers between devices  119 us (46%)
  other arithmetic  38.8 us (15%)
  local copies, waits for them, and re-layouts  33.1 us (13%)
  blocking collectives  21.6 us (8%)
  starting transfers between devices  18.8 us (7%)
  matrix products  14.8 us (6%)
  between operations  14.2 us (5%)
    psum x1, waiting for transfers between devices, body(): modal = lax.psum(partial_value, 'elem')  103 us
    all_gather x1, blocking collectives, body(): lax.all_gather(adj_rows, 'elem', axis=0, tiled=True)  21.6 us
    scatter-add x1, other arithmetic, body(): summed = jnp.zeros((elem_rows + 1, record_width), jnp.float32).at[got_slo...  14.9 us
    all_to_all x1, waiting for transfers between devices, body(): lax.all_to_all(send_rec.reshape(owners, capacity, record_width), 'elem',...  14.4 us
    scatter x1, local copies, waits for them, and re-layouts, body(): send_rec = jnp.zeros((owners * capacity, record_width), records.dtype).at...  10.4 us
    gather x3, other arithmetic, body(): slot_rank = jnp.arange(pan_rows, dtype=jnp.int32) - starts[sorted_owner]  10.2 us
    concatenate x1, other arithmetic, with_halo(): array = jnp.concatenate([before, array, after], axis=dim)  7.57 us
    all_to_all x1, starting transfers between devices, body(): lax.all_to_all(send_slot.reshape(owners, capacity), 'elem', split_axis=0,...  7.39 us
  transfers between devices with their start and end apart: 5, of which 3 were waited for; matrix products, arithmetic and copies ran while one was open for 5% of the time, Pallas kernels for 0%

commit v1 on v0

v1 whole, which is shorter than its diff:
```python
import functools

import jax
import jax.numpy as jnp
from jax import lax
from jax.experimental import pallas as pl
from jax.experimental.pallas import tpu as pltpu
from jax.sharding import PartitionSpec as P

LANES = 128
TAIL = 16
REACH = 8
BF = jnp.bfloat16
F32 = jnp.float32
NT = (((1,), (1,)), ((), ()))
TN = (((0,), (0,)), ((), ()))


def call(kernel, out_shape, *operands, smem=(), scratch=(), flops=0, limit=48 * 2**20):
    space = [pltpu.SMEM if k in smem else pltpu.VMEM for k in range(len(operands))]
    moved = sum(x.size * x.dtype.itemsize for x in operands)
    return pl.pallas_call(
        kernel,
        out_shape=out_shape,
        in_specs=[pl.BlockSpec(memory_space=s) for s in space],
        out_specs=jax.tree.map(lambda _: pl.BlockSpec(memory_space=pltpu.VMEM), out_shape),
        scratch_shapes=list(scratch),
        compiler_params=pltpu.CompilerParams(vmem_limit_bytes=limit),
        cost_estimate=pl.CostEstimate(flops=flops, bytes_accessed=moved, transcendentals=0),
    )(*operands)


def shape(dims, dtype):
    return jax.ShapeDtypeStruct(dims, dtype)


def hot(rows, key):
    row = lax.broadcasted_iota(jnp.int32, (rows, key.shape[1]), 0).astype(F32).astype(BF)
    return jnp.where(row == key, jnp.ones((), BF), jnp.zeros((), BF))


def pack_kernel(owners, cap, owner_ref, slot_ref, rec_ref, out_ref):
    pan = rec_ref.shape[0]
    pieces = pan // LANES
    owner = owner_ref[...]
    match = lax.broadcasted_iota(jnp.int32, (owners, pan), 0) == owner
    match_f = jnp.where(match, 1.0, 0.0)
    before = lax.broadcasted_iota(jnp.int32, (LANES, LANES), 0)
    after = lax.broadcasted_iota(jnp.int32, (LANES, LANES), 1)
    triangle = jnp.where(before <= after, 1.0, 0.0).astype(BF)
    stacked = jnp.concatenate(
        [match_f[:, k * LANES : (k + 1) * LANES] for k in range(pieces)], axis=0
    ).astype(BF)
    running = jnp.dot(stacked, triangle, preferred_element_type=F32)
    offset = jnp.zeros((owners, 1), F32)
    ranks = []
    for k in range(pieces):
        piece = running[k * owners : (k + 1) * owners] + offset
        picked = match_f[:, k * LANES : (k + 1) * LANES] * piece
        ranks.append(jnp.sum(picked, axis=0, keepdims=True) - 1.0)
        offset = piece[:, LANES - 1 : LANES]
    rank = jnp.concatenate(ranks, axis=1)
    slot = jnp.concatenate([slot_ref[k : k + 1, :] for k in range(pieces)], axis=1)
    high = (slot >> 6).astype(F32)
    low = (slot & 63).astype(F32)
    weights = jnp.concatenate([match_f * high, match_f * low], axis=0).astype(BF)
    share = LANES // cap
    shift = lax.rem(lax.axis_index("elem"), share) * cap
    spread = hot(LANES, (rank + shift.astype(F32)).astype(BF))
    slots = lax.dot_general(weights, spread, NT, preferred_element_type=F32)
    records = rec_ref[...]
    tail_row = lax.broadcasted_iota(jnp.int32, (TAIL, LANES), 0)
    for o in range(owners):
        key = jnp.where(owner == o, rank, -1.0).astype(BF)
        out_ref[o, 0:cap, :] = jnp.dot(
            hot(cap, key), records, preferred_element_type=F32
        ).astype(BF)
        tail = jnp.where(
            tail_row == 0,
            slots[o : o + 1],
            jnp.where(tail_row == 1, slots[owners + o : owners + o + 1], 0.0),
        )
        out_ref[o, cap : cap + TAIL, :] = tail.astype(BF)


def read_slots(got_ref, cap):
    owners = got_ref.shape[0]
    share = LANES // cap
    rows = []
    for group in range(owners // share):
        tail = got_ref[group * share, cap : cap + TAIL, :].astype(F32)
        for k in range(1, share):
            tail += got_ref[group * share + k, cap : cap + TAIL, :].astype(F32)
        rows.append(tail[0:1] * 64.0 + tail[1:2])
    return jnp.concatenate(rows, axis=1)


def loads_at(slots, records, base, rows):
    key = slots - base.astype(F32)
    key = jnp.where((key >= 0.0) & (key < float(rows)), key, -1.0).astype(BF)
    return jnp.dot(hot(rows, key), records, preferred_element_type=F32).astype(BF)


def edge_kernel(cap, elem_rows, halo, got_ref, near_ref, far_ref):
    odd = lax.rem(lax.axis_index("elem"), 2)
    slots = read_slots(got_ref, cap)
    records = got_ref[:, 0:cap, :].reshape(-1, LANES)
    last = elem_rows - halo
    chunk = 256
    for k in range(halo // chunk):
        base = jnp.where(odd == 1, last, 0) + k * chunk
        far_ref[k * chunk : (k + 1) * chunk, :] = loads_at(slots, records, base, chunk)
    for k in range(halo // chunk):
        base = jnp.where(odd == 1, 0, last) + k * chunk
        near_ref[k * chunk : (k + 1) * chunk, :] = loads_at(slots, records, base, chunk)


def stiffen(stiff_ref, cols_ref, ext_ref, block, first_col):
    size = stiff_ref.shape[2]
    total = None
    for j in range(stiff_ref.shape[1]):
        start = pl.multiple_of((cols_ref[j, block] - first_col) * size, 32)
        part = jnp.dot(
            stiff_ref[block, j], ext_ref[pl.ds(start, size), :], preferred_element_type=F32
        )
        total = part if total is None else total + part
    return total.astype(BF)


def middle_kernel(
    cap, halo, got_ref, near_ref, far_ref, stiff_ref, cols_ref, modes_ref,
    loads_ref, st_ref, modal_ref,
):
    elem_rows = modes_ref.shape[0]
    blocks, _, size, _ = stiff_ref.shape
    me = lax.axis_index("elem")
    odd = lax.rem(me, 2)
    last = elem_rows - halo
    near_at = pl.multiple_of(jnp.where(odd == 1, 0, last), 32)
    far_at = pl.multiple_of(jnp.where(odd == 1, last, 0), 32)
    loads_ref[pl.ds(near_at, halo), :] = near_ref[...]
    loads_ref[pl.ds(far_at, halo), :] = far_ref[...]
    slots = read_slots(got_ref, cap)
    records = got_ref[:, 0:cap, :].reshape(-1, LANES)
    chunk = 256
    for k in range((last - halo) // chunk):
        base = halo + k * chunk
        loads_ref[base : base + chunk, :] = loads_at(slots, records, jnp.int32(base), chunk)
    for b in range(REACH, blocks - REACH):
        st_ref[(b - REACH) * size : (b - REACH + 1) * size, :] = stiffen(
            stiff_ref, cols_ref, loads_ref, b, me * blocks
        )
    modal_ref[...] = lax.dot_general(
        st_ref[...], modes_ref[halo:last, :], TN, preferred_element_type=F32
    )


def outer_kernel(
    halo, loads_ref, near_ref, far_ref, stiff_ref, cols_ref, modes_ref, modal_ref,
    st_ref, keep_ref, send_ref, ext_ref, total_ref,
):
    elem_rows = modes_ref.shape[0]
    blocks, _, size, _ = stiff_ref.shape
    me = lax.axis_index("elem")
    odd = lax.rem(me, 2)
    last = elem_rows - halo
    end = halo + elem_rows
    near_at = pl.multiple_of(jnp.where(odd == 1, 0, end), 32)
    far_at = pl.multiple_of(jnp.where(odd == 1, end, 0), 32)
    ext_ref[pl.ds(near_at, halo), :] = near_ref[...]
    ext_ref[pl.ds(far_at, halo), :] = far_ref[...]
    ext_ref[halo:end, :] = loads_ref[...]
    first_col = me * blocks - REACH
    for k in range(REACH):
        st_ref[k * size : (k + 1) * size, :] = stiffen(
            stiff_ref, cols_ref, ext_ref, k, first_col
        )
        st_ref[halo + k * size : halo + (k + 1) * size, :] = stiffen(
            stiff_ref, cols_ref, ext_ref, blocks - REACH + k, first_col
        )
    total_ref[...] = (
        modal_ref[...]
        + lax.dot_general(st_ref[0:halo, :], modes_ref[0:halo, :], TN, preferred_element_type=F32)
        + lax.dot_general(st_ref[halo:, :], modes_ref[last:, :], TN, preferred_element_type=F32)
    )
    half = total_ref.shape[0] // 2
    keep_ref[...] = total_ref[pl.ds(pl.multiple_of(odd * half, 8), half), :]
    send_ref[...] = total_ref[pl.ds(pl.multiple_of((1 - odd) * half, 8), half), :]


def pair_kernel(mine_ref, other_ref, keep_ref, send_ref, total_ref):
    bit = lax.rem(lax.axis_index("elem") // 2, 2)
    total_ref[...] = mine_ref[...] + other_ref[...]
    half = total_ref.shape[0] // 2
    keep_ref[...] = total_ref[pl.ds(pl.multiple_of(bit * half, 8), half), :]
    send_ref[...] = total_ref[pl.ds(pl.multiple_of((1 - bit) * half, 8), half), :].astype(BF)


def add_kernel(mine_ref, other_ref, total_ref, send_ref):
    total = mine_ref[...] + other_ref[...].astype(F32)
    total_ref[...] = total
    send_ref[...] = total.astype(BF)


def split_kernel(a_ref, high_ref, low_ref):
    a = a_ref[...]
    high = a.astype(BF)
    high_ref[...] = high
    low_ref[...] = (a - high.astype(F32)).astype(BF)


def admit_kernel(count, mine_ref, *refs):
    others, (high_ref, low_ref, adj_ref) = refs[:count], refs[count:]
    total = mine_ref[...]
    for other in others:
        total += other[...].astype(F32)
    high = total.astype(BF)
    low = (total - high.astype(F32)).astype(BF)
    adj = lax.dot_general(high, high_ref[...], NT, preferred_element_type=F32)
    adj += lax.dot_general(high, low_ref[...], NT, preferred_element_type=F32)
    adj += lax.dot_general(low, high_ref[...], NT, preferred_element_type=F32)
    adj_ref[...] = adj.astype(BF)


def back_kernel(halo, own_ref, y_ref, core_ref, both_ref, modes_ref, mid_ref, out_ref, adj_ref, sens_ref, field_ref):
    me = lax.axis_index("elem")
    odd = lax.rem(me, 2)
    bit = lax.rem(me // 2, 2)
    quarter = own_ref.shape[0]
    for ref, c, y in (
        (own_ref, odd, bit),
        (y_ref, odd, 1 - bit),
        (core_ref, 1 - odd, bit),
        (both_ref, 1 - odd, 1 - bit),
    ):
        at = pl.multiple_of((2 * c + y) * quarter, 16)
        field_ref[pl.ds(at, quarter), :] = ref[...]
    field = field_ref[...]
    elem_rows = modes_ref.shape[0]
    last = elem_rows - halo
    chunk = 256
    for k in range(elem_rows // chunk):
        at = k * chunk
        part = lax.dot_general(
            modes_ref[at : at + chunk, :], field, NT, preferred_element_type=F32
        )
        adj_ref[at : at + chunk, :] = part.astype(BF)
        if at < halo:
            st = out_ref[at : at + chunk, :]
        elif at < last:
            st = mid_ref[at - halo : at - halo + chunk, :]
        else:
            st = out_ref[at - last + halo : at - last + halo + chunk, :]
        product = part * st.astype(F32)
        for i in range(chunk // LANES):
            row = jnp.sum(product[i * LANES : (i + 1) * LANES, :].T, axis=0, keepdims=True)
            sens_ref[at // LANES + i : at // LANES + i + 1, :] = row


def body(records, panel_owner, panel_slot, stiff_blocks, block_cols, modes, admittance):
    owners = lax.axis_size("elem")
    pan, width = records.shape
    cap = 2 * pan // owners
    elem_rows, mode_count = modes.shape
    blocks, nnz, size, _ = stiff_blocks.shape
    halo = REACH * size

    def swap(array, mask):
        return lax.ppermute(array, "elem", [(i, i ^ mask) for i in range(owners)])

    def swap_far(array):
        pairs = [(i, i + 1) for i in range(1, owners - 1, 2)]
        return lax.ppermute(array, "elem", pairs + [(j, i) for i, j in pairs])

    packed = call(
        functools.partial(pack_kernel, owners, cap),
        shape((owners, cap + TAIL, width), BF),
        panel_owner.reshape(1, pan),
        panel_slot.reshape(pan // LANES, LANES),
        records,
        flops=2 * owners * cap * pan * width,
    )
    got = lax.all_to_all(packed, "elem", split_axis=0, concat_axis=0, tiled=True)
    a_high, a_low = call(
        split_kernel,
        (shape(admittance.shape, BF), shape(admittance.shape, BF)),
        admittance,
        flops=4 * admittance.size,
    )
    near, far = call(
        functools.partial(edge_kernel, cap, elem_rows, halo),
        (shape((halo, width), BF), shape((halo, width), BF)),
        got,
        flops=2 * owners * cap * 2 * halo * width,
    )
    got_far = swap_far(far)
    got_near = swap(near, 1)
    cols = block_cols.T
    loads, st_mid, modal_mid = call(
        functools.partial(middle_kernel, cap, halo),
        (
            shape((elem_rows, width), BF),
            shape((elem_rows - 2 * halo, width), BF),
            shape((width, mode_count), F32),
        ),
        got, near, far, stiff_blocks, cols, modes,
        smem=(4,),
        flops=elem_rows * width * mode_count,
    )
    st_out, keep, send = call(
        functools.partial(outer_kernel, halo),
        (
            shape((2 * halo, width), BF),
            shape((width // 2, mode_count), F32),
            shape((width // 2, mode_count), F32),
        ),
        loads, got_near, got_far, stiff_blocks, cols, modes, modal_mid,
        smem=(4,),
        scratch=(pltpu.VMEM((elem_rows + 2 * halo, width), BF), pltpu.VMEM((width, mode_count), F32)),
        flops=elem_rows * width * mode_count,
    )
    quarter = width // 4
    keep, send = call(
        pair_kernel,
        (shape((quarter, mode_count), F32), shape((quarter, mode_count), BF)),
        keep, swap(send, 1),
        scratch=(pltpu.VMEM((width // 2, mode_count), F32),),
    )
    total, send = call(
        add_kernel,
        (shape((quarter, mode_count), F32), shape((quarter, mode_count), BF)),
        keep, swap(send, 2),
    )
    groups = owners // 4
    others = [swap(send, 4 * k) for k in reversed(range(1, groups))]
    own = call(
        functools.partial(admit_kernel, len(others)),
        shape((quarter, mode_count), BF),
        total, *others, a_high, a_low,
        flops=6 * quarter * mode_count * mode_count,
    )
    across = swap(own, 2)
    beside = swap(own, 1)
    both = swap(across, 1)
    adjoint, sensitivity = call(
        functools.partial(back_kernel, halo),
        (shape((elem_rows, width), BF), shape((elem_rows // LANES, LANES), F32)),
        own, across, beside, both, modes, st_mid, st_out,
        scratch=(pltpu.VMEM((width, mode_count), BF),),
        flops=2 * elem_rows * width * mode_count,
    )
    return adjoint, sensitivity.reshape(elem_rows)


def solution(mesh):
    in_specs = (
        P(("case", "elem"), None),
        P("elem", None),
        P("elem"),
        P("elem", None, None, None),
        P("elem", None),
        P("elem", None),
        P("case", None),
    )
    out_specs = (P(("case", "elem"), None), P(("case", "elem")))
    return jax.shard_map(body, mesh=mesh, in_specs=in_specs, out_specs=out_specs, check_vma=False)
```

time: 261 us -> 72.3 us (0.28)
  waiting for transfers between devices: 119 us -> 11.1 us
  other arithmetic: 38.8 us -> 0 us
  local copies, waits for them, and re-layouts: 33.1 us -> 2.33 us
  Pallas kernels: 0 us -> 23.6 us
  matrix products: 14.8 us -> 0 us
  between operations: 14.2 us -> 0.75 us
  starting transfers between devices: 18.8 us -> 9.55 us
  blocking collectives: 21.6 us -> 24.6 us
    psum x1 -> x0, waiting for transfers between devices: 103 us -> none  [body(): modal = lax.psum(partial_value, 'elem')]
    all_to_all x0 -> x1, blocking collectives: none -> 24.6 us  [body(): lax.all_to_all(packed, 'elem', split_axis=0, concat_axis=0, tiled=True)]
    pallas_call x0 -> x9, Pallas kernels: none -> 23.6 us  [call(): pl.pallas_call(kernel, out_shape=out_shape, in_specs=[pl.BlockSpec(memory...]
    all_gather x1 -> x0, blocking collectives: 21.6 us -> none  [body(): lax.all_gather(adj_rows, 'elem', axis=0, tiled=True)]
    scatter x2 -> x0, local copies, waits for them, and re-layouts: 15.3 us -> none  [the longest x1 10.4 us: body(): send_rec = jnp.zeros((owners * capacity, record_width), records.dtype).at...]
    scatter-add x1 -> x0, other arithmetic: 14.9 us -> none  [body(): summed = jnp.zeros((elem_rows + 1, record_width), jnp.float32).at[got_slo...]
    dot_general x4 -> x0, matrix products: 14.8 us -> none  [the longest x1 5.82 us: body(): jnp.dot(modes, lax.all_gather(adj_rows, 'elem', axis=0, tiled=True), pref...]
    all_to_all x2 -> x0, waiting for transfers between devices: 14.4 us -> none  [the longest x1 14.4 us: body(): lax.all_to_all(send_rec.reshape(owners, capacity, record_width), 'elem',...]
  transfers between devices with their start and end apart: 5 -> 10, of which waited for: 3 -> 6; matrix products, arithmetic and copies ran while one was open for 5% -> 0% of each run, Pallas kernels for 0% -> 12%
where the time goes in v1:
time: 72.3 us; the launch traced here: 71.9 us
  blocking collectives  24.6 us (34%)
  Pallas kernels  23.6 us (33%)
  waiting for transfers between devices  11.1 us (15%)
  starting transfers between devices  9.55 us (13%)
  local copies, waits for them, and re-layouts  2.33 us (3%)
  between operations  0.75 us (1%)
    all_to_all x1, blocking collectives, body(): lax.all_to_all(packed, 'elem', split_axis=0, concat_axis=0, tiled=True)  24.6 us
    pallas_call x9, Pallas kernels, call(): pl.pallas_call(kernel, out_shape=out_shape, in_specs=[pl.BlockSpec(memory...  23.6 us
    ppermute x9, waiting for transfers between devices, swap(): return lax.ppermute(array, 'elem', [(i, i ^ mask) for i in range(owners)])  11.1 us
    ppermute x9, starting transfers between devices, swap(): return lax.ppermute(array, 'elem', [(i, i ^ mask) for i in range(owners)])  8.89 us
    unnamed x10, local copies, waits for them, and re-layouts  2.33 us
  transfers between devices with their start and end apart: 10, of which 6 were waited for; matrix products, arithmetic and copies ran while one was open for 0% of the time, Pallas kernels for 12%

profile of v1, /device:TPU:0, one launch (start us, length us, event | category | flops | bytes accessed | tf_op | source)
XLA Modules:
  0.0 71.9 jit_solution(17183987676475298533)
XLA Ops:
  0.6 0.9 %copy-done.2 = bf16[1024,128]{1,0:T(8,128)(2,1)S(1)} copy-done((bf16[1024,128]{1,0:T(8,128)(2,1)S(1)}, bf16[1024,128]{1,0:T(8,128)(2,1)}, u32[]{:S(2)}) %copy-start.2) | copy-done | bytes 262168
  1.6 0.7 copy-done.3
  2.3 0.7 copy-done.4
  3.0 1.9 %shard_map.86 = bf16[16,144,128]{2,1,0:T(8,128)(2,1)S(1)} custom-call(s32[1,1024]{1,0:T(1,128)S(1)} %bitcast.6, s32[8,128]{1,0:T(8,128)S(1)} %bitcast.7, bf16[1024,128]{1,0:T(8,128)(2,1)S(1)} %copy-done.2), custom_call_target="tpu_custom_call" | custom-call | flops 536870912 | bytes 270336 | tf_op jit(solution)/shard_map/pallas_call | solution.py:22
  4.9 24.6 %all_to_all.5.got_ref = bf16[16,144,128]{2,1,0:T(8,128)(2,1)S(1)} all-to-all(bf16[16,144,128]{2,1,0:T(8,128)(2,1)S(1)} %shard_map.86), channel_id=1, replica_groups=mesh['case'=2,'elem'=16] {'elem'}, dimensions={0} | all-to-all | bytes 1179648 | tf_op jit(solution)/shard_map/all_to_all | solution.py:283
  29.5 1.8 %shard_map.87 = (bf16[768,128]{1,0:T(8,128)(2,1)S(1)}, bf16[768,128]{1,0:T(8,128)(2,1)S(1)}) custom-call(bf16[16,144,128]{2,1,0:T(8,128)(2,1)S(1)} %all_to_all.5.got_ref), custom_call_target="tpu_custom_call" | custom-call | flops 805306368 | bytes 589824 | tf_op jit(solution)/shard_map/pallas_call | solution.py:22
  31.5 0.7 collective-permute-start.1
  32.2 5.6 %shard_map.88 = (bf16[3072,128]{1,0:T(8,128)(2,1)S(1)}, bf16[1536,128]{1,0:T(8,128)(2,1)S(1)}, f32[128,1024]{1,0:T(8,128)S(1)}) custom-call(bf16[16,144,128]{2,1,0:T(8,128)(2,1)S(1)} %all_to_all.5.got_ref, bf16[768,128]{1,0:T(8,128)(2,1)S(1)} %get-tuple-element.18.near_ref, bf16[768,128]{1,0:T(8,128)(2,1)S(1)} %get-tuple-element.19.far_ref, ...), custom_call_target="tpu_custom_call" | custom-call | flops 402653184 | bytes 9044352 | tf_op jit(solution)/shard_map/pallas_call | solution.py:22
  37.7 4.0 %shard_map.89 = (bf16[1536,128]{1,0:T(8,128)(2,1)S(1)}, f32[64,1024]{1,0:T(8,128)S(1)}, f32[64,1024]{1,0:T(8,128)S(1)}) custom-call(bf16[3072,128]{1,0:T(8,128)(2,1)S(1)} %get-tuple-element.20.loads_ref, bf16[768,128]{1,0:T(8,128)(2,1)S(1)} %collective-permute-done.near_ref, bf16[768,128]{1,0:T(8,128)(2,1)S(1)} %collective-permute-done.1.far_ref, ...), custom_call_target="tpu_custom_call" | custom-call | flops 402653184 | bytes 9765248 | tf_op jit(solution)/shard_map/pallas_call | solution.py:22
  41.7 2.0 %collective-permute-start.2 = (f32[64,1024]{1,0:T(8,128)S(1)}, f32[64,1024]{1,0:T(8,128)S(1)}, u32[]{:S(2)}, u32[]{:S(2)}) collective-permute-start(f32[64,1024]{1,0:T(8,128)S(1)} %get-tuple-element.23), channel_id=1, source_target_pairs={{0,1},{1,0},{2,3},{3,2},{4,5},{5,4},{6,7},{7,6},{8,9},{9,8},{10,11... | collective-permute-start | bytes 786440 | tf_op jit(solution)/shard_map/ppermute | solution.py:269
  43.7 1.2 %collective-permute-done.2.other_ref = f32[64,1024]{1,0:T(8,128)S(1)} collective-permute-done((f32[64,1024]{1,0:T(8,128)S(1)}, f32[64,1024]{1,0:T(8,128)S(1)}, u32[]{:S(2)}, u32[]{:S(2)}) %collective-permute-start.2) | collective-permute-done | bytes 262176 | tf_op jit(solution)/shard_map/ppermute | solution.py:269
  44.9 1.9 %collective-permute-start.3 = (bf16[32,1024]{1,0:T(8,128)(2,1)S(1)}, bf16[32,1024]{1,0:T(8,128)(2,1)S(1)}, u32[]{:S(2)}, u32[]{:S(2)}) collective-permute-start(bf16[32,1024]{1,0:T(8,128)(2,1)S(1)} %get-tuple-element.25), channel_id=1, source_target_pairs={{0,2},{1,3},{2,0},{3,1},{4,6},{5,7},{6,4},{7,5},{8,10},{9,11},{10,... | collective-permute-start | bytes 196616 | tf_op jit(solution)/shard_map/ppermute | solution.py:269
  46.8 2.5 %collective-permute-done.3.other_ref = bf16[32,1024]{1,0:T(8,128)(2,1)S(1)} collective-permute-done((bf16[32,1024]{1,0:T(8,128)(2,1)S(1)}, bf16[32,1024]{1,0:T(8,128)(2,1)S(1)}, u32[]{:S(2)}, u32[]{:S(2)}) %collective-permute-start.3) | collective-permute-done | bytes 65568 | tf_op jit(solution)/shard_map/ppermute | solution.py:269
  49.4 2.0 %collective-permute-start.6 = (bf16[32,1024]{1,0:T(8,128)(2,1)S(1)}, bf16[32,1024]{1,0:T(8,128)(2,1)S(1)}, u32[]{:S(2)}, u32[]{:S(2)}) collective-permute-start(bf16[32,1024]{1,0:T(8,128)(2,1)S(1)} %get-tuple-element.27), channel_id=1, source_target_pairs={{0,4},{1,5},{2,6},{3,7},{4,0},{5,1},{6,2},{7,3},{8,12},{9,13},{10,... | collective-permute-start | bytes 196616 | tf_op jit(solution)/shard_map/ppermute | solution.py:269
  51.4 1.4 %collective-permute-start.5 = (bf16[32,1024]{1,0:T(8,128)(2,1)S(1)}, bf16[32,1024]{1,0:T(8,128)(2,1)S(1)}, u32[]{:S(2)}, u32[]{:S(2)}) collective-permute-start(bf16[32,1024]{1,0:T(8,128)(2,1)S(1)} %get-tuple-element.27), channel_id=1, source_target_pairs={{0,8},{1,9},{2,10},{3,11},{4,12},{5,13},{6,14},{7,15},{8,0},{9,1},... | collective-permute-start | bytes 196616 | tf_op jit(solution)/shard_map/ppermute | solution.py:269
  52.8 1.1 %collective-permute-start.4 = (bf16[32,1024]{1,0:T(8,128)(2,1)S(1)}, bf16[32,1024]{1,0:T(8,128)(2,1)S(1)}, u32[]{:S(2)}, u32[]{:S(2)}) collective-permute-start(bf16[32,1024]{1,0:T(8,128)(2,1)S(1)} %get-tuple-element.27), channel_id=1, source_target_pairs={{0,12},{1,13},{2,14},{3,15},{4,8},{5,9},{6,10},{7,11},{8,4},{9,5},... | collective-permute-start | bytes 196616 | tf_op jit(solution)/shard_map/ppermute | solution.py:269
  53.8 2.9 %shard_map.92 = (bf16[1024,1024]{1,0:T(8,128)(2,1)S(1)}, bf16[1024,1024]{1,0:T(8,128)(2,1)S(1)}) custom-call(f32[1024,1024]{1,0:T(8,128)} %a_ref.1), custom_call_target="tpu_custom_call" | custom-call | flops 4194304 | bytes 4194304 | tf_op jit(solution)/shard_map/pallas_call | solution.py:22
  56.7 1.4 %collective-permute-done.5.refs_1_ = bf16[32,1024]{1,0:T(8,128)(2,1)S(1)} collective-permute-done((bf16[32,1024]{1,0:T(8,128)(2,1)S(1)}, bf16[32,1024]{1,0:T(8,128)(2,1)S(1)}, u32[]{:S(2)}, u32[]{:S(2)}) %collective-permute-start.5) | collective-permute-done | bytes 65568 | tf_op jit(solution)/shard_map/ppermute | solution.py:269
  58.1 0.8 %collective-permute-done.4.refs_0_ = bf16[32,1024]{1,0:T(8,128)(2,1)S(1)} collective-permute-done((bf16[32,1024]{1,0:T(8,128)(2,1)S(1)}, bf16[32,1024]{1,0:T(8,128)(2,1)S(1)}, u32[]{:S(2)}, u32[]{:S(2)}) %collective-permute-start.4) | collective-permute-done | bytes 65568 | tf_op jit(solution)/shard_map/ppermute | solution.py:269
  58.9 1.9 %shard_map.93.own_ref = bf16[32,1024]{1,0:T(8,128)(2,1)S(1)} custom-call(f32[32,1024]{1,0:T(8,128)S(1)} %get-tuple-element.26.mine_ref, bf16[32,1024]{1,0:T(8,128)(2,1)S(1)} %collective-permute-done.4.refs_0_, bf16[32,1024]{1,0:T(8,128)(2,1)S(1)} %collective-permute-done.5.refs_1_, bf16[32,1024]{1,0:T(8,128)(2,1)S(1)} %collective-permute-done.6.refs_2_, ...), custom_call_target="tpu_custom_call" | custom-call | flops 201326592 | bytes 4521984 | tf_op jit(solution)/shard_map/pallas_call | solution.py:22
  60.9 0.3 collective-permute-start.7
  61.2 3.9 %collective-permute-done.7.y_ref = bf16[32,1024]{1,0:T(8,128)(2,1)S(1)} collective-permute-done((bf16[32,1024]{1,0:T(8,128)(2,1)S(1)}, bf16[32,1024]{1,0:T(8,128)(2,1)S(1)}, u32[]{:S(2)}, u32[]{:S(2)}) %collective-permute-start.7) | collective-permute-done | bytes 65568 | tf_op jit(solution)/shard_map/ppermute | solution.py:269
  65.1 1.2 %collective-permute-done.9.both_ref = bf16[32,1024]{1,0:T(8,128)(2,1)S(1)} collective-permute-done((bf16[32,1024]{1,0:T(8,128)(2,1)S(1)}, bf16[32,1024]{1,0:T(8,128)(2,1)S(1)}, u32[]{:S(2)}, u32[]{:S(2)}) %collective-permute-start.9) | collective-permute-done | bytes 65568 | tf_op jit(solution)/shard_map/ppermute | solution.py:269
  66.4 5.5 %shard_map.94 = (bf16[3072,128]{1,0:T(8,128)(2,1)}, f32[24,128]{1,0:T(8,128)}) custom-call(bf16[32,1024]{1,0:T(8,128)(2,1)S(1)} %shard_map.93.own_ref, bf16[32,1024]{1,0:T(8,128)(2,1)S(1)} %collective-permute-done.7.y_ref, bf16[32,1024]{1,0:T(8,128)(2,1)S(1)} %collective-permute-done.8.core_ref, bf16[32,1024]{1,0:T(8,128)(2,1)S(1)} %collective-permute-done.9.both_ref, ...), custom_call_target="tpu_custom_call" | custom-call | flops 805306368 | bytes 7340032 | tf_op jit(solution)/shard_map/pallas_call | solution.py:22
  (16 shorter events, 0.3 us)
Async XLA Ops:
  0.6 1.0 %copy-start.2 = (bf16[1024,128]{1,0:T(8,128)(2,1)S(1)}, bf16[1024,128]{1,0:T(8,128)(2,1)}, u32[]{:S(2)}) copy-start(bf16[1024,128]{1,0:T(8,128)(2,1)} %rec_ref.1) | copy-start | bytes 786436
  1.6 0.7 copy-start.3
  2.3 0.7 copy-start.4
  4.9 27.3 %copy-start = (bf16[32,3,96,96]{3,2,1,0:T(8,128)(2,1)S(1)}, bf16[32,3,96,96]{3,2,1,0:T(8,128)(2,1)}, u32[]{:S(2)}) copy-start(bf16[32,3,96,96]{3,2,1,0:T(8,128)(2,1)} %stiff_ref.3) | copy-start | bytes 5308420
  4.9 27.3 %copy-start.1 = (s32[32,3]{0,1:T(4,128)S(1)}, s32[32,3]{0,1:T(4,128)}, u32[]{:S(2)}) copy-start(s32[32,3]{0,1:T(4,128)} %param.11) | copy-start | bytes 1156
  31.3 6.4 %collective-permute-start = (bf16[768,128]{1,0:T(8,128)(2,1)S(1)}, bf16[768,128]{1,0:T(8,128)(2,1)S(1)}, u32[]{:S(2)}, u32[]{:S(2)}) collective-permute-start(bf16[768,128]{1,0:T(8,128)(2,1)S(1)} %get-tuple-element.18.near_ref), channel_id=1, source_target_pairs={{0,1},{1,0},{2,3},{3,2},{4,5},{5,4},{6,7},{7,6},{8,9},{9,8},{10,11... | collective-permute-start | bytes 589832 | tf_op jit(solution)/shard_map/ppermute | solution.py:269
  31.5 6.3 %collective-permute-start.1 = (bf16[768,128]{1,0:T(8,128)(2,1)S(1)}, bf16[768,128]{1,0:T(8,128)(2,1)S(1)}, u32[]{:S(2)}, u32[]{:S(2)}) collective-permute-start(bf16[768,128]{1,0:T(8,128)(2,1)S(1)} %get-tuple-element.19.far_ref), channel_id=1, source_target_pairs={{1,2},{3,4},{5,6},{7,8},{9,10},{11,12},{13,14},{2,1},{4,3},{6,5},{... | collective-permute-start | bytes 589832 | tf_op jit(solution)/shard_map/ppermute | solution.py:273
  41.7 3.2 %collective-permute-start.2 = (f32[64,1024]{1,0:T(8,128)S(1)}, f32[64,1024]{1,0:T(8,128)S(1)}, u32[]{:S(2)}, u32[]{:S(2)}) collective-permute-start(f32[64,1024]{1,0:T(8,128)S(1)} %get-tuple-element.23), channel_id=1, source_target_pairs={{0,1},{1,0},{2,3},{3,2},{4,5},{5,4},{6,7},{7,6},{8,9},{9,8},{10,11... | collective-permute-start | bytes 786440 | tf_op jit(solution)/shard_map/ppermute | solution.py:269
  44.9 4.4 %collective-permute-start.3 = (bf16[32,1024]{1,0:T(8,128)(2,1)S(1)}, bf16[32,1024]{1,0:T(8,128)(2,1)S(1)}, u32[]{:S(2)}, u32[]{:S(2)}) collective-permute-start(bf16[32,1024]{1,0:T(8,128)(2,1)S(1)} %get-tuple-element.25), channel_id=1, source_target_pairs={{0,2},{1,3},{2,0},{3,1},{4,6},{5,7},{6,4},{7,5},{8,10},{9,11},{10,... | collective-permute-start | bytes 196616 | tf_op jit(solution)/shard_map/ppermute | solution.py:269
  49.4 7.3 %collective-permute-start.6 = (bf16[32,1024]{1,0:T(8,128)(2,1)S(1)}, bf16[32,1024]{1,0:T(8,128)(2,1)S(1)}, u32[]{:S(2)}, u32[]{:S(2)}) collective-permute-start(bf16[32,1024]{1,0:T(8,128)(2,1)S(1)} %get-tuple-element.27), channel_id=1, source_target_pairs={{0,4},{1,5},{2,6},{3,7},{4,0},{5,1},{6,2},{7,3},{8,12},{9,13},{10,... | collective-permute-start | bytes 196616 | tf_op jit(solution)/shard_map/ppermute | solution.py:269
  51.4 6.8 %collective-permute-start.5 = (bf16[32,1024]{1,0:T(8,128)(2,1)S(1)}, bf16[32,1024]{1,0:T(8,128)(2,1)S(1)}, u32[]{:S(2)}, u32[]{:S(2)}) collective-permute-start(bf16[32,1024]{1,0:T(8,128)(2,1)S(1)} %get-tuple-element.27), channel_id=1, source_target_pairs={{0,8},{1,9},{2,10},{3,11},{4,12},{5,13},{6,14},{7,15},{8,0},{9,1},... | collective-permute-start | bytes 196616 | tf_op jit(solution)/shard_map/ppermute | solution.py:269
  52.8 6.2 %collective-permute-start.4 = (bf16[32,1024]{1,0:T(8,128)(2,1)S(1)}, bf16[32,1024]{1,0:T(8,128)(2,1)S(1)}, u32[]{:S(2)}, u32[]{:S(2)}) collective-permute-start(bf16[32,1024]{1,0:T(8,128)(2,1)S(1)} %get-tuple-element.27), channel_id=1, source_target_pairs={{0,12},{1,13},{2,14},{3,15},{4,8},{5,9},{6,10},{7,11},{8,4},{9,5},... | collective-permute-start | bytes 196616 | tf_op jit(solution)/shard_map/ppermute | solution.py:269
  60.9 4.3 %collective-permute-start.7 = (bf16[32,1024]{1,0:T(8,128)(2,1)S(1)}, bf16[32,1024]{1,0:T(8,128)(2,1)S(1)}, u32[]{:S(2)}, u32[]{:S(2)}) collective-permute-start(bf16[32,1024]{1,0:T(8,128)(2,1)S(1)} %shard_map.93.own_ref), channel_id=1, source_target_pairs={{0,2},{1,3},{2,0},{3,1},{4,6},{5,7},{6,4},{7,5},{8,10},{9,11},{10,... | collective-permute-start | bytes 196616 | tf_op jit(solution)/shard_map/ppermute | solution.py:269
  61.2 3.9 %collective-permute-start.8 = (bf16[32,1024]{1,0:T(8,128)(2,1)S(1)}, bf16[32,1024]{1,0:T(8,128)(2,1)S(1)}, u32[]{:S(2)}, u32[]{:S(2)}) collective-permute-start(bf16[32,1024]{1,0:T(8,128)(2,1)S(1)} %shard_map.93.own_ref), channel_id=1, source_target_pairs={{0,1},{1,0},{2,3},{3,2},{4,5},{5,4},{6,7},{7,6},{8,9},{9,8},{10,11... | collective-permute-start | bytes 196616 | tf_op jit(solution)/shard_map/ppermute | solution.py:269
  65.1 1.3 %collective-permute-start.9 = (bf16[32,1024]{1,0:T(8,128)(2,1)S(1)}, bf16[32,1024]{1,0:T(8,128)(2,1)S(1)}, u32[]{:S(2)}, u32[]{:S(2)}) collective-permute-start(bf16[32,1024]{1,0:T(8,128)(2,1)S(1)} %collective-permute-done.7.y_ref), channel_id=1, source_target_pairs={{0,1},{1,0},{2,3},{3,2},{4,5},{5,4},{6,7},{7,6},{8,9},{9,8},{10,11... | collective-permute-start | bytes 196616 | tf_op jit(solution)/shard_map/ppermute | solution.py:269

commit v2 on v1

v2 whole, which is shorter than its diff:
```python
import functools

import jax
import jax.numpy as jnp
from jax import lax
from jax.experimental import pallas as pl
from jax.experimental.pallas import tpu as pltpu
from jax.sharding import PartitionSpec as P

LANES = 128
TAIL = 16
REACH = 8
BF = jnp.bfloat16
F32 = jnp.float32
NT = (((1,), (1,)), ((), ()))
NN = (((1,), (0,)), ((), ()))
TN = (((0,), (0,)), ((), ()))


def call(kernel, out_shape, *operands, smem=(), hbm=(), out=pltpu.VMEM, scratch=(), flops=0, limit=16 * 2**20):
    space = [
        pltpu.SMEM if k in smem else pltpu.HBM if k in hbm else pltpu.VMEM
        for k in range(len(operands))
    ]
    moved = sum(x.size * x.dtype.itemsize for x in operands)
    return pl.pallas_call(
        kernel,
        out_shape=out_shape,
        in_specs=[pl.BlockSpec(memory_space=s) for s in space],
        out_specs=jax.tree.map(lambda _: pl.BlockSpec(memory_space=out), out_shape),
        scratch_shapes=list(scratch),
        compiler_params=pltpu.CompilerParams(vmem_limit_bytes=limit),
        cost_estimate=pl.CostEstimate(flops=flops, bytes_accessed=moved, transcendentals=0),
    )(*operands)


def shape(dims, dtype):
    return jax.ShapeDtypeStruct(dims, dtype)


def odd_core():
    return lax.rem(lax.axis_index("elem"), 2)


def hot(rows, key):
    row = lax.broadcasted_iota(jnp.int32, (rows, key.shape[1]), 0).astype(F32).astype(BF)
    return jnp.where(row == key, jnp.ones((), BF), jnp.zeros((), BF))


def write_messages(cross, cap, chips, owner, rank, records, slots_ref, out_ref):
    me = lax.axis_index("elem")
    core = lax.rem(me + cross, 2)
    y, z = lax.rem(me // 2, 2), me // 4
    share, owners = LANES // cap, 2 * chips
    tail_row = lax.broadcasted_iota(jnp.int32, (TAIL, LANES), 0) - 2 * cross
    for j in range(chips):
        dz, dy = j // 2, j % 2
        to = (lax.rem(z + dz, chips // 2) * 2 + lax.rem(y + dy, 2)) * 2 + core
        key = jnp.where(owner == to, rank, -1.0).astype(BF)
        out_ref[j, 0:cap, :] = jnp.dot(
            hot(cap, key), records, preferred_element_type=F32
        ).astype(BF)
        place = (dy * 2 + cross) % share
        high = slots_ref[place, pl.ds(to, 1), :]
        low = slots_ref[place, pl.ds(owners + to, 1), :]
        tail = jnp.where(tail_row == 0, high, jnp.where(tail_row == 1, low, 0.0))
        out_ref[j, cap : cap + TAIL, :] = tail.astype(BF)


def pack_kernel(
    cap, owner_ref, slot_ref, rec_ref, cross_ref, rank_ref, slots_ref, held_ref
):
    pan = rec_ref.shape[0]
    owners = slots_ref.shape[1] // 2
    pieces = pan // LANES
    before = lax.broadcasted_iota(jnp.int32, (LANES, LANES), 0)
    after = lax.broadcasted_iota(jnp.int32, (LANES, LANES), 1)
    triangle = jnp.where(before <= after, 1.0, 0.0).astype(BF)
    owner = owner_ref[...]
    slot = jnp.concatenate([slot_ref[k : k + 1, :] for k in range(pieces)], axis=1)
    held_ref[...] = rec_ref[...]
    match = lax.broadcasted_iota(jnp.int32, (owners, pan), 0) == owner
    match_f = jnp.where(match, 1.0, 0.0)
    stacked = jnp.concatenate(
        [match_f[:, k * LANES : (k + 1) * LANES] for k in range(pieces)], axis=0
    ).astype(BF)
    running = jnp.dot(stacked, triangle, preferred_element_type=F32)
    offset = jnp.zeros((owners, 1), F32)
    ranks = []
    for k in range(pieces):
        piece = running[k * owners : (k + 1) * owners] + offset
        picked = match_f[:, k * LANES : (k + 1) * LANES] * piece
        ranks.append(jnp.sum(picked, axis=0, keepdims=True) - 1.0)
        offset = piece[:, LANES - 1 : LANES]
    rank = jnp.concatenate(ranks, axis=1)
    rank_ref[...] = rank
    high = (slot >> 6).astype(F32)
    low = (slot & 63).astype(F32)
    weights = jnp.concatenate([match_f * high, match_f * low], axis=0).astype(BF)
    for place in range(LANES // cap):
        spread = hot(LANES, (rank + float(place * cap)).astype(BF))
        slots_ref[place] = lax.dot_general(weights, spread, NT, preferred_element_type=F32)
    write_messages(1, cap, owners // 2, owner, rank, rec_ref[...], slots_ref, cross_ref)


def pack_own_kernel(cap, owner_ref, rank_ref, slots_ref, rec_ref, own_ref):
    chips = slots_ref.shape[1] // 4
    write_messages(
        0, cap, chips, owner_ref[...], rank_ref[...], rec_ref[...], slots_ref, own_ref
    )


def merge_kernel(cap, own_ref, cross_ref, *out_refs):
    for j, ref in enumerate(out_refs):
        ref[0:cap] = own_ref[j, 0:cap]
        ref[cap : 2 * cap] = cross_ref[j, 0:cap]
        ref[2 * cap :] = own_ref[j, cap:] + cross_ref[j, cap:]


def loads_at(slots, records, base, rows):
    key = slots - base.astype(F32)
    key = jnp.where((key >= 0.0) & (key < float(rows)), key, -1.0).astype(BF)
    return jnp.dot(hot(rows, key), records, preferred_element_type=F32).astype(BF)


CHUNK = 256


def far_kernel(cap, elem_rows, count, *refs):
    got_refs, (far_ref, slots_ref, records_ref) = refs[:count], refs[count:]
    share = LANES // cap
    order = [(ref, x) for ref in got_refs for x in range(2)]
    for k, ref in enumerate(got_refs):
        records_ref[2 * k * cap : 2 * (k + 1) * cap, :] = ref[0 : 2 * cap, :]
    rows = []
    for group in range(len(order) // share):
        row = None
        for ref, x in order[group * share : (group + 1) * share]:
            tail = ref[2 * cap :, :].astype(F32)
            part = tail[2 * x : 2 * x + 1] * 64.0 + tail[2 * x + 1 : 2 * x + 2]
            row = part if row is None else row + part
        rows.append(row)
    slots = jnp.concatenate(rows, axis=1)
    slots_ref[...] = slots
    halo = far_ref.shape[0]
    first = jnp.where(odd_core() == 1, elem_rows - halo, 0)
    records = records_ref[...]
    for k in range(halo // CHUNK):
        far_ref[k * CHUNK : (k + 1) * CHUNK, :] = loads_at(
            slots, records, first + k * CHUNK, CHUNK
        )


def near_kernel(elem_rows, slots_ref, records_ref, near_ref):
    halo = near_ref.shape[0]
    first = jnp.where(odd_core() == 1, 0, elem_rows - halo)
    for k in range(halo // CHUNK):
        near_ref[k * CHUNK : (k + 1) * CHUNK, :] = loads_at(
            slots_ref[...], records_ref[...], first + k * CHUNK, CHUNK
        )


def stiffen(stiff_ref, cols_ref, loads_ref, block, first_col):
    size = stiff_ref.shape[2]
    total = None
    for j in range(stiff_ref.shape[1]):
        start = pl.multiple_of((cols_ref[j, block] - first_col) * size, 32)
        part = jnp.dot(
            stiff_ref[block, j], loads_ref[pl.ds(start, size), :], preferred_element_type=F32
        )
        total = part if total is None else total + part
    return total.astype(BF)


def middle_kernel(
    slots_ref, records_ref, near_ref, far_ref, stiff_ref, cols_ref, loads_ref, st_ref
):
    elem_rows = loads_ref.shape[0]
    halo = near_ref.shape[0]
    blocks, _, size, _ = stiff_ref.shape
    odd = odd_core()
    last = elem_rows - halo
    near_at = pl.multiple_of(jnp.where(odd == 1, 0, last), 32)
    far_at = pl.multiple_of(jnp.where(odd == 1, last, 0), 32)
    loads_ref[pl.ds(near_at, halo), :] = near_ref[...]
    loads_ref[pl.ds(far_at, halo), :] = far_ref[...]
    for k in range((last - halo) // CHUNK):
        base = halo + k * CHUNK
        loads_ref[base : base + CHUNK, :] = loads_at(
            slots_ref[...], records_ref[...], jnp.int32(base), CHUNK
        )
    first_col = lax.axis_index("elem") * blocks
    for b in range(REACH, blocks - REACH):
        st_ref[(b - REACH) * size : (b - REACH + 1) * size, :] = stiffen(
            stiff_ref, cols_ref, loads_ref, b, first_col
        )


def outer_rows(side, loads_ref, got_ref, stiff_ref, cols_ref, st_ref, ext_ref):
    halo = got_ref.shape[0]
    blocks, _, size, _ = stiff_ref.shape
    end = halo + loads_ref.shape[0]
    got_at = pl.multiple_of(side * end, 32)
    ext_ref[halo:end, :] = loads_ref[...]
    ext_ref[pl.ds(got_at, halo), :] = got_ref[...]
    first_col = lax.axis_index("elem") * blocks - REACH
    for k in range(REACH):
        st_ref[k * size : (k + 1) * size, :] = stiffen(
            stiff_ref, cols_ref, ext_ref, side * (blocks - REACH) + k, first_col
        )


def near_rows_kernel(
    loads_ref, got_ref, stiff_ref, cols_ref, modes_ref, mid_ref, st_ref, modal_ref, ext_ref
):
    side = 1 - odd_core()
    outer_rows(side, loads_ref, got_ref, stiff_ref, cols_ref, st_ref, ext_ref)
    halo = got_ref.shape[0]
    last = modes_ref.shape[0] - halo
    at = pl.multiple_of(side * last, 32)
    modal_ref[...] = lax.dot_general(
        mid_ref[...], modes_ref[halo:last, :], TN, preferred_element_type=F32
    ) + lax.dot_general(
        st_ref[...], modes_ref[pl.ds(at, halo), :], TN, preferred_element_type=F32
    )


def far_rows_kernel(
    loads_ref, got_ref, stiff_ref, cols_ref, modes_ref, near_ref, modal_ref,
    edge_ref, keep_ref, send_ref, ext_ref, st_ref, total_ref,
):
    odd = odd_core()
    outer_rows(odd, loads_ref, got_ref, stiff_ref, cols_ref, st_ref, ext_ref)
    halo = got_ref.shape[0]
    last = modes_ref.shape[0] - halo
    at = pl.multiple_of(odd * last, 32)
    total_ref[...] = modal_ref[...] + lax.dot_general(
        st_ref[...], modes_ref[pl.ds(at, halo), :], TN, preferred_element_type=F32
    )
    half = total_ref.shape[0] // 2
    keep_ref[...] = total_ref[pl.ds(pl.multiple_of(odd * half, 8), half), :]
    send_ref[...] = total_ref[pl.ds(pl.multiple_of((1 - odd) * half, 8), half), :]
    edge_ref[pl.ds(pl.multiple_of(odd * halo, 32), halo), :] = st_ref[...]
    edge_ref[pl.ds(pl.multiple_of((1 - odd) * halo, 32), halo), :] = near_ref[...]


def pair_kernel(mine_ref, other_ref, keep_ref, send_ref, total_ref):
    bit = lax.rem(lax.axis_index("elem") // 2, 2)
    total_ref[...] = mine_ref[...] + other_ref[...]
    half = total_ref.shape[0] // 2
    keep_ref[...] = total_ref[pl.ds(pl.multiple_of(bit * half, 8), half), :]
    send_ref[...] = total_ref[pl.ds(pl.multiple_of((1 - bit) * half, 8), half), :].astype(BF)


def add_kernel(mine_ref, other_ref, total_ref, send_ref):
    total = mine_ref[...] + other_ref[...].astype(F32)
    total_ref[...] = total
    send_ref[...] = total.astype(BF)


def split_kernel(a_ref, high_ref, low_ref):
    a = a_ref[...].T
    high = a.astype(BF)
    high_ref[...] = high
    low_ref[...] = (a - high.astype(F32)).astype(BF)


def admit_kernel(count, mine_ref, *refs):
    others, (high_ref, low_ref, adj_ref) = refs[:count], refs[count:]
    total = mine_ref[...]
    for other in others:
        total += other[...].astype(F32)
    high = total.astype(BF)
    low = (total - high.astype(F32)).astype(BF)
    both = lax.dot_general(
        jnp.concatenate([high, low], axis=0), high_ref[...], NN, preferred_element_type=F32
    )
    rows = mine_ref.shape[0]
    adj = both[:rows] + both[rows:]
    adj += lax.dot_general(high, low_ref[...], NN, preferred_element_type=F32)
    adj_ref[...] = adj.astype(BF)


def back_kernel(
    own_ref, y_ref, core_ref, both_ref, modes_ref, mid_ref, edge_ref, adj_hbm, sens_hbm,
    adj_ref, sens_ref, field_ref, sems,
):
    me = lax.axis_index("elem")
    odd = lax.rem(me, 2)
    bit = lax.rem(me // 2, 2)
    quarter = own_ref.shape[0]
    for ref, c, y in (
        (own_ref, odd, bit),
        (y_ref, odd, 1 - bit),
        (core_ref, 1 - odd, bit),
        (both_ref, 1 - odd, 1 - bit),
    ):
        at = pl.multiple_of((2 * c + y) * quarter, 16)
        field_ref[pl.ds(at, quarter), :] = ref[...]
    field = field_ref[...]
    elem_rows = modes_ref.shape[0]
    halo = edge_ref.shape[0] // 2
    last = elem_rows - halo
    leaving = []
    for k in range(elem_rows // CHUNK):
        at = k * CHUNK
        part = lax.dot_general(
            modes_ref[at : at + CHUNK, :], field, NT, preferred_element_type=F32
        )
        adj_ref[at : at + CHUNK, :] = part.astype(BF)
        rows = pl.ds(at, CHUNK)
        leaving.append(pltpu.make_async_copy(adj_ref.at[rows], adj_hbm.at[rows], sems.at[k]))
        leaving[-1].start()
        if at < halo:
            st = edge_ref[at : at + CHUNK, :]
        elif at < last:
            st = mid_ref[at - halo : at - halo + CHUNK, :]
        else:
            st = edge_ref[at - last + halo : at - last + halo + CHUNK, :]
        product = part * st.astype(F32)
        for i in range(CHUNK // LANES):
            row = jnp.sum(product[i * LANES : (i + 1) * LANES, :].T, axis=0, keepdims=True)
            sens_ref[at // LANES + i : at // LANES + i + 1, :] = row
    leaving.append(pltpu.make_async_copy(sens_ref, sens_hbm, sems.at[elem_rows // CHUNK]))
    leaving[-1].start()
    for copy in leaving:
        copy.wait()


def body(records, panel_owner, panel_slot, stiff_blocks, block_cols, modes, admittance):
    owners = lax.axis_size("elem")
    chips = owners // 2
    pan, width = records.shape
    cap = 2 * pan // owners
    share = LANES // cap
    elem_rows, mode_count = modes.shape
    blocks, nnz, size, _ = stiff_blocks.shape
    halo = REACH * size
    message = (chips, cap + TAIL, width)

    def swap(array, mask):
        return lax.ppermute(array, "elem", [(i, i ^ mask) for i in range(owners)])

    def swap_far(array):
        pairs = [(i, i + 1) for i in range(1, owners - 1, 2)]
        return lax.ppermute(array, "elem", pairs + [(j, i) for i, j in pairs])

    def turn(array, dz, dy):
        pairs = []
        for i in range(owners):
            z, y, core = i // 4, i // 2 % 2, i % 2
            pairs.append((i, ((z + dz) % (chips // 2) * 2 + (y + dy) % 2) * 2 + core))
        return lax.ppermute(array, "elem", pairs)

    owner = panel_owner.reshape(1, pan)
    cross, rank, slots, held = call(
        functools.partial(pack_kernel, cap),
        (
            shape(message, BF),
            shape((1, pan), F32),
            shape((share, 2 * owners, LANES), F32),
            shape((pan, width), BF),
        ),
        owner,
        panel_slot.reshape(pan // LANES, LANES),
        records,
        flops=owners * cap * pan * width,
    )
    got_cross = swap(cross, 1)
    own = call(
        functools.partial(pack_own_kernel, cap),
        shape(message, BF),
        owner, rank, slots, held,
        flops=owners * cap * pan * width,
    )
    packed = call(
        functools.partial(merge_kernel, cap),
        (shape((2 * cap + TAIL, width), BF),) * chips,
        own, got_cross,
    )
    offsets = range(1, chips)
    got = {j: turn(packed[j], j // 2, j % 2) for j in offsets}
    got[0] = packed[0]
    total_rows = owners * cap
    far, slot_row, landed = call(
        functools.partial(far_kernel, cap, elem_rows, chips),
        (shape((halo, width), BF), shape((1, total_rows), F32), shape((total_rows, width), BF)),
        *[got[j] for j in range(chips)],
        flops=8 * total_rows * halo * width,
    )
    got_far = swap_far(far)
    near = call(
        functools.partial(near_kernel, elem_rows),
        shape((halo, width), BF),
        slot_row, landed,
        flops=2 * total_rows * halo * width,
    )
    got_near = swap(near, 1)
    cols = block_cols.T
    loads, st_mid = call(
        middle_kernel,
        (shape((elem_rows, width), BF), shape((elem_rows - 2 * halo, width), BF)),
        slot_row, landed, near, far, stiff_blocks, cols,
        smem=(5,),
        flops=4 * total_rows * halo * width,
    )
    extended = pltpu.VMEM((elem_rows + 2 * halo, width), BF)
    st_near, modal_near = call(
        near_rows_kernel,
        (shape((halo, width), BF), shape((width, mode_count), F32)),
        loads, got_near, stiff_blocks, cols, modes, st_mid,
        smem=(3,),
        scratch=(extended,),
        flops=2 * (elem_rows - halo) * width * mode_count,
    )
    st_edge, keep, send = call(
        far_rows_kernel,
        (
            shape((2 * halo, width), BF),
            shape((width // 2, mode_count), F32),
            shape((width // 2, mode_count), F32),
        ),
        loads, got_far, stiff_blocks, cols, modes, st_near, modal_near,
        smem=(3,),
        scratch=(extended, pltpu.VMEM((halo, width), BF), pltpu.VMEM((width, mode_count), F32)),
        flops=2 * halo * width * mode_count,
    )
    quarter = width // 4
    piece = shape((quarter, mode_count), BF)
    keep, send = call(
        pair_kernel,
        (shape((quarter, mode_count), F32), piece),
        keep, swap(send, 1),
        scratch=(pltpu.VMEM((width // 2, mode_count), F32),),
    )
    total, send = call(
        add_kernel, (shape((quarter, mode_count), F32), piece), keep, swap(send, 2)
    )
    groups = chips // 2
    steps = sorted(range(1, groups), key=lambda k: min(k, groups - k))
    others = [turn(send, k, 0) for k in steps]
    a_high, a_low = call(
        split_kernel,
        (shape(admittance.shape, BF), shape(admittance.shape, BF)),
        admittance,
        flops=4 * admittance.size,
    )
    mine = call(
        functools.partial(admit_kernel, len(others)),
        piece,
        total, *others, a_high, a_low,
        flops=6 * quarter * mode_count * mode_count,
    )
    across = swap(mine, 2)
    beside = swap(mine, 1)
    both = swap(across, 1)
    adjoint, sensitivity = call(
        back_kernel,
        (shape((elem_rows, width), BF), shape((elem_rows // LANES, LANES), F32)),
        mine, across, beside, both, modes, st_mid, st_edge,
        out=pltpu.HBM,
        scratch=(
            pltpu.VMEM((elem_rows, width), BF),
            pltpu.VMEM((elem_rows // LANES, LANES), F32),
            pltpu.VMEM((width, mode_count), BF),
            pltpu.SemaphoreType.DMA((elem_rows // CHUNK + 1,)),
        ),
        flops=2 * elem_rows * width * mode_count,
    )
    return adjoint, sensitivity.reshape(elem_rows)


def solution(mesh):
    in_specs = (
        P(("case", "elem"), None),
        P("elem", None),
        P("elem"),
        P("elem", None, None, None),
        P("elem", None),
        P("elem", None),
        P("case", None),
    )
    out_specs = (P(("case", "elem"), None), P(("case", "elem")))
    return jax.shard_map(body, mesh=mesh, in_specs=in_specs, out_specs=out_specs, check_vma=False)
```

time: 72.3 us -> 63.1 us (0.87)
  blocking collectives: 24.6 us -> 0 us
  starting transfers between devices: 9.55 us -> 25.9 us
  Pallas kernels: 23.6 us -> 14.9 us
  waiting for transfers between devices: 11.1 us -> 18.9 us
    all_to_all x1 -> x0, blocking collectives: 24.6 us -> none  [body(): lax.all_to_all(packed, 'elem', split_axis=0, concat_axis=0, tiled=True)]
    ppermute x0 -> x10, starting transfers between devices: none -> 17.8 us  [turn(): return lax.ppermute(array, 'elem', pairs)]
    ppermute x0 -> x10, waiting for transfers between devices: none -> 10.2 us  [turn(): return lax.ppermute(array, 'elem', pairs)]
    pallas_call x9 -> x13, Pallas kernels: 23.6 us -> 14.9 us  [call(): pl.pallas_call(kernel, out_shape=out_shape, in_specs=[pl.BlockSpec(memory...]
    ppermute x9 -> x7, waiting for transfers between devices: 11.1 us -> 8.65 us  [swap(): return lax.ppermute(array, 'elem', [(i, i ^ mask) for i in range(owners)])]
    ppermute x9 -> x7, starting transfers between devices: 8.89 us -> 7.35 us  [swap(): return lax.ppermute(array, 'elem', [(i, i ^ mask) for i in range(owners)])]
    unnamed x10 -> x16, local copies, waits for them, and re-layouts: 2.33 us -> 2.34 us
  transfers between devices with their start and end apart: 10 -> 18, of which waited for: 6 -> 10; matrix products, arithmetic and copies ran while one was open for 0% -> 0% of each run, Pallas kernels for 12% -> 10%
where the time goes in v2:
time: 63.1 us; the launch traced here: 62.9 us
  starting transfers between devices  25.9 us (41%)
  waiting for transfers between devices  18.9 us (30%)
  Pallas kernels  14.9 us (24%)
  local copies, waits for them, and re-layouts  2.34 us (4%)
  between operations  0.97 us (2%)
    ppermute x10, starting transfers between devices, turn(): return lax.ppermute(array, 'elem', pairs)  17.8 us
    pallas_call x13, Pallas kernels, call(): pl.pallas_call(kernel, out_shape=out_shape, in_specs=[pl.BlockSpec(memory...  14.9 us
    ppermute x10, waiting for transfers between devices, turn(): return lax.ppermute(array, 'elem', pairs)  10.2 us
    ppermute x7, waiting for transfers between devices, swap(): return lax.ppermute(array, 'elem', [(i, i ^ mask) for i in range(owners)])  8.65 us
    ppermute x7, starting transfers between devices, swap(): return lax.ppermute(array, 'elem', [(i, i ^ mask) for i in range(owners)])  7.35 us
    unnamed x16, local copies, waits for them, and re-layouts  2.34 us
  transfers between devices with their start and end apart: 18, of which 10 were waited for; matrix products, arithmetic and copies ran while one was open for 0% of the time, Pallas kernels for 10%

profile of v2, /device:TPU:0, one launch (start us, length us, event | category | flops | bytes accessed | tf_op | source)
XLA Modules:
  0.0 62.9 jit_solution(4421826994556778318)
XLA Ops:
  3.0 1.4 %shard_map.86 = (bf16[8,144,128]{2,1,0:T(8,128)(2,1)S(1)}, f32[1,1024]{1,0:T(1,128)S(1)}, f32[1,32,128]{2,1,0:T(8,128)S(1)}, bf16[1024,128]{1,0:T(8,128)(2,1)S(1)}) custom-call(s32[1,1024]{1,0:T(1,128)S(1)} %bitcast.10, s32[8,128]{1,0:T(8,128)S(1)} %bitcast.9, bf16[1024,128]{1,0:T(8,128)(2,1)S(1)} %copy-done.3), custom_call_target="tpu_custom_call" | custom-call | flops 268435456 | bytes 270336 | tf_op jit(solution)/shard_map/pallas_call | solution.py:26
  6.1 3.0 %collective-permute-start.1 = (bf16[272,128]{1,0:T(8,128)(2,1)S(1)}, bf16[272,128]{1,0:T(8,128)(2,1)S(1)}, u32[]{:S(2)}, u32[]{:S(2)}) collective-permute-start(bf16[272,128]{1,0:T(8,128)(2,1)S(1)} %get-tuple-element.37), channel_id=1, source_target_pairs={{0,2},{1,3},{2,0},{3,1},{4,6},{5,7},{6,4},{7,5},{8,10},{9,11},{10,... | collective-permute-start | bytes 208904 | tf_op jit(solution)/shard_map/ppermute | solution.py:353
  9.1 1.6 %collective-permute-start.2 = (bf16[272,128]{1,0:T(8,128)(2,1)S(1)}, bf16[272,128]{1,0:T(8,128)(2,1)S(1)}, u32[]{:S(2)}, u32[]{:S(2)}) collective-permute-start(bf16[272,128]{1,0:T(8,128)(2,1)S(1)} %get-tuple-element.38), channel_id=1, source_target_pairs={{0,4},{1,5},{2,6},{3,7},{4,8},{5,9},{6,10},{7,11},{8,12},{9,13},{1... | collective-permute-start | bytes 208904 | tf_op jit(solution)/shard_map/ppermute | solution.py:353
  10.6 1.5 %collective-permute-start.3 = (bf16[272,128]{1,0:T(8,128)(2,1)S(1)}, bf16[272,128]{1,0:T(8,128)(2,1)S(1)}, u32[]{:S(2)}, u32[]{:S(2)}) collective-permute-start(bf16[272,128]{1,0:T(8,128)(2,1)S(1)} %get-tuple-element.39), channel_id=1, source_target_pairs={{0,6},{1,7},{2,4},{3,5},{4,10},{5,11},{6,8},{7,9},{8,14},{9,15},{1... | collective-permute-start | bytes 208904 | tf_op jit(solution)/shard_map/ppermute | solution.py:353
  12.2 1.1 %collective-permute-start.4 = (bf16[272,128]{1,0:T(8,128)(2,1)S(1)}, bf16[272,128]{1,0:T(8,128)(2,1)S(1)}, u32[]{:S(2)}, u32[]{:S(2)}) collective-permute-start(bf16[272,128]{1,0:T(8,128)(2,1)S(1)} %get-tuple-element.40), channel_id=1, source_target_pairs={{0,8},{1,9},{2,10},{3,11},{4,12},{5,13},{6,14},{7,15},{8,0},{9,1},... | collective-permute-start | bytes 208904 | tf_op jit(solution)/shard_map/ppermute | solution.py:353
  13.2 2.8 %collective-permute-start.5 = (bf16[272,128]{1,0:T(8,128)(2,1)S(1)}, bf16[272,128]{1,0:T(8,128)(2,1)S(1)}, u32[]{:S(2)}, u32[]{:S(2)}) collective-permute-start(bf16[272,128]{1,0:T(8,128)(2,1)S(1)} %get-tuple-element.41), channel_id=1, source_target_pairs={{0,10},{1,11},{2,8},{3,9},{4,14},{5,15},{6,12},{7,13},{8,2},{9,3},... | collective-permute-start | bytes 208904 | tf_op jit(solution)/shard_map/ppermute | solution.py:353
  16.0 2.2 %collective-permute-start.6 = (bf16[272,128]{1,0:T(8,128)(2,1)S(1)}, bf16[272,128]{1,0:T(8,128)(2,1)S(1)}, u32[]{:S(2)}, u32[]{:S(2)}) collective-permute-start(bf16[272,128]{1,0:T(8,128)(2,1)S(1)} %get-tuple-element.42), channel_id=1, source_target_pairs={{0,12},{1,13},{2,14},{3,15},{4,0},{5,1},{6,2},{7,3},{8,4},{9,5},{1... | collective-permute-start | bytes 208904 | tf_op jit(solution)/shard_map/ppermute | solution.py:353
  18.5 2.5 %collective-permute-done.4.refs_4_ = bf16[272,128]{1,0:T(8,128)(2,1)S(1)} collective-permute-done((bf16[272,128]{1,0:T(8,128)(2,1)S(1)}, bf16[272,128]{1,0:T(8,128)(2,1)S(1)}, u32[]{:S(2)}, u32[]{:S(2)}) %collective-permute-start.4) | collective-permute-done | bytes 69664 | tf_op jit(solution)/shard_map/ppermute | solution.py:353
  21.1 2.7 %collective-permute-done.5.refs_5_ = bf16[272,128]{1,0:T(8,128)(2,1)S(1)} collective-permute-done((bf16[272,128]{1,0:T(8,128)(2,1)S(1)}, bf16[272,128]{1,0:T(8,128)(2,1)S(1)}, u32[]{:S(2)}, u32[]{:S(2)}) %collective-permute-start.5) | collective-permute-done | bytes 69664 | tf_op jit(solution)/shard_map/ppermute | solution.py:353
  24.0 1.0 %shard_map.89 = (bf16[768,128]{1,0:T(8,128)(2,1)S(1)}, f32[1,2048]{1,0:T(1,128)S(1)}, bf16[2048,128]{1,0:T(8,128)(2,1)S(1)}) custom-call(bf16[272,128]{1,0:T(8,128)(2,1)S(1)} %get-tuple-element.36.refs_0_, bf16[272,128]{1,0:T(8,128)(2,1)S(1)} %collective-permute-done.1.refs_1_, bf16[272,128]{1,0:T(8,128)(2,1)S(1)} %collective-permute-done.2.refs_2_, ...), custom_call_target="tpu_custom_call" | custom-call | flops 1610612736 | bytes 557056 | tf_op jit(solution)/shard_map/pallas_call | solution.py:26
  26.8 2.8 %shard_map.91 = (bf16[3072,128]{1,0:T(8,128)(2,1)S(1)}, bf16[1536,128]{1,0:T(8,128)(2,1)S(1)}) custom-call(f32[1,2048]{1,0:T(1,128)S(1)} %get-tuple-element.44.slots_ref, bf16[2048,128]{1,0:T(8,128)(2,1)S(1)} %get-tuple-element.45.records_ref, bf16[768,128]{1,0:T(8,128)(2,1)S(1)} %shard_map.90.near_ref, bf16[768,128]{1,0:T(8,128)(2,1)S(1)} %get-tuple-element.46.far_ref, ...), custom_call_target="tpu_custom_call" | custom-call | flops 805306368 | bytes 2695552 | tf_op jit(solution)/shard_map/pallas_call | solution.py:26
  29.7 1.7 %shard_map.92 = (bf16[768,128]{1,0:T(8,128)(2,1)S(1)}, f32[128,1024]{1,0:T(8,128)S(1)}) custom-call(bf16[3072,128]{1,0:T(8,128)(2,1)S(1)} %get-tuple-element.47.loads_ref, bf16[768,128]{1,0:T(8,128)(2,1)S(1)} %collective-permute-done.9.got_ref, bf16[32,3,96,96]{3,2,1,0:T(8,128)(2,1)S(1)} %copy-done, s32[3,32]{1,0:T(4,128)S(1)} %bitcast.7, ...), custom_call_target="tpu_custom_call" | custom-call | flops 603979776 | bytes 9437568 | tf_op jit(solution)/shard_map/pallas_call | solution.py:26
  31.4 1.3 %shard_map.93 = (bf16[1536,128]{1,0:T(8,128)(2,1)S(1)}, f32[64,1024]{1,0:T(8,128)S(1)}, f32[64,1024]{1,0:T(8,128)S(1)}) custom-call(bf16[3072,128]{1,0:T(8,128)(2,1)S(1)} %get-tuple-element.47.loads_ref, bf16[768,128]{1,0:T(8,128)(2,1)S(1)} %collective-permute-done.8.got_ref, bf16[32,3,96,96]{3,2,1,0:T(8,128)(2,1)S(1)} %copy-done, s32[3,32]{1,0:T(4,128)S(1)} %bitcast.8, ...), custom_call_target="tpu_custom_call" | custom-call | flops 201326592 | bytes 9765248 | tf_op jit(solution)/shard_map/pallas_call | solution.py:26
  32.8 3.0 %collective-permute-start.10 = (f32[64,1024]{1,0:T(8,128)S(1)}, f32[64,1024]{1,0:T(8,128)S(1)}, u32[]{:S(2)}, u32[]{:S(2)}) collective-permute-start(f32[64,1024]{1,0:T(8,128)S(1)} %get-tuple-element.52), channel_id=1, source_target_pairs={{0,1},{1,0},{2,3},{3,2},{4,5},{5,4},{6,7},{7,6},{8,9},{9,8},{10,11... | collective-permute-start | bytes 786440 | tf_op jit(solution)/shard_map/ppermute | solution.py:342
  35.8 1.2 %collective-permute-done.10.other_ref = f32[64,1024]{1,0:T(8,128)S(1)} collective-permute-done((f32[64,1024]{1,0:T(8,128)S(1)}, f32[64,1024]{1,0:T(8,128)S(1)}, u32[]{:S(2)}, u32[]{:S(2)}) %collective-permute-start.10) | collective-permute-done | bytes 262176 | tf_op jit(solution)/shard_map/ppermute | solution.py:342
  37.0 2.8 %collective-permute-start.11 = (bf16[32,1024]{1,0:T(8,128)(2,1)S(1)}, bf16[32,1024]{1,0:T(8,128)(2,1)S(1)}, u32[]{:S(2)}, u32[]{:S(2)}) collective-permute-start(bf16[32,1024]{1,0:T(8,128)(2,1)S(1)} %get-tuple-element.54), channel_id=1, source_target_pairs={{0,2},{1,3},{2,0},{3,1},{4,6},{5,7},{6,4},{7,5},{8,10},{9,11},{10,... | collective-permute-start | bytes 196616 | tf_op jit(solution)/shard_map/ppermute | solution.py:342
  39.8 2.4 %collective-permute-done.11.other_ref = bf16[32,1024]{1,0:T(8,128)(2,1)S(1)} collective-permute-done((bf16[32,1024]{1,0:T(8,128)(2,1)S(1)}, bf16[32,1024]{1,0:T(8,128)(2,1)S(1)}, u32[]{:S(2)}, u32[]{:S(2)}) %collective-permute-start.11) | collective-permute-done | bytes 65568 | tf_op jit(solution)/shard_map/ppermute | solution.py:342
  42.2 2.5 %collective-permute-start.14 = (bf16[32,1024]{1,0:T(8,128)(2,1)S(1)}, bf16[32,1024]{1,0:T(8,128)(2,1)S(1)}, u32[]{:S(2)}, u32[]{:S(2)}) collective-permute-start(bf16[32,1024]{1,0:T(8,128)(2,1)S(1)} %get-tuple-element.56), channel_id=1, source_target_pairs={{0,8},{1,9},{2,10},{3,11},{4,12},{5,13},{6,14},{7,15},{8,0},{9,1},... | collective-permute-start | bytes 196616 | tf_op jit(solution)/shard_map/ppermute | solution.py:353
  44.7 3.0 %collective-permute-start.13 = (bf16[32,1024]{1,0:T(8,128)(2,1)S(1)}, bf16[32,1024]{1,0:T(8,128)(2,1)S(1)}, u32[]{:S(2)}, u32[]{:S(2)}) collective-permute-start(bf16[32,1024]{1,0:T(8,128)(2,1)S(1)} %get-tuple-element.56), channel_id=1, source_target_pairs={{0,12},{1,13},{2,14},{3,15},{4,0},{5,1},{6,2},{7,3},{8,4},{9,5},{1... | collective-permute-start | bytes 196616 | tf_op jit(solution)/shard_map/ppermute | solution.py:353
  47.7 1.3 %shard_map.96 = (bf16[1024,1024]{1,0:T(8,128)(2,1)S(1)}, bf16[1024,1024]{1,0:T(8,128)(2,1)S(1)}) custom-call(f32[1024,1024]{1,0:T(8,128)S(1)} %copy-done.1), custom_call_target="tpu_custom_call" | custom-call | flops 4194304 | bytes 4194304 | tf_op jit(solution)/shard_map/pallas_call | solution.py:26
  49.6 4.2 %collective-permute-done.12.refs_0_ = bf16[32,1024]{1,0:T(8,128)(2,1)S(1)} collective-permute-done((bf16[32,1024]{1,0:T(8,128)(2,1)S(1)}, bf16[32,1024]{1,0:T(8,128)(2,1)S(1)}, u32[]{:S(2)}, u32[]{:S(2)}) %collective-permute-start.12) | collective-permute-done | bytes 65568 | tf_op jit(solution)/shard_map/ppermute | solution.py:353
  55.5 3.3 %collective-permute-done.15.y_ref = bf16[32,1024]{1,0:T(8,128)(2,1)S(1)} collective-permute-done((bf16[32,1024]{1,0:T(8,128)(2,1)S(1)}, bf16[32,1024]{1,0:T(8,128)(2,1)S(1)}, u32[]{:S(2)}, u32[]{:S(2)}) %collective-permute-start.15) | collective-permute-done | bytes 65568 | tf_op jit(solution)/shard_map/ppermute | solution.py:342
  58.8 1.2 %collective-permute-done.17.both_ref = bf16[32,1024]{1,0:T(8,128)(2,1)S(1)} collective-permute-done((bf16[32,1024]{1,0:T(8,128)(2,1)S(1)}, bf16[32,1024]{1,0:T(8,128)(2,1)S(1)}, u32[]{:S(2)}, u32[]{:S(2)}) %collective-permute-start.17) | collective-permute-done | bytes 65568 | tf_op jit(solution)/shard_map/ppermute | solution.py:342
  60.1 2.7 %shard_map.98 = (bf16[3072,128]{1,0:T(8,128)(2,1)}, f32[24,128]{1,0:T(8,128)}) custom-call(bf16[32,1024]{1,0:T(8,128)(2,1)S(1)} %shard_map.97.own_ref, bf16[32,1024]{1,0:T(8,128)(2,1)S(1)} %collective-permute-done.15.y_ref, bf16[32,1024]{1,0:T(8,128)(2,1)S(1)} %collective-permute-done.16.core_ref, bf16[32,1024]{1,0:T(8,128)(2,1)S(1)} %collective-permute-done.17.both_ref, ...), custom_call_target="tpu_custom_call" | custom-call | flops 805306368 | bytes 7340032 | tf_op jit(solution)/shard_map/pallas_call | solution.py:26
  (42 shorter events, 8.7 us)
Async XLA Ops:
  0.6 1.0 %copy-start.3 = (bf16[1024,128]{1,0:T(8,128)(2,1)S(1)}, bf16[1024,128]{1,0:T(8,128)(2,1)}, u32[]{:S(2)}) copy-start(bf16[1024,128]{1,0:T(8,128)(2,1)} %rec_ref.1) | copy-start | bytes 786436
  4.3 1.7 %collective-permute-start = (bf16[8,144,128]{2,1,0:T(8,128)(2,1)S(1)}, bf16[8,144,128]{2,1,0:T(8,128)(2,1)S(1)}, u32[]{:S(2)}, u32[]{:S(2)}) collective-permute-start(bf16[8,144,128]{2,1,0:T(8,128)(2,1)S(1)} %get-tuple-element.35), channel_id=1, source_target_pairs={{0,1},{1,0},{2,3},{3,2},{4,5},{5,4},{6,7},{7,6},{8,9},{9,8},{10,11... | collective-permute-start | bytes 884744 | tf_op jit(solution)/shard_map/ppermute | solution.py:342
  6.1 20.7 %copy-start = (bf16[32,3,96,96]{3,2,1,0:T(8,128)(2,1)S(1)}, bf16[32,3,96,96]{3,2,1,0:T(8,128)(2,1)}, u32[]{:S(2)}) copy-start(bf16[32,3,96,96]{3,2,1,0:T(8,128)(2,1)} %stiff_ref.5) | copy-start | bytes 5308420
  6.1 20.7 %copy-start.2 = (s32[32,3]{0,1:T(4,128)S(1)}, s32[32,3]{0,1:T(4,128)}, u32[]{:S(2)}) copy-start(s32[32,3]{0,1:T(4,128)} %param.11) | copy-start | bytes 1156
  6.1 23.6 %slice-start = ((s8[6291456]{0:T(1024)(128)(4,1)}), s8[4194304]{0:T(1024)(128)(4,1)S(1)}, s32[]{:S(2)}) async-start(s8[6291456]{0:T(1024)(128)(4,1)} %bitcast.4), calls=%async_computation | async-start | bytes 8388608
  6.1 9.9 %collective-permute-start.1 = (bf16[272,128]{1,0:T(8,128)(2,1)S(1)}, bf16[272,128]{1,0:T(8,128)(2,1)S(1)}, u32[]{:S(2)}, u32[]{:S(2)}) collective-permute-start(bf16[272,128]{1,0:T(8,128)(2,1)S(1)} %get-tuple-element.37), channel_id=1, source_target_pairs={{0,2},{1,3},{2,0},{3,1},{4,6},{5,7},{6,4},{7,5},{8,10},{9,11},{10,... | collective-permute-start | bytes 208904 | tf_op jit(solution)/shard_map/ppermute | solution.py:353
  9.1 9.2 %collective-permute-start.2 = (bf16[272,128]{1,0:T(8,128)(2,1)S(1)}, bf16[272,128]{1,0:T(8,128)(2,1)S(1)}, u32[]{:S(2)}, u32[]{:S(2)}) collective-permute-start(bf16[272,128]{1,0:T(8,128)(2,1)S(1)} %get-tuple-element.38), channel_id=1, source_target_pairs={{0,4},{1,5},{2,6},{3,7},{4,8},{5,9},{6,10},{7,11},{8,12},{9,13},{1... | collective-permute-start | bytes 208904 | tf_op jit(solution)/shard_map/ppermute | solution.py:353
  10.6 7.9 %collective-permute-start.3 = (bf16[272,128]{1,0:T(8,128)(2,1)S(1)}, bf16[272,128]{1,0:T(8,128)(2,1)S(1)}, u32[]{:S(2)}, u32[]{:S(2)}) collective-permute-start(bf16[272,128]{1,0:T(8,128)(2,1)S(1)} %get-tuple-element.39), channel_id=1, source_target_pairs={{0,6},{1,7},{2,4},{3,5},{4,10},{5,11},{6,8},{7,9},{8,14},{9,15},{1... | collective-permute-start | bytes 208904 | tf_op jit(solution)/shard_map/ppermute | solution.py:353
  12.2 8.9 %collective-permute-start.4 = (bf16[272,128]{1,0:T(8,128)(2,1)S(1)}, bf16[272,128]{1,0:T(8,128)(2,1)S(1)}, u32[]{:S(2)}, u32[]{:S(2)}) collective-permute-start(bf16[272,128]{1,0:T(8,128)(2,1)S(1)} %get-tuple-element.40), channel_id=1, source_target_pairs={{0,8},{1,9},{2,10},{3,11},{4,12},{5,13},{6,14},{7,15},{8,0},{9,1},... | collective-permute-start | bytes 208904 | tf_op jit(solution)/shard_map/ppermute | solution.py:353
  13.2 10.5 %collective-permute-start.5 = (bf16[272,128]{1,0:T(8,128)(2,1)S(1)}, bf16[272,128]{1,0:T(8,128)(2,1)S(1)}, u32[]{:S(2)}, u32[]{:S(2)}) collective-permute-start(bf16[272,128]{1,0:T(8,128)(2,1)S(1)} %get-tuple-element.41), channel_id=1, source_target_pairs={{0,10},{1,11},{2,8},{3,9},{4,14},{5,15},{6,12},{7,13},{8,2},{9,3},... | collective-permute-start | bytes 208904 | tf_op jit(solution)/shard_map/ppermute | solution.py:353
  16.0 7.7 %collective-permute-start.6 = (bf16[272,128]{1,0:T(8,128)(2,1)S(1)}, bf16[272,128]{1,0:T(8,128)(2,1)S(1)}, u32[]{:S(2)}, u32[]{:S(2)}) collective-permute-start(bf16[272,128]{1,0:T(8,128)(2,1)S(1)} %get-tuple-element.42), channel_id=1, source_target_pairs={{0,12},{1,13},{2,14},{3,15},{4,0},{5,1},{6,2},{7,3},{8,4},{9,5},{1... | collective-permute-start | bytes 208904 | tf_op jit(solution)/shard_map/ppermute | solution.py:353
  18.3 5.7 %collective-permute-start.7 = (bf16[272,128]{1,0:T(8,128)(2,1)S(1)}, bf16[272,128]{1,0:T(8,128)(2,1)S(1)}, u32[]{:S(2)}, u32[]{:S(2)}) collective-permute-start(bf16[272,128]{1,0:T(8,128)(2,1)S(1)} %get-tuple-element.43), channel_id=1, source_target_pairs={{0,14},{1,15},{2,12},{3,13},{4,2},{5,3},{6,0},{7,1},{8,6},{9,7},{1... | collective-permute-start | bytes 208904 | tf_op jit(solution)/shard_map/ppermute | solution.py:353
  24.0 5.6 %slice-start.1 = ((s8[6291456]{0:T(1024)(128)(4,1)}), s8[2097152]{0:T(1024)(128)(4,1)S(1)}, s32[]{:S(2)}) async-start(s8[6291456]{0:T(1024)(128)(4,1)} %bitcast.4), calls=%async_computation.1 | async-start | bytes 4194304
  26.0 3.6 %collective-permute-start.9 = (bf16[768,128]{1,0:T(8,128)(2,1)S(1)}, bf16[768,128]{1,0:T(8,128)(2,1)S(1)}, u32[]{:S(2)}, u32[]{:S(2)}) collective-permute-start(bf16[768,128]{1,0:T(8,128)(2,1)S(1)} %shard_map.90.near_ref), channel_id=1, source_target_pairs={{0,1},{1,0},{2,3},{3,2},{4,5},{5,4},{6,7},{7,6},{8,9},{9,8},{10,11... | collective-permute-start | bytes 589832 | tf_op jit(solution)/shard_map/ppermute | solution.py:342
  26.1 5.3 %collective-permute-start.8 = (bf16[768,128]{1,0:T(8,128)(2,1)S(1)}, bf16[768,128]{1,0:T(8,128)(2,1)S(1)}, u32[]{:S(2)}, u32[]{:S(2)}) collective-permute-start(bf16[768,128]{1,0:T(8,128)(2,1)S(1)} %get-tuple-element.46.far_ref), channel_id=1, source_target_pairs={{1,2},{3,4},{5,6},{7,8},{9,10},{11,12},{13,14},{2,1},{4,3},{6,5},{... | collective-permute-start | bytes 589832 | tf_op jit(solution)/shard_map/ppermute | solution.py:346
  31.4 16.3 %copy-start.1 = (f32[1024,1024]{1,0:T(8,128)S(1)}, f32[1024,1024]{1,0:T(8,128)}, u32[]{:S(2)}) copy-start(f32[1024,1024]{1,0:T(8,128)} %a_ref.1) | copy-start | bytes 12582916
  32.8 4.2 %collective-permute-start.10 = (f32[64,1024]{1,0:T(8,128)S(1)}, f32[64,1024]{1,0:T(8,128)S(1)}, u32[]{:S(2)}, u32[]{:S(2)}) collective-permute-start(f32[64,1024]{1,0:T(8,128)S(1)} %get-tuple-element.52), channel_id=1, source_target_pairs={{0,1},{1,0},{2,3},{3,2},{4,5},{5,4},{6,7},{7,6},{8,9},{9,8},{10,11... | collective-permute-start | bytes 786440 | tf_op jit(solution)/shard_map/ppermute | solution.py:342
  37.0 5.2 %collective-permute-start.11 = (bf16[32,1024]{1,0:T(8,128)(2,1)S(1)}, bf16[32,1024]{1,0:T(8,128)(2,1)S(1)}, u32[]{:S(2)}, u32[]{:S(2)}) collective-permute-start(bf16[32,1024]{1,0:T(8,128)(2,1)S(1)} %get-tuple-element.54), channel_id=1, source_target_pairs={{0,2},{1,3},{2,0},{3,1},{4,6},{5,7},{6,4},{7,5},{8,10},{9,11},{10,... | collective-permute-start | bytes 196616 | tf_op jit(solution)/shard_map/ppermute | solution.py:342
  42.2 6.7 %collective-permute-start.14 = (bf16[32,1024]{1,0:T(8,128)(2,1)S(1)}, bf16[32,1024]{1,0:T(8,128)(2,1)S(1)}, u32[]{:S(2)}, u32[]{:S(2)}) collective-permute-start(bf16[32,1024]{1,0:T(8,128)(2,1)S(1)} %get-tuple-element.56), channel_id=1, source_target_pairs={{0,8},{1,9},{2,10},{3,11},{4,12},{5,13},{6,14},{7,15},{8,0},{9,1},... | collective-permute-start | bytes 196616 | tf_op jit(solution)/shard_map/ppermute | solution.py:353
  44.7 4.9 %collective-permute-start.13 = (bf16[32,1024]{1,0:T(8,128)(2,1)S(1)}, bf16[32,1024]{1,0:T(8,128)(2,1)S(1)}, u32[]{:S(2)}, u32[]{:S(2)}) collective-permute-start(bf16[32,1024]{1,0:T(8,128)(2,1)S(1)} %get-tuple-element.56), channel_id=1, source_target_pairs={{0,12},{1,13},{2,14},{3,15},{4,0},{5,1},{6,2},{7,3},{8,4},{9,5},{1... | collective-permute-start | bytes 196616 | tf_op jit(solution)/shard_map/ppermute | solution.py:353
  47.7 6.1 %collective-permute-start.12 = (bf16[32,1024]{1,0:T(8,128)(2,1)S(1)}, bf16[32,1024]{1,0:T(8,128)(2,1)S(1)}, u32[]{:S(2)}, u32[]{:S(2)}) collective-permute-start(bf16[32,1024]{1,0:T(8,128)(2,1)S(1)} %get-tuple-element.56), channel_id=1, source_target_pairs={{0,4},{1,5},{2,6},{3,7},{4,8},{5,9},{6,10},{7,11},{8,12},{9,13},{1... | collective-permute-start | bytes 196616 | tf_op jit(solution)/shard_map/ppermute | solution.py:353
  54.6 4.3 %collective-permute-start.15 = (bf16[32,1024]{1,0:T(8,128)(2,1)S(1)}, bf16[32,1024]{1,0:T(8,128)(2,1)S(1)}, u32[]{:S(2)}, u32[]{:S(2)}) collective-permute-start(bf16[32,1024]{1,0:T(8,128)(2,1)S(1)} %shard_map.97.own_ref), channel_id=1, source_target_pairs={{0,2},{1,3},{2,0},{3,1},{4,6},{5,7},{6,4},{7,5},{8,10},{9,11},{10,... | collective-permute-start | bytes 196616 | tf_op jit(solution)/shard_map/ppermute | solution.py:342
  55.5 3.4 %collective-permute-start.16 = (bf16[32,1024]{1,0:T(8,128)(2,1)S(1)}, bf16[32,1024]{1,0:T(8,128)(2,1)S(1)}, u32[]{:S(2)}, u32[]{:S(2)}) collective-permute-start(bf16[32,1024]{1,0:T(8,128)(2,1)S(1)} %shard_map.97.own_ref), channel_id=1, source_target_pairs={{0,1},{1,0},{2,3},{3,2},{4,5},{5,4},{6,7},{7,6},{8,9},{9,8},{10,11... | collective-permute-start | bytes 196616 | tf_op jit(solution)/shard_map/ppermute | solution.py:342
  58.8 1.3 %collective-permute-start.17 = (bf16[32,1024]{1,0:T(8,128)(2,1)S(1)}, bf16[32,1024]{1,0:T(8,128)(2,1)S(1)}, u32[]{:S(2)}, u32[]{:S(2)}) collective-permute-start(bf16[32,1024]{1,0:T(8,128)(2,1)S(1)} %collective-permute-done.15.y_ref), channel_id=1, source_target_pairs={{0,1},{1,0},{2,3},{3,2},{4,5},{5,4},{6,7},{7,6},{8,9},{9,8},{10,11... | collective-permute-start | bytes 196616 | tf_op jit(solution)/shard_map/ppermute | solution.py:342
  (2 other events, 1.4 us)

commit v3 on v2

--- a/solution.py
+++ b/solution.py
@@ -117,17 +117,16 @@
         ref[2 * cap :] = own_ref[j, cap:] + cross_ref[j, cap:]
 
 
+CHUNK = 256
+
+
 def loads_at(slots, records, base, rows):
     key = slots - base.astype(F32)
     key = jnp.where((key >= 0.0) & (key < float(rows)), key, -1.0).astype(BF)
-    return jnp.dot(hot(rows, key), records, preferred_element_type=F32).astype(BF)
-
-
-CHUNK = 256
-
-
-def far_kernel(cap, elem_rows, count, *refs):
-    got_refs, (far_ref, slots_ref, records_ref) = refs[:count], refs[count:]
+    return jnp.dot(hot(rows, key), records, preferred_element_type=F32)
+
+
+def land(cap, got_refs, records_ref):
     share = LANES // cap
     order = [(ref, x) for ref in got_refs for x in range(2)]
     for k, ref in enumerate(got_refs):
@@ -140,24 +139,42 @@
             part = tail[2 * x : 2 * x + 1] * 64.0 + tail[2 * x + 1 : 2 * x + 2]
             row = part if row is None else row + part
         rows.append(row)
-    slots = jnp.concatenate(rows, axis=1)
+    return jnp.concatenate(rows, axis=1)
+
+
+def early_kernel(cap, count, *refs):
+    got_refs, (sum_ref, records_ref) = refs[:count], refs[count:]
+    slots = land(cap, got_refs, records_ref)
+    records = records_ref[...]
+    for k in range(sum_ref.shape[0] // CHUNK):
+        at = k * CHUNK
+        sum_ref[at : at + CHUNK, :] = loads_at(slots, records, jnp.int32(at), CHUNK)
+
+
+def far_kernel(cap, count, *refs):
+    got_refs, (sum_ref, far_ref, slots_ref, records_ref) = refs[:count], refs[count:]
+    slots = land(cap, got_refs, records_ref)
     slots_ref[...] = slots
     halo = far_ref.shape[0]
-    first = jnp.where(odd_core() == 1, elem_rows - halo, 0)
+    first = jnp.where(odd_core() == 1, sum_ref.shape[0] - halo, 0)
     records = records_ref[...]
     for k in range(halo // CHUNK):
-        far_ref[k * CHUNK : (k + 1) * CHUNK, :] = loads_at(
-            slots, records, first + k * CHUNK, CHUNK
-        )
-
-
-def near_kernel(elem_rows, slots_ref, records_ref, near_ref):
+        base = first + k * CHUNK
+        start = sum_ref[pl.ds(pl.multiple_of(base, CHUNK), CHUNK), :]
+        far_ref[k * CHUNK : (k + 1) * CHUNK, :] = (
+            start + loads_at(slots, records, base, CHUNK)
+        ).astype(BF)
+
+
+def near_kernel(sum_ref, slots_ref, records_ref, near_ref):
     halo = near_ref.shape[0]
-    first = jnp.where(odd_core() == 1, 0, elem_rows - halo)
+    first = jnp.where(odd_core() == 1, 0, sum_ref.shape[0] - halo)
     for k in range(halo // CHUNK):
-        near_ref[k * CHUNK : (k + 1) * CHUNK, :] = loads_at(
-            slots_ref[...], records_ref[...], first + k * CHUNK, CHUNK
-        )
+        base = first + k * CHUNK
+        start = sum_ref[pl.ds(pl.multiple_of(base, CHUNK), CHUNK), :]
+        near_ref[k * CHUNK : (k + 1) * CHUNK, :] = (
+            start + loads_at(slots_ref[...], records_ref[...], base, CHUNK)
+        ).astype(BF)
 
 
 def stiffen(stiff_ref, cols_ref, loads_ref, block, first_col):
@@ -173,7 +190,7 @@
 
 
 def middle_kernel(
-    slots_ref, records_ref, near_ref, far_ref, stiff_ref, cols_ref, loads_ref, st_ref
+    sum_ref, slots_ref, records_ref, near_ref, far_ref, stiff_ref, cols_ref, loads_ref, st_ref
 ):
     elem_rows = loads_ref.shape[0]
     halo = near_ref.shape[0]
@@ -186,9 +203,10 @@
     loads_ref[pl.ds(far_at, halo), :] = far_ref[...]
     for k in range((last - halo) // CHUNK):
         base = halo + k * CHUNK
-        loads_ref[base : base + CHUNK, :] = loads_at(
-            slots_ref[...], records_ref[...], jnp.int32(base), CHUNK
-        )
+        loads_ref[base : base + CHUNK, :] = (
+            sum_ref[base : base + CHUNK, :]
+            + loads_at(slots_ref[...], records_ref[...], jnp.int32(base), CHUNK)
+        ).astype(BF)
     first_col = lax.axis_index("elem") * blocks
     for b in range(REACH, blocks - REACH):
         st_ref[(b - REACH) * size : (b - REACH + 1) * size, :] = stiffen(
@@ -281,8 +299,20 @@
     adj_ref[...] = adj.astype(BF)
 
 
+def turn_kernel(modes_ref, mid_ref, edge_ref, modes_t_ref, st_t_ref):
+    elem_rows = modes_ref.shape[0]
+    halo = edge_ref.shape[0] // 2
+    last = elem_rows - halo
+    for k in range(elem_rows // CHUNK):
+        at = k * CHUNK
+        modes_t_ref[:, at : at + CHUNK] = modes_ref[at : at + CHUNK, :].T
+    st_t_ref[:, 0:halo] = edge_ref[0:halo, :].T
+    st_t_ref[:, halo:last] = mid_ref[...].T
+    st_t_ref[:, last:] = edge_ref[halo:, :].T
+
+
 def back_kernel(
-    own_ref, y_ref, core_ref, both_ref, modes_ref, mid_ref, edge_ref, adj_hbm, sens_hbm,
+    own_ref, y_ref, core_ref, both_ref, modes_ref, st_ref, adj_hbm, sens_hbm,
     adj_ref, sens_ref, field_ref, sems,
 ):
     me = lax.axis_index("elem")
@@ -298,29 +328,19 @@
         at = pl.multiple_of((2 * c + y) * quarter, 16)
         field_ref[pl.ds(at, quarter), :] = ref[...]
     field = field_ref[...]
-    elem_rows = modes_ref.shape[0]
-    halo = edge_ref.shape[0] // 2
-    last = elem_rows - halo
+    elem_rows = modes_ref.shape[1]
     leaving = []
     for k in range(elem_rows // CHUNK):
         at = k * CHUNK
-        part = lax.dot_general(
-            modes_ref[at : at + CHUNK, :], field, NT, preferred_element_type=F32
-        )
-        adj_ref[at : at + CHUNK, :] = part.astype(BF)
+        part = jnp.dot(field, modes_ref[:, at : at + CHUNK], preferred_element_type=F32)
+        row = jnp.sum(part * st_ref[:, at : at + CHUNK].astype(F32), axis=0, keepdims=True)
+        for i in range(CHUNK // LANES):
+            cols = slice(i * LANES, (i + 1) * LANES)
+            adj_ref[at + i * LANES : at + (i + 1) * LANES, :] = part[:, cols].T.astype(BF)
+            sens_ref[at // LANES + i : at // LANES + i + 1, :] = row[:, cols]
         rows = pl.ds(at, CHUNK)
         leaving.append(pltpu.make_async_copy(adj_ref.at[rows], adj_hbm.at[rows], sems.at[k]))
         leaving[-1].start()
-        if at < halo:
-            st = edge_ref[at : at + CHUNK, :]
-        elif at < last:
-            st = mid_ref[at - halo : at - halo + CHUNK, :]
-        else:
-            st = edge_ref[at - last + halo : at - last + halo + CHUNK, :]
-        product = part * st.astype(F32)
-        for i in range(CHUNK // LANES):
-            row = jnp.sum(product[i * LANES : (i + 1) * LANES, :].T, axis=0, keepdims=True)
-            sens_ref[at // LANES + i : at // LANES + i + 1, :] = row
     leaving.append(pltpu.make_async_copy(sens_ref, sens_hbm, sems.at[elem_rows // CHUNK]))
     leaving[-1].start()
     for copy in leaving:
@@ -381,28 +401,36 @@
     offsets = range(1, chips)
     got = {j: turn(packed[j], j // 2, j % 2) for j in offsets}
     got[0] = packed[0]
-    total_rows = owners * cap
+    half = chips // 2
+    late_rows = half * 2 * cap
+    early = call(
+        functools.partial(early_kernel, cap, half),
+        shape((elem_rows, width), F32),
+        *[got[j] for j in range(half)],
+        scratch=(pltpu.VMEM((late_rows, width), BF),),
+        flops=2 * late_rows * elem_rows * width,
+    )
     far, slot_row, landed = call(
-        functools.partial(far_kernel, cap, elem_rows, chips),
-        (shape((halo, width), BF), shape((1, total_rows), F32), shape((total_rows, width), BF)),
-        *[got[j] for j in range(chips)],
-        flops=8 * total_rows * halo * width,
+        functools.partial(far_kernel, cap, chips - half),
+        (shape((halo, width), BF), shape((1, late_rows), F32), shape((late_rows, width), BF)),
+        *[got[j] for j in range(half, chips)], early,
+        flops=16 * late_rows * halo * width,
     )
     got_far = swap_far(far)
     near = call(
-        functools.partial(near_kernel, elem_rows),
+        near_kernel,
         shape((halo, width), BF),
-        slot_row, landed,
-        flops=2 * total_rows * halo * width,
+        early, slot_row, landed,
+        flops=2 * late_rows * halo * width,
     )
     got_near = swap(near, 1)
     cols = block_cols.T
     loads, st_mid = call(
         middle_kernel,
         (shape((elem_rows, width), BF), shape((elem_rows - 2 * halo, width), BF)),
-        slot_row, landed, near, far, stiff_blocks, cols,
-        smem=(5,),
-        flops=4 * total_rows * halo * width,
+        early, slot_row, landed, near, far, stiff_blocks, cols,
+        smem=(6,),
+        flops=4 * late_rows * halo * width,
     )
     extended = pltpu.VMEM((elem_rows + 2 * halo, width), BF)
     st_near, modal_near = call(
@@ -453,11 +481,17 @@
     )
     across = swap(mine, 2)
     beside = swap(mine, 1)
+    modes_t, st_t = call(
+        turn_kernel,
+        (shape((mode_count, elem_rows), BF), shape((width, elem_rows), BF)),
+        modes, st_mid, st_edge,
+    )
+    across, modes_t, st_t = lax.optimization_barrier((across, modes_t, st_t))
     both = swap(across, 1)
     adjoint, sensitivity = call(
         back_kernel,
         (shape((elem_rows, width), BF), shape((elem_rows // LANES, LANES), F32)),
-        mine, across, beside, both, modes, st_mid, st_edge,
+        mine, across, beside, both, modes_t, st_t,
         out=pltpu.HBM,
         scratch=(
             pltpu.VMEM((elem_rows, width), BF),

time: 63.1 us -> 61.6 us (0.976)
  waiting for transfers between devices: 18.9 us -> 15 us
  Pallas kernels: 14.9 us -> 16.3 us
  starting transfers between devices: 25.9 us -> 26.8 us
    ppermute x7, waiting for transfers between devices: 8.65 us -> 6.56 us  [swap(): return lax.ppermute(array, 'elem', [(i, i ^ mask) for i in range(owners)])]
    ppermute x10, waiting for transfers between devices: 10.2 us -> 8.4 us  [turn(): return lax.ppermute(array, 'elem', pairs)]
    pallas_call x13 -> x15, Pallas kernels: 14.9 us -> 16.3 us  [call(): pl.pallas_call(kernel, out_shape=out_shape, in_specs=[pl.BlockSpec(memory...]
    ppermute x7, starting transfers between devices: 7.35 us -> 8.24 us  [swap(): return lax.ppermute(array, 'elem', [(i, i ^ mask) for i in range(owners)])]
  transfers between devices with their start and end apart: 18 -> 18, of which waited for: 10 -> 10; matrix products, arithmetic and copies ran while one was open for 0% -> 0% of each run, Pallas kernels for 10% -> 16%
where the time goes in v3:
time: 61.6 us; the launch traced here: 61.3 us
  starting transfers between devices  26.8 us (44%)
  Pallas kernels  16.3 us (26%)
  waiting for transfers between devices  15 us (24%)
  local copies, waits for them, and re-layouts  2.34 us (4%)
  between operations  1 us (2%)
    ppermute x10, starting transfers between devices, turn(): return lax.ppermute(array, 'elem', pairs)  17.9 us
    pallas_call x15, Pallas kernels, call(): pl.pallas_call(kernel, out_shape=out_shape, in_specs=[pl.BlockSpec(memory...  16.3 us
    ppermute x10, waiting for transfers between devices, turn(): return lax.ppermute(array, 'elem', pairs)  8.4 us
    ppermute x7, starting transfers between devices, swap(): return lax.ppermute(array, 'elem', [(i, i ^ mask) for i in range(owners)])  8.24 us
    ppermute x7, waiting for transfers between devices, swap(): return lax.ppermute(array, 'elem', [(i, i ^ mask) for i in range(owners)])  6.56 us
    unnamed x16, local copies, waits for them, and re-layouts  2.34 us
  transfers between devices with their start and end apart: 18, of which 10 were waited for; matrix products, arithmetic and copies ran while one was open for 0% of the time, Pallas kernels for 16%

profile of v3, /device:TPU:0, one launch (start us, length us, event | category | flops | bytes accessed | tf_op | source)
XLA Modules:
  0.0 61.3 jit_solution(14555028887848520441)
XLA Ops:
  3.0 1.4 %shard_map.86 = (bf16[8,144,128]{2,1,0:T(8,128)(2,1)S(1)}, f32[1,1024]{1,0:T(1,128)S(1)}, f32[1,32,128]{2,1,0:T(8,128)S(1)}, bf16[1024,128]{1,0:T(8,128)(2,1)S(1)}) custom-call(s32[1,1024]{1,0:T(1,128)S(1)} %bitcast.10, s32[8,128]{1,0:T(8,128)S(1)} %bitcast.9, bf16[1024,128]{1,0:T(8,128)(2,1)S(1)} %copy-done.3), custom_call_target="tpu_custom_call" | custom-call | flops 268435456 | bytes 270336 | tf_op jit(solution)/shard_map/pallas_call | solution.py:26
  6.1 3.0 %collective-permute-start.1 = (bf16[272,128]{1,0:T(8,128)(2,1)S(1)}, bf16[272,128]{1,0:T(8,128)(2,1)S(1)}, u32[]{:S(2)}, u32[]{:S(2)}) collective-permute-start(bf16[272,128]{1,0:T(8,128)(2,1)S(1)} %get-tuple-element.42), channel_id=1, source_target_pairs={{0,2},{1,3},{2,0},{3,1},{4,6},{5,7},{6,4},{7,5},{8,10},{9,11},{10,... | collective-permute-start | bytes 208904 | tf_op jit(solution)/shard_map/ppermute | solution.py:373
  9.1 1.6 %collective-permute-start.2 = (bf16[272,128]{1,0:T(8,128)(2,1)S(1)}, bf16[272,128]{1,0:T(8,128)(2,1)S(1)}, u32[]{:S(2)}, u32[]{:S(2)}) collective-permute-start(bf16[272,128]{1,0:T(8,128)(2,1)S(1)} %get-tuple-element.43), channel_id=1, source_target_pairs={{0,4},{1,5},{2,6},{3,7},{4,8},{5,9},{6,10},{7,11},{8,12},{9,13},{1... | collective-permute-start | bytes 208904 | tf_op jit(solution)/shard_map/ppermute | solution.py:373
  10.6 1.5 %collective-permute-start.3 = (bf16[272,128]{1,0:T(8,128)(2,1)S(1)}, bf16[272,128]{1,0:T(8,128)(2,1)S(1)}, u32[]{:S(2)}, u32[]{:S(2)}) collective-permute-start(bf16[272,128]{1,0:T(8,128)(2,1)S(1)} %get-tuple-element.44), channel_id=1, source_target_pairs={{0,6},{1,7},{2,4},{3,5},{4,10},{5,11},{6,8},{7,9},{8,14},{9,15},{1... | collective-permute-start | bytes 208904 | tf_op jit(solution)/shard_map/ppermute | solution.py:373
  12.1 1.1 %collective-permute-start.4 = (bf16[272,128]{1,0:T(8,128)(2,1)S(1)}, bf16[272,128]{1,0:T(8,128)(2,1)S(1)}, u32[]{:S(2)}, u32[]{:S(2)}) collective-permute-start(bf16[272,128]{1,0:T(8,128)(2,1)S(1)} %get-tuple-element.45), channel_id=1, source_target_pairs={{0,8},{1,9},{2,10},{3,11},{4,12},{5,13},{6,14},{7,15},{8,0},{9,1},... | collective-permute-start | bytes 208904 | tf_op jit(solution)/shard_map/ppermute | solution.py:373
  13.2 2.8 %collective-permute-start.5 = (bf16[272,128]{1,0:T(8,128)(2,1)S(1)}, bf16[272,128]{1,0:T(8,128)(2,1)S(1)}, u32[]{:S(2)}, u32[]{:S(2)}) collective-permute-start(bf16[272,128]{1,0:T(8,128)(2,1)S(1)} %get-tuple-element.46), channel_id=1, source_target_pairs={{0,10},{1,11},{2,8},{3,9},{4,14},{5,15},{6,12},{7,13},{8,2},{9,3},... | collective-permute-start | bytes 208904 | tf_op jit(solution)/shard_map/ppermute | solution.py:373
  16.0 2.2 %collective-permute-start.6 = (bf16[272,128]{1,0:T(8,128)(2,1)S(1)}, bf16[272,128]{1,0:T(8,128)(2,1)S(1)}, u32[]{:S(2)}, u32[]{:S(2)}) collective-permute-start(bf16[272,128]{1,0:T(8,128)(2,1)S(1)} %get-tuple-element.47), channel_id=1, source_target_pairs={{0,12},{1,13},{2,14},{3,15},{4,0},{5,1},{6,2},{7,3},{8,4},{9,5},{1... | collective-permute-start | bytes 208904 | tf_op jit(solution)/shard_map/ppermute | solution.py:373
  18.5 1.8 %shard_map.89.refs_4_.sum_ref = f32[3072,128]{1,0:T(8,128)S(1)} custom-call(bf16[272,128]{1,0:T(8,128)(2,1)S(1)} %get-tuple-element.41.refs_0_, bf16[272,128]{1,0:T(8,128)(2,1)S(1)} %collective-permute-done.1.refs_1_, bf16[272,128]{1,0:T(8,128)(2,1)S(1)} %collective-permute-done.2.refs_2_, bf16[272,128]{1,0:T(8,128)(2,1)S(1)} %collective-permute-done.3.refs_3_), custom_call_target="tpu_custom_call" | custom-call | flops 805306368 | bytes 278528 | tf_op jit(solution)/shard_map/pallas_call | solution.py:26
  21.1 2.7 %collective-permute-done.5.refs_1_ = bf16[272,128]{1,0:T(8,128)(2,1)S(1)} collective-permute-done((bf16[272,128]{1,0:T(8,128)(2,1)S(1)}, bf16[272,128]{1,0:T(8,128)(2,1)S(1)}, u32[]{:S(2)}, u32[]{:S(2)}) %collective-permute-start.5) | collective-permute-done | bytes 69664 | tf_op jit(solution)/shard_map/ppermute | solution.py:373
  26.0 2.0 %shard_map.92 = (bf16[3072,128]{1,0:T(8,128)(2,1)S(1)}, bf16[1536,128]{1,0:T(8,128)(2,1)S(1)}) custom-call(f32[3072,128]{1,0:T(8,128)S(1)} %shard_map.89.refs_4_.sum_ref, f32[1,1024]{1,0:T(1,128)S(1)} %get-tuple-element.49.slots_ref, bf16[1024,128]{1,0:T(8,128)(2,1)S(1)} %get-tuple-element.50.records_ref, bf16[768,128]{1,0:T(8,128)(2,1)S(1)} %shard_map.91.near_ref, ...), custom_call_target="tpu_custom_call" | custom-call | flops 402653184 | bytes 4002176 | tf_op jit(solution)/shard_map/pallas_call | solution.py:26
  28.0 1.7 %shard_map.93 = (bf16[768,128]{1,0:T(8,128)(2,1)S(1)}, f32[128,1024]{1,0:T(8,128)S(1)}) custom-call(bf16[3072,128]{1,0:T(8,128)(2,1)S(1)} %get-tuple-element.52.loads_ref, bf16[768,128]{1,0:T(8,128)(2,1)S(1)} %collective-permute-done.9.got_ref, bf16[32,3,96,96]{3,2,1,0:T(8,128)(2,1)S(1)} %copy-done, s32[3,32]{1,0:T(4,128)S(1)} %bitcast.7, ...), custom_call_target="tpu_custom_call" | custom-call | flops 603979776 | bytes 9437568 | tf_op jit(solution)/shard_map/pallas_call | solution.py:26
  29.8 1.3 %shard_map.94 = (bf16[1536,128]{1,0:T(8,128)(2,1)S(1)}, f32[64,1024]{1,0:T(8,128)S(1)}, f32[64,1024]{1,0:T(8,128)S(1)}) custom-call(bf16[3072,128]{1,0:T(8,128)(2,1)S(1)} %get-tuple-element.52.loads_ref, bf16[768,128]{1,0:T(8,128)(2,1)S(1)} %collective-permute-done.8.got_ref, bf16[32,3,96,96]{3,2,1,0:T(8,128)(2,1)S(1)} %copy-done, s32[3,32]{1,0:T(4,128)S(1)} %bitcast.8, ...), custom_call_target="tpu_custom_call" | custom-call | flops 201326592 | bytes 9765248 | tf_op jit(solution)/shard_map/pallas_call | solution.py:26
  31.1 3.8 %collective-permute-start.10 = (f32[64,1024]{1,0:T(8,128)S(1)}, f32[64,1024]{1,0:T(8,128)S(1)}, u32[]{:S(2)}, u32[]{:S(2)}) collective-permute-start(f32[64,1024]{1,0:T(8,128)S(1)} %get-tuple-element.57), channel_id=1, source_target_pairs={{0,1},{1,0},{2,3},{3,2},{4,5},{5,4},{6,7},{7,6},{8,9},{9,8},{10,11... | collective-permute-start | bytes 786440 | tf_op jit(solution)/shard_map/ppermute | solution.py:362
  35.0 1.2 %collective-permute-done.10.other_ref = f32[64,1024]{1,0:T(8,128)S(1)} collective-permute-done((f32[64,1024]{1,0:T(8,128)S(1)}, f32[64,1024]{1,0:T(8,128)S(1)}, u32[]{:S(2)}, u32[]{:S(2)}) %collective-permute-start.10) | collective-permute-done | bytes 262176 | tf_op jit(solution)/shard_map/ppermute | solution.py:362
  36.2 2.8 %collective-permute-start.11 = (bf16[32,1024]{1,0:T(8,128)(2,1)S(1)}, bf16[32,1024]{1,0:T(8,128)(2,1)S(1)}, u32[]{:S(2)}, u32[]{:S(2)}) collective-permute-start(bf16[32,1024]{1,0:T(8,128)(2,1)S(1)} %get-tuple-element.59), channel_id=1, source_target_pairs={{0,2},{1,3},{2,0},{3,1},{4,6},{5,7},{6,4},{7,5},{8,10},{9,11},{10,... | collective-permute-start | bytes 196616 | tf_op jit(solution)/shard_map/ppermute | solution.py:362
  39.0 2.4 %collective-permute-done.11.other_ref = bf16[32,1024]{1,0:T(8,128)(2,1)S(1)} collective-permute-done((bf16[32,1024]{1,0:T(8,128)(2,1)S(1)}, bf16[32,1024]{1,0:T(8,128)(2,1)S(1)}, u32[]{:S(2)}, u32[]{:S(2)}) %collective-permute-start.11) | collective-permute-done | bytes 65568 | tf_op jit(solution)/shard_map/ppermute | solution.py:362
  41.4 2.7 %collective-permute-start.14 = (bf16[32,1024]{1,0:T(8,128)(2,1)S(1)}, bf16[32,1024]{1,0:T(8,128)(2,1)S(1)}, u32[]{:S(2)}, u32[]{:S(2)}) collective-permute-start(bf16[32,1024]{1,0:T(8,128)(2,1)S(1)} %get-tuple-element.61), channel_id=1, source_target_pairs={{0,8},{1,9},{2,10},{3,11},{4,12},{5,13},{6,14},{7,15},{8,0},{9,1},... | collective-permute-start | bytes 196616 | tf_op jit(solution)/shard_map/ppermute | solution.py:373
  44.1 2.7 %collective-permute-start.13 = (bf16[32,1024]{1,0:T(8,128)(2,1)S(1)}, bf16[32,1024]{1,0:T(8,128)(2,1)S(1)}, u32[]{:S(2)}, u32[]{:S(2)}) collective-permute-start(bf16[32,1024]{1,0:T(8,128)(2,1)S(1)} %get-tuple-element.61), channel_id=1, source_target_pairs={{0,12},{1,13},{2,14},{3,15},{4,0},{5,1},{6,2},{7,3},{8,4},{9,5},{1... | collective-permute-start | bytes 196616 | tf_op jit(solution)/shard_map/ppermute | solution.py:373
  46.9 1.3 %shard_map.97 = (bf16[1024,1024]{1,0:T(8,128)(2,1)S(1)}, bf16[1024,1024]{1,0:T(8,128)(2,1)S(1)}) custom-call(f32[1024,1024]{1,0:T(8,128)S(1)} %copy-done.1), custom_call_target="tpu_custom_call" | custom-call | flops 4194304 | bytes 4194304 | tf_op jit(solution)/shard_map/pallas_call | solution.py:26
  48.8 4.2 %collective-permute-done.12.refs_0_ = bf16[32,1024]{1,0:T(8,128)(2,1)S(1)} collective-permute-done((bf16[32,1024]{1,0:T(8,128)(2,1)S(1)}, bf16[32,1024]{1,0:T(8,128)(2,1)S(1)}, u32[]{:S(2)}, u32[]{:S(2)}) %collective-permute-start.12) | collective-permute-done | bytes 65568 | tf_op jit(solution)/shard_map/ppermute | solution.py:373
  54.7 2.0 %shard_map.99 = (bf16[1024,3072]{1,0:T(8,128)(2,1)S(1)}, bf16[128,3072]{1,0:T(8,128)(2,1)S(1)}) custom-call(bf16[3072,1024]{1,0:T(8,128)(2,1)S(1)} %bitcast.5, bf16[1536,128]{1,0:T(8,128)(2,1)S(1)} %get-tuple-element.53.mid_ref, bf16[1536,128]{1,0:T(8,128)(2,1)S(1)} %get-tuple-element.64.edge_ref), custom_call_target="tpu_custom_call" | custom-call | bytes 7077888 | tf_op jit(solution)/shard_map/pallas_call | solution.py:26
  56.8 1.3 %collective-permute-done.15.y_ref = bf16[32,1024]{1,0:T(8,128)(2,1)S(1)} collective-permute-done((bf16[32,1024]{1,0:T(8,128)(2,1)S(1)}, bf16[32,1024]{1,0:T(8,128)(2,1)S(1)}, u32[]{:S(2)}, u32[]{:S(2)}) %collective-permute-start.15) | collective-permute-done | bytes 65568 | tf_op jit(solution)/shard_map/ppermute | solution.py:362
  58.0 1.2 %collective-permute-done.17.both_ref = bf16[32,1024]{1,0:T(8,128)(2,1)S(1)} collective-permute-done((bf16[32,1024]{1,0:T(8,128)(2,1)S(1)}, bf16[32,1024]{1,0:T(8,128)(2,1)S(1)}, u32[]{:S(2)}, u32[]{:S(2)}) %collective-permute-start.17) | collective-permute-done | bytes 65568 | tf_op jit(solution)/shard_map/ppermute | solution.py:362
  59.3 1.9 %shard_map.100 = (bf16[3072,128]{1,0:T(8,128)(2,1)}, f32[24,128]{1,0:T(8,128)}) custom-call(bf16[32,1024]{1,0:T(8,128)(2,1)S(1)} %shard_map.98.own_ref, bf16[32,1024]{1,0:T(8,128)(2,1)S(1)} %collective-permute-done.15.y_ref, bf16[32,1024]{1,0:T(8,128)(2,1)S(1)} %collective-permute-done.16.core_ref, bf16[32,1024]{1,0:T(8,128)(2,1)S(1)} %collective-permute-done.17.both_ref, ...), custom_call_target="tpu_custom_call" | custom-call | flops 805306368 | bytes 7340032 | tf_op jit(solution)/shard_map/pallas_call | solution.py:26
  (44 shorter events, 9.7 us)
Async XLA Ops:
  0.6 1.0 %copy-start.3 = (bf16[1024,128]{1,0:T(8,128)(2,1)S(1)}, bf16[1024,128]{1,0:T(8,128)(2,1)}, u32[]{:S(2)}) copy-start(bf16[1024,128]{1,0:T(8,128)(2,1)} %rec_ref.1) | copy-start | bytes 786436
  4.3 1.7 %collective-permute-start = (bf16[8,144,128]{2,1,0:T(8,128)(2,1)S(1)}, bf16[8,144,128]{2,1,0:T(8,128)(2,1)S(1)}, u32[]{:S(2)}, u32[]{:S(2)}) collective-permute-start(bf16[8,144,128]{2,1,0:T(8,128)(2,1)S(1)} %get-tuple-element.40), channel_id=1, source_target_pairs={{0,1},{1,0},{2,3},{3,2},{4,5},{5,4},{6,7},{7,6},{8,9},{9,8},{10,11... | collective-permute-start | bytes 884744 | tf_op jit(solution)/shard_map/ppermute | solution.py:362
  6.1 9.9 %collective-permute-start.1 = (bf16[272,128]{1,0:T(8,128)(2,1)S(1)}, bf16[272,128]{1,0:T(8,128)(2,1)S(1)}, u32[]{:S(2)}, u32[]{:S(2)}) collective-permute-start(bf16[272,128]{1,0:T(8,128)(2,1)S(1)} %get-tuple-element.42), channel_id=1, source_target_pairs={{0,2},{1,3},{2,0},{3,1},{4,6},{5,7},{6,4},{7,5},{8,10},{9,11},{10,... | collective-permute-start | bytes 208904 | tf_op jit(solution)/shard_map/ppermute | solution.py:373
  9.1 9.2 %collective-permute-start.2 = (bf16[272,128]{1,0:T(8,128)(2,1)S(1)}, bf16[272,128]{1,0:T(8,128)(2,1)S(1)}, u32[]{:S(2)}, u32[]{:S(2)}) collective-permute-start(bf16[272,128]{1,0:T(8,128)(2,1)S(1)} %get-tuple-element.43), channel_id=1, source_target_pairs={{0,4},{1,5},{2,6},{3,7},{4,8},{5,9},{6,10},{7,11},{8,12},{9,13},{1... | collective-permute-start | bytes 208904 | tf_op jit(solution)/shard_map/ppermute | solution.py:373
  10.6 7.9 %collective-permute-start.3 = (bf16[272,128]{1,0:T(8,128)(2,1)S(1)}, bf16[272,128]{1,0:T(8,128)(2,1)S(1)}, u32[]{:S(2)}, u32[]{:S(2)}) collective-permute-start(bf16[272,128]{1,0:T(8,128)(2,1)S(1)} %get-tuple-element.44), channel_id=1, source_target_pairs={{0,6},{1,7},{2,4},{3,5},{4,10},{5,11},{6,8},{7,9},{8,14},{9,15},{1... | collective-permute-start | bytes 208904 | tf_op jit(solution)/shard_map/ppermute | solution.py:373
  12.1 8.9 %collective-permute-start.4 = (bf16[272,128]{1,0:T(8,128)(2,1)S(1)}, bf16[272,128]{1,0:T(8,128)(2,1)S(1)}, u32[]{:S(2)}, u32[]{:S(2)}) collective-permute-start(bf16[272,128]{1,0:T(8,128)(2,1)S(1)} %get-tuple-element.45), channel_id=1, source_target_pairs={{0,8},{1,9},{2,10},{3,11},{4,12},{5,13},{6,14},{7,15},{8,0},{9,1},... | collective-permute-start | bytes 208904 | tf_op jit(solution)/shard_map/ppermute | solution.py:373
  13.2 10.5 %collective-permute-start.5 = (bf16[272,128]{1,0:T(8,128)(2,1)S(1)}, bf16[272,128]{1,0:T(8,128)(2,1)S(1)}, u32[]{:S(2)}, u32[]{:S(2)}) collective-permute-start(bf16[272,128]{1,0:T(8,128)(2,1)S(1)} %get-tuple-element.46), channel_id=1, source_target_pairs={{0,10},{1,11},{2,8},{3,9},{4,14},{5,15},{6,12},{7,13},{8,2},{9,3},... | collective-permute-start | bytes 208904 | tf_op jit(solution)/shard_map/ppermute | solution.py:373
  16.0 7.7 %collective-permute-start.6 = (bf16[272,128]{1,0:T(8,128)(2,1)S(1)}, bf16[272,128]{1,0:T(8,128)(2,1)S(1)}, u32[]{:S(2)}, u32[]{:S(2)}) collective-permute-start(bf16[272,128]{1,0:T(8,128)(2,1)S(1)} %get-tuple-element.47), channel_id=1, source_target_pairs={{0,12},{1,13},{2,14},{3,15},{4,0},{5,1},{6,2},{7,3},{8,4},{9,5},{1... | collective-permute-start | bytes 208904 | tf_op jit(solution)/shard_map/ppermute | solution.py:373
  18.3 5.7 %collective-permute-start.7 = (bf16[272,128]{1,0:T(8,128)(2,1)S(1)}, bf16[272,128]{1,0:T(8,128)(2,1)S(1)}, u32[]{:S(2)}, u32[]{:S(2)}) collective-permute-start(bf16[272,128]{1,0:T(8,128)(2,1)S(1)} %get-tuple-element.48), channel_id=1, source_target_pairs={{0,14},{1,15},{2,12},{3,13},{4,2},{5,3},{6,0},{7,1},{8,6},{9,7},{1... | collective-permute-start | bytes 208904 | tf_op jit(solution)/shard_map/ppermute | solution.py:373
  18.5 9.5 %slice-start = ((s8[6291456]{0:T(1024)(128)(4,1)}), s8[4194304]{0:T(1024)(128)(4,1)S(1)}, s32[]{:S(2)}) async-start(s8[6291456]{0:T(1024)(128)(4,1)} %bitcast.4), calls=%async_computation | async-start | bytes 8388608
  20.3 5.6 %copy-start.2 = (s32[32,3]{0,1:T(4,128)S(1)}, s32[32,3]{0,1:T(4,128)}, u32[]{:S(2)}) copy-start(s32[32,3]{0,1:T(4,128)} %param.11) | copy-start | bytes 1156
  20.3 7.7 %slice-start.1 = ((s8[6291456]{0:T(1024)(128)(4,1)}), s8[2097152]{0:T(1024)(128)(4,1)S(1)}, s32[]{:S(2)}) async-start(s8[6291456]{0:T(1024)(128)(4,1)} %bitcast.4), calls=%async_computation.1 | async-start | bytes 4194304
  24.0 1.9 %copy-start = (bf16[32,3,96,96]{3,2,1,0:T(8,128)(2,1)S(1)}, bf16[32,3,96,96]{3,2,1,0:T(8,128)(2,1)}, u32[]{:S(2)}) copy-start(bf16[32,3,96,96]{3,2,1,0:T(8,128)(2,1)} %stiff_ref.5) | copy-start | bytes 5308420
  25.2 2.8 %collective-permute-start.9 = (bf16[768,128]{1,0:T(8,128)(2,1)S(1)}, bf16[768,128]{1,0:T(8,128)(2,1)S(1)}, u32[]{:S(2)}, u32[]{:S(2)}) collective-permute-start(bf16[768,128]{1,0:T(8,128)(2,1)S(1)} %shard_map.91.near_ref), channel_id=1, source_target_pairs={{0,1},{1,0},{2,3},{3,2},{4,5},{5,4},{6,7},{7,6},{8,9},{9,8},{10,11... | collective-permute-start | bytes 589832 | tf_op jit(solution)/shard_map/ppermute | solution.py:362
  25.2 4.5 %collective-permute-start.8 = (bf16[768,128]{1,0:T(8,128)(2,1)S(1)}, bf16[768,128]{1,0:T(8,128)(2,1)S(1)}, u32[]{:S(2)}, u32[]{:S(2)}) collective-permute-start(bf16[768,128]{1,0:T(8,128)(2,1)S(1)} %get-tuple-element.51.far_ref), channel_id=1, source_target_pairs={{1,2},{3,4},{5,6},{7,8},{9,10},{11,12},{13,14},{2,1},{4,3},{6,5},{... | collective-permute-start | bytes 589832 | tf_op jit(solution)/shard_map/ppermute | solution.py:366
  29.7 17.1 %copy-start.1 = (f32[1024,1024]{1,0:T(8,128)S(1)}, f32[1024,1024]{1,0:T(8,128)}, u32[]{:S(2)}) copy-start(f32[1024,1024]{1,0:T(8,128)} %a_ref.1) | copy-start | bytes 12582916
  31.1 5.0 %collective-permute-start.10 = (f32[64,1024]{1,0:T(8,128)S(1)}, f32[64,1024]{1,0:T(8,128)S(1)}, u32[]{:S(2)}, u32[]{:S(2)}) collective-permute-start(f32[64,1024]{1,0:T(8,128)S(1)} %get-tuple-element.57), channel_id=1, source_target_pairs={{0,1},{1,0},{2,3},{3,2},{4,5},{5,4},{6,7},{7,6},{8,9},{9,8},{10,11... | collective-permute-start | bytes 786440 | tf_op jit(solution)/shard_map/ppermute | solution.py:362
  36.2 5.2 %collective-permute-start.11 = (bf16[32,1024]{1,0:T(8,128)(2,1)S(1)}, bf16[32,1024]{1,0:T(8,128)(2,1)S(1)}, u32[]{:S(2)}, u32[]{:S(2)}) collective-permute-start(bf16[32,1024]{1,0:T(8,128)(2,1)S(1)} %get-tuple-element.59), channel_id=1, source_target_pairs={{0,2},{1,3},{2,0},{3,1},{4,6},{5,7},{6,4},{7,5},{8,10},{9,11},{10,... | collective-permute-start | bytes 196616 | tf_op jit(solution)/shard_map/ppermute | solution.py:362
  41.4 6.8 %collective-permute-start.14 = (bf16[32,1024]{1,0:T(8,128)(2,1)S(1)}, bf16[32,1024]{1,0:T(8,128)(2,1)S(1)}, u32[]{:S(2)}, u32[]{:S(2)}) collective-permute-start(bf16[32,1024]{1,0:T(8,128)(2,1)S(1)} %get-tuple-element.61), channel_id=1, source_target_pairs={{0,8},{1,9},{2,10},{3,11},{4,12},{5,13},{6,14},{7,15},{8,0},{9,1},... | collective-permute-start | bytes 196616 | tf_op jit(solution)/shard_map/ppermute | solution.py:373
  44.1 4.6 %collective-permute-start.13 = (bf16[32,1024]{1,0:T(8,128)(2,1)S(1)}, bf16[32,1024]{1,0:T(8,128)(2,1)S(1)}, u32[]{:S(2)}, u32[]{:S(2)}) collective-permute-start(bf16[32,1024]{1,0:T(8,128)(2,1)S(1)} %get-tuple-element.61), channel_id=1, source_target_pairs={{0,12},{1,13},{2,14},{3,15},{4,0},{5,1},{6,2},{7,3},{8,4},{9,5},{1... | collective-permute-start | bytes 196616 | tf_op jit(solution)/shard_map/ppermute | solution.py:373
  46.8 6.1 %collective-permute-start.12 = (bf16[32,1024]{1,0:T(8,128)(2,1)S(1)}, bf16[32,1024]{1,0:T(8,128)(2,1)S(1)}, u32[]{:S(2)}, u32[]{:S(2)}) collective-permute-start(bf16[32,1024]{1,0:T(8,128)(2,1)S(1)} %get-tuple-element.61), channel_id=1, source_target_pairs={{0,4},{1,5},{2,6},{3,7},{4,8},{5,9},{6,10},{7,11},{8,12},{9,13},{1... | collective-permute-start | bytes 196616 | tf_op jit(solution)/shard_map/ppermute | solution.py:373
  53.7 4.3 %collective-permute-start.15 = (bf16[32,1024]{1,0:T(8,128)(2,1)S(1)}, bf16[32,1024]{1,0:T(8,128)(2,1)S(1)}, u32[]{:S(2)}, u32[]{:S(2)}) collective-permute-start(bf16[32,1024]{1,0:T(8,128)(2,1)S(1)} %shard_map.98.own_ref), channel_id=1, source_target_pairs={{0,2},{1,3},{2,0},{3,1},{4,6},{5,7},{6,4},{7,5},{8,10},{9,11},{10,... | collective-permute-start | bytes 196616 | tf_op jit(solution)/shard_map/ppermute | solution.py:362
  56.7 1.3 %collective-permute-start.16 = (bf16[32,1024]{1,0:T(8,128)(2,1)S(1)}, bf16[32,1024]{1,0:T(8,128)(2,1)S(1)}, u32[]{:S(2)}, u32[]{:S(2)}) collective-permute-start(bf16[32,1024]{1,0:T(8,128)(2,1)S(1)} %shard_map.98.own_ref), channel_id=1, source_target_pairs={{0,1},{1,0},{2,3},{3,2},{4,5},{5,4},{6,7},{7,6},{8,9},{9,8},{10,11... | collective-permute-start | bytes 196616 | tf_op jit(solution)/shard_map/ppermute | solution.py:362
  58.0 1.3 %collective-permute-start.17 = (bf16[32,1024]{1,0:T(8,128)(2,1)S(1)}, bf16[32,1024]{1,0:T(8,128)(2,1)S(1)}, u32[]{:S(2)}, u32[]{:S(2)}) collective-permute-start(bf16[32,1024]{1,0:T(8,128)(2,1)S(1)} %collective-permute-done.15.y_ref), channel_id=1, source_target_pairs={{0,1},{1,0},{2,3},{3,2},{4,5},{5,4},{6,7},{7,6},{8,9},{9,8},{10,11... | collective-permute-start | bytes 196616 | tf_op jit(solution)/shard_map/ppermute | solution.py:362
  (2 other events, 1.4 us)

commit v4 on v3

--- a/solution.py
+++ b/solution.py
@@ -68,17 +68,27 @@
 
 
 def pack_kernel(
-    cap, owner_ref, slot_ref, rec_ref, cross_ref, rank_ref, slots_ref, held_ref
+    cap, owner_hbm, slot_hbm, rec_hbm, cross_ref, owner_ref, rank_ref, slots_ref, rec_ref,
+    slot_ref, sems,
 ):
+    copies = [
+        pltpu.make_async_copy(source, target, sems.at[k])
+        for k, (source, target) in enumerate(
+            ((owner_hbm, owner_ref), (slot_hbm, slot_ref), (rec_hbm, rec_ref))
+        )
+    ]
+    for copy in copies:
+        copy.start()
     pan = rec_ref.shape[0]
     owners = slots_ref.shape[1] // 2
     pieces = pan // LANES
     before = lax.broadcasted_iota(jnp.int32, (LANES, LANES), 0)
     after = lax.broadcasted_iota(jnp.int32, (LANES, LANES), 1)
     triangle = jnp.where(before <= after, 1.0, 0.0).astype(BF)
+    copies[0].wait()
+    copies[1].wait()
     owner = owner_ref[...]
     slot = jnp.concatenate([slot_ref[k : k + 1, :] for k in range(pieces)], axis=1)
-    held_ref[...] = rec_ref[...]
     match = lax.broadcasted_iota(jnp.int32, (owners, pan), 0) == owner
     match_f = jnp.where(match, 1.0, 0.0)
     stacked = jnp.concatenate(
@@ -100,6 +110,7 @@
     for place in range(LANES // cap):
         spread = hot(LANES, (rank + float(place * cap)).astype(BF))
         slots_ref[place] = lax.dot_general(weights, spread, NT, preferred_element_type=F32)
+    copies[2].wait()
     write_messages(1, cap, owners // 2, owner, rank, rec_ref[...], slots_ref, cross_ref)
 
 
@@ -358,6 +369,9 @@
     halo = REACH * size
     message = (chips, cap + TAIL, width)
 
+    def stay(array):
+        return pltpu.with_memory_space_constraint(array, pltpu.HBM)
+
     def swap(array, mask):
         return lax.ppermute(array, "elem", [(i, i ^ mask) for i in range(owners)])
 
@@ -372,18 +386,23 @@
             pairs.append((i, ((z + dz) % (chips // 2) * 2 + (y + dy) % 2) * 2 + core))
         return lax.ppermute(array, "elem", pairs)
 
-    owner = panel_owner.reshape(1, pan)
-    cross, rank, slots, held = call(
+    cross, owner, rank, slots, held = call(
         functools.partial(pack_kernel, cap),
         (
             shape(message, BF),
+            shape((1, pan), jnp.int32),
             shape((1, pan), F32),
             shape((share, 2 * owners, LANES), F32),
             shape((pan, width), BF),
         ),
-        owner,
-        panel_slot.reshape(pan // LANES, LANES),
-        records,
+        stay(panel_owner.reshape(1, pan)),
+        stay(panel_slot.reshape(pan // LANES, LANES)),
+        stay(records),
+        hbm=(0, 1, 2),
+        scratch=(
+            pltpu.VMEM((pan // LANES, LANES), jnp.int32),
+            pltpu.SemaphoreType.DMA((3,)),
+        ),
         flops=owners * cap * pan * width,
     )
     got_cross = swap(cross, 1)

time: 61.6 us -> 60.1 us (0.976)
  local copies, waits for them, and re-layouts: 2.34 us -> 0.03 us
  Pallas kernels: 16.3 us -> 17.2 us
    unnamed x16 -> x10, local copies, waits for them, and re-layouts: 2.34 us -> 0.03 us
    pallas_call x15, Pallas kernels: 16.3 us -> 17.2 us  [call(): pl.pallas_call(kernel, out_shape=out_shape, in_specs=[pl.BlockSpec(memory...]
where the time goes in v4:
time: 60.1 us; the launch traced here: 59.9 us
  starting transfers between devices  26.8 us (45%)
  Pallas kernels  17.2 us (29%)
  waiting for transfers between devices  15 us (25%)
  between operations  0.99 us (2%)
    ppermute x10, starting transfers between devices, turn(): return lax.ppermute(array, 'elem', pairs)  17.8 us
    pallas_call x15, Pallas kernels, call(): pl.pallas_call(kernel, out_shape=out_shape, in_specs=[pl.BlockSpec(memory...  17.2 us
    ppermute x10, waiting for transfers between devices, turn(): return lax.ppermute(array, 'elem', pairs)  8.4 us
    ppermute x7, starting transfers between devices, swap(): return lax.ppermute(array, 'elem', [(i, i ^ mask) for i in range(owners)])  8.24 us
    ppermute x7, waiting for transfers between devices, swap(): return lax.ppermute(array, 'elem', [(i, i ^ mask) for i in range(owners)])  6.55 us
  transfers between devices with their start and end apart: 18, of which 10 were waited for; matrix products, arithmetic and copies ran while one was open for 0% of the time, Pallas kernels for 16%

profile of v4, /device:TPU:0, one launch (start us, length us, event | category | flops | bytes accessed | tf_op | source)
XLA Modules:
  0.0 59.9 jit_solution(16823378120954460137)
XLA Ops:
  0.6 2.3 %shard_map.86 = (bf16[8,144,128]{2,1,0:T(8,128)(2,1)S(1)}, s32[1,1024]{1,0:T(1,128)S(1)}, f32[1,1024]{1,0:T(1,128)S(1)}, f32[1,32,128]{2,1,0:T(8,128)S(1)}, bf16[1024,128]{1,0:T(8,128)(2,1)S(1)}) custom-call(s32[1,1024]{1,0:T(1,128)} %bitcast.10, s32[8,128]{1,0:T(8,128)} %bitcast.11, bf16[1024,128]{1,0:T(8,128)(2,1)} %rec_hbm.1), custom_call_target="tpu_custom_call" | custom-call | flops 268435456 | bytes 270336 | tf_op jit(solution)/shard_map/pallas_call | solution.py:26
  4.7 3.0 %collective-permute-start.1 = (bf16[272,128]{1,0:T(8,128)(2,1)S(1)}, bf16[272,128]{1,0:T(8,128)(2,1)S(1)}, u32[]{:S(2)}, u32[]{:S(2)}) collective-permute-start(bf16[272,128]{1,0:T(8,128)(2,1)S(1)} %get-tuple-element.44), channel_id=1, source_target_pairs={{0,2},{1,3},{2,0},{3,1},{4,6},{5,7},{6,4},{7,5},{8,10},{9,11},{10,... | collective-permute-start | bytes 208904 | tf_op jit(solution)/shard_map/ppermute | solution.py:387
  7.6 1.6 %collective-permute-start.2 = (bf16[272,128]{1,0:T(8,128)(2,1)S(1)}, bf16[272,128]{1,0:T(8,128)(2,1)S(1)}, u32[]{:S(2)}, u32[]{:S(2)}) collective-permute-start(bf16[272,128]{1,0:T(8,128)(2,1)S(1)} %get-tuple-element.45), channel_id=1, source_target_pairs={{0,4},{1,5},{2,6},{3,7},{4,8},{5,9},{6,10},{7,11},{8,12},{9,13},{1... | collective-permute-start | bytes 208904 | tf_op jit(solution)/shard_map/ppermute | solution.py:387
  9.2 1.5 %collective-permute-start.3 = (bf16[272,128]{1,0:T(8,128)(2,1)S(1)}, bf16[272,128]{1,0:T(8,128)(2,1)S(1)}, u32[]{:S(2)}, u32[]{:S(2)}) collective-permute-start(bf16[272,128]{1,0:T(8,128)(2,1)S(1)} %get-tuple-element.46), channel_id=1, source_target_pairs={{0,6},{1,7},{2,4},{3,5},{4,10},{5,11},{6,8},{7,9},{8,14},{9,15},{1... | collective-permute-start | bytes 208904 | tf_op jit(solution)/shard_map/ppermute | solution.py:387
  10.7 1.1 %collective-permute-start.4 = (bf16[272,128]{1,0:T(8,128)(2,1)S(1)}, bf16[272,128]{1,0:T(8,128)(2,1)S(1)}, u32[]{:S(2)}, u32[]{:S(2)}) collective-permute-start(bf16[272,128]{1,0:T(8,128)(2,1)S(1)} %get-tuple-element.47), channel_id=1, source_target_pairs={{0,8},{1,9},{2,10},{3,11},{4,12},{5,13},{6,14},{7,15},{8,0},{9,1},... | collective-permute-start | bytes 208904 | tf_op jit(solution)/shard_map/ppermute | solution.py:387
  11.8 2.8 %collective-permute-start.5 = (bf16[272,128]{1,0:T(8,128)(2,1)S(1)}, bf16[272,128]{1,0:T(8,128)(2,1)S(1)}, u32[]{:S(2)}, u32[]{:S(2)}) collective-permute-start(bf16[272,128]{1,0:T(8,128)(2,1)S(1)} %get-tuple-element.48), channel_id=1, source_target_pairs={{0,10},{1,11},{2,8},{3,9},{4,14},{5,15},{6,12},{7,13},{8,2},{9,3},... | collective-permute-start | bytes 208904 | tf_op jit(solution)/shard_map/ppermute | solution.py:387
  14.6 2.2 %collective-permute-start.6 = (bf16[272,128]{1,0:T(8,128)(2,1)S(1)}, bf16[272,128]{1,0:T(8,128)(2,1)S(1)}, u32[]{:S(2)}, u32[]{:S(2)}) collective-permute-start(bf16[272,128]{1,0:T(8,128)(2,1)S(1)} %get-tuple-element.49), channel_id=1, source_target_pairs={{0,12},{1,13},{2,14},{3,15},{4,0},{5,1},{6,2},{7,3},{8,4},{9,5},{1... | collective-permute-start | bytes 208904 | tf_op jit(solution)/shard_map/ppermute | solution.py:387
  17.1 1.8 %shard_map.89.refs_4_.sum_ref = f32[3072,128]{1,0:T(8,128)S(1)} custom-call(bf16[272,128]{1,0:T(8,128)(2,1)S(1)} %get-tuple-element.43.refs_0_, bf16[272,128]{1,0:T(8,128)(2,1)S(1)} %collective-permute-done.1.refs_1_, bf16[272,128]{1,0:T(8,128)(2,1)S(1)} %collective-permute-done.2.refs_2_, bf16[272,128]{1,0:T(8,128)(2,1)S(1)} %collective-permute-done.3.refs_3_), custom_call_target="tpu_custom_call" | custom-call | flops 805306368 | bytes 278528 | tf_op jit(solution)/shard_map/pallas_call | solution.py:26
  19.6 2.7 %collective-permute-done.5.refs_1_ = bf16[272,128]{1,0:T(8,128)(2,1)S(1)} collective-permute-done((bf16[272,128]{1,0:T(8,128)(2,1)S(1)}, bf16[272,128]{1,0:T(8,128)(2,1)S(1)}, u32[]{:S(2)}, u32[]{:S(2)}) %collective-permute-start.5) | collective-permute-done | bytes 69664 | tf_op jit(solution)/shard_map/ppermute | solution.py:387
  24.5 2.0 %shard_map.92 = (bf16[3072,128]{1,0:T(8,128)(2,1)S(1)}, bf16[1536,128]{1,0:T(8,128)(2,1)S(1)}) custom-call(f32[3072,128]{1,0:T(8,128)S(1)} %shard_map.89.refs_4_.sum_ref, f32[1,1024]{1,0:T(1,128)S(1)} %get-tuple-element.51.slots_ref, bf16[1024,128]{1,0:T(8,128)(2,1)S(1)} %get-tuple-element.52.records_ref, bf16[768,128]{1,0:T(8,128)(2,1)S(1)} %shard_map.91.near_ref, ...), custom_call_target="tpu_custom_call" | custom-call | flops 402653184 | bytes 4002176 | tf_op jit(solution)/shard_map/pallas_call | solution.py:26
  26.6 1.7 %shard_map.93 = (bf16[768,128]{1,0:T(8,128)(2,1)S(1)}, f32[128,1024]{1,0:T(8,128)S(1)}) custom-call(bf16[3072,128]{1,0:T(8,128)(2,1)S(1)} %get-tuple-element.54.loads_ref, bf16[768,128]{1,0:T(8,128)(2,1)S(1)} %collective-permute-done.9.got_ref, bf16[32,3,96,96]{3,2,1,0:T(8,128)(2,1)S(1)} %copy-done, s32[3,32]{1,0:T(4,128)S(1)} %bitcast.7, ...), custom_call_target="tpu_custom_call" | custom-call | flops 603979776 | bytes 9437568 | tf_op jit(solution)/shard_map/pallas_call | solution.py:26
  28.4 1.3 %shard_map.94 = (bf16[1536,128]{1,0:T(8,128)(2,1)S(1)}, f32[64,1024]{1,0:T(8,128)S(1)}, f32[64,1024]{1,0:T(8,128)S(1)}) custom-call(bf16[3072,128]{1,0:T(8,128)(2,1)S(1)} %get-tuple-element.54.loads_ref, bf16[768,128]{1,0:T(8,128)(2,1)S(1)} %collective-permute-done.8.got_ref, bf16[32,3,96,96]{3,2,1,0:T(8,128)(2,1)S(1)} %copy-done, s32[3,32]{1,0:T(4,128)S(1)} %bitcast.8, ...), custom_call_target="tpu_custom_call" | custom-call | flops 201326592 | bytes 9765248 | tf_op jit(solution)/shard_map/pallas_call | solution.py:26
  29.7 3.8 %collective-permute-start.10 = (f32[64,1024]{1,0:T(8,128)S(1)}, f32[64,1024]{1,0:T(8,128)S(1)}, u32[]{:S(2)}, u32[]{:S(2)}) collective-permute-start(f32[64,1024]{1,0:T(8,128)S(1)} %get-tuple-element.59), channel_id=1, source_target_pairs={{0,1},{1,0},{2,3},{3,2},{4,5},{5,4},{6,7},{7,6},{8,9},{9,8},{10,11... | collective-permute-start | bytes 786440 | tf_op jit(solution)/shard_map/ppermute | solution.py:376
  33.5 1.2 %collective-permute-done.10.other_ref = f32[64,1024]{1,0:T(8,128)S(1)} collective-permute-done((f32[64,1024]{1,0:T(8,128)S(1)}, f32[64,1024]{1,0:T(8,128)S(1)}, u32[]{:S(2)}, u32[]{:S(2)}) %collective-permute-start.10) | collective-permute-done | bytes 262176 | tf_op jit(solution)/shard_map/ppermute | solution.py:376
  34.8 2.8 %collective-permute-start.11 = (bf16[32,1024]{1,0:T(8,128)(2,1)S(1)}, bf16[32,1024]{1,0:T(8,128)(2,1)S(1)}, u32[]{:S(2)}, u32[]{:S(2)}) collective-permute-start(bf16[32,1024]{1,0:T(8,128)(2,1)S(1)} %get-tuple-element.61), channel_id=1, source_target_pairs={{0,2},{1,3},{2,0},{3,1},{4,6},{5,7},{6,4},{7,5},{8,10},{9,11},{10,... | collective-permute-start | bytes 196616 | tf_op jit(solution)/shard_map/ppermute | solution.py:376
  37.6 2.4 %collective-permute-done.11.other_ref = bf16[32,1024]{1,0:T(8,128)(2,1)S(1)} collective-permute-done((bf16[32,1024]{1,0:T(8,128)(2,1)S(1)}, bf16[32,1024]{1,0:T(8,128)(2,1)S(1)}, u32[]{:S(2)}, u32[]{:S(2)}) %collective-permute-start.11) | collective-permute-done | bytes 65568 | tf_op jit(solution)/shard_map/ppermute | solution.py:376
  40.0 2.7 %collective-permute-start.14 = (bf16[32,1024]{1,0:T(8,128)(2,1)S(1)}, bf16[32,1024]{1,0:T(8,128)(2,1)S(1)}, u32[]{:S(2)}, u32[]{:S(2)}) collective-permute-start(bf16[32,1024]{1,0:T(8,128)(2,1)S(1)} %get-tuple-element.63), channel_id=1, source_target_pairs={{0,8},{1,9},{2,10},{3,11},{4,12},{5,13},{6,14},{7,15},{8,0},{9,1},... | collective-permute-start | bytes 196616 | tf_op jit(solution)/shard_map/ppermute | solution.py:387
  42.7 2.7 %collective-permute-start.13 = (bf16[32,1024]{1,0:T(8,128)(2,1)S(1)}, bf16[32,1024]{1,0:T(8,128)(2,1)S(1)}, u32[]{:S(2)}, u32[]{:S(2)}) collective-permute-start(bf16[32,1024]{1,0:T(8,128)(2,1)S(1)} %get-tuple-element.63), channel_id=1, source_target_pairs={{0,12},{1,13},{2,14},{3,15},{4,0},{5,1},{6,2},{7,3},{8,4},{9,5},{1... | collective-permute-start | bytes 196616 | tf_op jit(solution)/shard_map/ppermute | solution.py:387
  45.4 1.3 %shard_map.97 = (bf16[1024,1024]{1,0:T(8,128)(2,1)S(1)}, bf16[1024,1024]{1,0:T(8,128)(2,1)S(1)}) custom-call(f32[1024,1024]{1,0:T(8,128)S(1)} %copy-done.1), custom_call_target="tpu_custom_call" | custom-call | flops 4194304 | bytes 4194304 | tf_op jit(solution)/shard_map/pallas_call | solution.py:26
  47.3 4.2 %collective-permute-done.12.refs_0_ = bf16[32,1024]{1,0:T(8,128)(2,1)S(1)} collective-permute-done((bf16[32,1024]{1,0:T(8,128)(2,1)S(1)}, bf16[32,1024]{1,0:T(8,128)(2,1)S(1)}, u32[]{:S(2)}, u32[]{:S(2)}) %collective-permute-start.12) | collective-permute-done | bytes 65568 | tf_op jit(solution)/shard_map/ppermute | solution.py:387
  53.2 2.0 %shard_map.99 = (bf16[1024,3072]{1,0:T(8,128)(2,1)S(1)}, bf16[128,3072]{1,0:T(8,128)(2,1)S(1)}) custom-call(bf16[3072,1024]{1,0:T(8,128)(2,1)S(1)} %bitcast.5, bf16[1536,128]{1,0:T(8,128)(2,1)S(1)} %get-tuple-element.55.mid_ref, bf16[1536,128]{1,0:T(8,128)(2,1)S(1)} %get-tuple-element.66.edge_ref), custom_call_target="tpu_custom_call" | custom-call | bytes 7077888 | tf_op jit(solution)/shard_map/pallas_call | solution.py:26
  55.3 1.2 %collective-permute-done.15.y_ref = bf16[32,1024]{1,0:T(8,128)(2,1)S(1)} collective-permute-done((bf16[32,1024]{1,0:T(8,128)(2,1)S(1)}, bf16[32,1024]{1,0:T(8,128)(2,1)S(1)}, u32[]{:S(2)}, u32[]{:S(2)}) %collective-permute-start.15) | collective-permute-done | bytes 65568 | tf_op jit(solution)/shard_map/ppermute | solution.py:376
  56.6 1.2 %collective-permute-done.17.both_ref = bf16[32,1024]{1,0:T(8,128)(2,1)S(1)} collective-permute-done((bf16[32,1024]{1,0:T(8,128)(2,1)S(1)}, bf16[32,1024]{1,0:T(8,128)(2,1)S(1)}, u32[]{:S(2)}, u32[]{:S(2)}) %collective-permute-start.17) | collective-permute-done | bytes 65568 | tf_op jit(solution)/shard_map/ppermute | solution.py:376
  57.8 1.9 %shard_map.100 = (bf16[3072,128]{1,0:T(8,128)(2,1)}, f32[24,128]{1,0:T(8,128)}) custom-call(bf16[32,1024]{1,0:T(8,128)(2,1)S(1)} %shard_map.98.own_ref, bf16[32,1024]{1,0:T(8,128)(2,1)S(1)} %collective-permute-done.15.y_ref, bf16[32,1024]{1,0:T(8,128)(2,1)S(1)} %collective-permute-done.16.core_ref, bf16[32,1024]{1,0:T(8,128)(2,1)S(1)} %collective-permute-done.17.both_ref, ...), custom_call_target="tpu_custom_call" | custom-call | flops 805306368 | bytes 7340032 | tf_op jit(solution)/shard_map/pallas_call | solution.py:26
  (38 shorter events, 7.4 us)
Async XLA Ops:
  2.9 1.7 %collective-permute-start = (bf16[8,144,128]{2,1,0:T(8,128)(2,1)S(1)}, bf16[8,144,128]{2,1,0:T(8,128)(2,1)S(1)}, u32[]{:S(2)}, u32[]{:S(2)}) collective-permute-start(bf16[8,144,128]{2,1,0:T(8,128)(2,1)S(1)} %get-tuple-element.42), channel_id=1, source_target_pairs={{0,1},{1,0},{2,3},{3,2},{4,5},{5,4},{6,7},{7,6},{8,9},{9,8},{10,11... | collective-permute-start | bytes 884744 | tf_op jit(solution)/shard_map/ppermute | solution.py:376
  4.7 9.9 %collective-permute-start.1 = (bf16[272,128]{1,0:T(8,128)(2,1)S(1)}, bf16[272,128]{1,0:T(8,128)(2,1)S(1)}, u32[]{:S(2)}, u32[]{:S(2)}) collective-permute-start(bf16[272,128]{1,0:T(8,128)(2,1)S(1)} %get-tuple-element.44), channel_id=1, source_target_pairs={{0,2},{1,3},{2,0},{3,1},{4,6},{5,7},{6,4},{7,5},{8,10},{9,11},{10,... | collective-permute-start | bytes 208904 | tf_op jit(solution)/shard_map/ppermute | solution.py:387
  7.6 9.2 %collective-permute-start.2 = (bf16[272,128]{1,0:T(8,128)(2,1)S(1)}, bf16[272,128]{1,0:T(8,128)(2,1)S(1)}, u32[]{:S(2)}, u32[]{:S(2)}) collective-permute-start(bf16[272,128]{1,0:T(8,128)(2,1)S(1)} %get-tuple-element.45), channel_id=1, source_target_pairs={{0,4},{1,5},{2,6},{3,7},{4,8},{5,9},{6,10},{7,11},{8,12},{9,13},{1... | collective-permute-start | bytes 208904 | tf_op jit(solution)/shard_map/ppermute | solution.py:387
  9.2 7.9 %collective-permute-start.3 = (bf16[272,128]{1,0:T(8,128)(2,1)S(1)}, bf16[272,128]{1,0:T(8,128)(2,1)S(1)}, u32[]{:S(2)}, u32[]{:S(2)}) collective-permute-start(bf16[272,128]{1,0:T(8,128)(2,1)S(1)} %get-tuple-element.46), channel_id=1, source_target_pairs={{0,6},{1,7},{2,4},{3,5},{4,10},{5,11},{6,8},{7,9},{8,14},{9,15},{1... | collective-permute-start | bytes 208904 | tf_op jit(solution)/shard_map/ppermute | solution.py:387
  10.7 8.9 %collective-permute-start.4 = (bf16[272,128]{1,0:T(8,128)(2,1)S(1)}, bf16[272,128]{1,0:T(8,128)(2,1)S(1)}, u32[]{:S(2)}, u32[]{:S(2)}) collective-permute-start(bf16[272,128]{1,0:T(8,128)(2,1)S(1)} %get-tuple-element.47), channel_id=1, source_target_pairs={{0,8},{1,9},{2,10},{3,11},{4,12},{5,13},{6,14},{7,15},{8,0},{9,1},... | collective-permute-start | bytes 208904 | tf_op jit(solution)/shard_map/ppermute | solution.py:387
  11.8 10.5 %collective-permute-start.5 = (bf16[272,128]{1,0:T(8,128)(2,1)S(1)}, bf16[272,128]{1,0:T(8,128)(2,1)S(1)}, u32[]{:S(2)}, u32[]{:S(2)}) collective-permute-start(bf16[272,128]{1,0:T(8,128)(2,1)S(1)} %get-tuple-element.48), channel_id=1, source_target_pairs={{0,10},{1,11},{2,8},{3,9},{4,14},{5,15},{6,12},{7,13},{8,2},{9,3},... | collective-permute-start | bytes 208904 | tf_op jit(solution)/shard_map/ppermute | solution.py:387
  14.6 7.7 %collective-permute-start.6 = (bf16[272,128]{1,0:T(8,128)(2,1)S(1)}, bf16[272,128]{1,0:T(8,128)(2,1)S(1)}, u32[]{:S(2)}, u32[]{:S(2)}) collective-permute-start(bf16[272,128]{1,0:T(8,128)(2,1)S(1)} %get-tuple-element.49), channel_id=1, source_target_pairs={{0,12},{1,13},{2,14},{3,15},{4,0},{5,1},{6,2},{7,3},{8,4},{9,5},{1... | collective-permute-start | bytes 208904 | tf_op jit(solution)/shard_map/ppermute | solution.py:387
  16.9 5.7 %collective-permute-start.7 = (bf16[272,128]{1,0:T(8,128)(2,1)S(1)}, bf16[272,128]{1,0:T(8,128)(2,1)S(1)}, u32[]{:S(2)}, u32[]{:S(2)}) collective-permute-start(bf16[272,128]{1,0:T(8,128)(2,1)S(1)} %get-tuple-element.50), channel_id=1, source_target_pairs={{0,14},{1,15},{2,12},{3,13},{4,2},{5,3},{6,0},{7,1},{8,6},{9,7},{1... | collective-permute-start | bytes 208904 | tf_op jit(solution)/shard_map/ppermute | solution.py:387
  17.1 9.5 %slice-start = ((s8[6291456]{0:T(1024)(128)(4,1)}), s8[4194304]{0:T(1024)(128)(4,1)S(1)}, s32[]{:S(2)}) async-start(s8[6291456]{0:T(1024)(128)(4,1)} %bitcast.4), calls=%async_computation | async-start | bytes 8388608
  18.9 5.6 %copy-start.2 = (s32[32,3]{0,1:T(4,128)S(1)}, s32[32,3]{0,1:T(4,128)}, u32[]{:S(2)}) copy-start(s32[32,3]{0,1:T(4,128)} %param.11) | copy-start | bytes 1156
  18.9 7.7 %slice-start.1 = ((s8[6291456]{0:T(1024)(128)(4,1)}), s8[2097152]{0:T(1024)(128)(4,1)S(1)}, s32[]{:S(2)}) async-start(s8[6291456]{0:T(1024)(128)(4,1)} %bitcast.4), calls=%async_computation.1 | async-start | bytes 4194304
  22.6 1.9 %copy-start = (bf16[32,3,96,96]{3,2,1,0:T(8,128)(2,1)S(1)}, bf16[32,3,96,96]{3,2,1,0:T(8,128)(2,1)}, u32[]{:S(2)}) copy-start(bf16[32,3,96,96]{3,2,1,0:T(8,128)(2,1)} %stiff_ref.5) | copy-start | bytes 5308420
  23.8 2.8 %collective-permute-start.9 = (bf16[768,128]{1,0:T(8,128)(2,1)S(1)}, bf16[768,128]{1,0:T(8,128)(2,1)S(1)}, u32[]{:S(2)}, u32[]{:S(2)}) collective-permute-start(bf16[768,128]{1,0:T(8,128)(2,1)S(1)} %shard_map.91.near_ref), channel_id=1, source_target_pairs={{0,1},{1,0},{2,3},{3,2},{4,5},{5,4},{6,7},{7,6},{8,9},{9,8},{10,11... | collective-permute-start | bytes 589832 | tf_op jit(solution)/shard_map/ppermute | solution.py:376
  23.8 4.5 %collective-permute-start.8 = (bf16[768,128]{1,0:T(8,128)(2,1)S(1)}, bf16[768,128]{1,0:T(8,128)(2,1)S(1)}, u32[]{:S(2)}, u32[]{:S(2)}) collective-permute-start(bf16[768,128]{1,0:T(8,128)(2,1)S(1)} %get-tuple-element.53.far_ref), channel_id=1, source_target_pairs={{1,2},{3,4},{5,6},{7,8},{9,10},{11,12},{13,14},{2,1},{4,3},{6,5},{... | collective-permute-start | bytes 589832 | tf_op jit(solution)/shard_map/ppermute | solution.py:380
  28.3 17.1 %copy-start.1 = (f32[1024,1024]{1,0:T(8,128)S(1)}, f32[1024,1024]{1,0:T(8,128)}, u32[]{:S(2)}) copy-start(f32[1024,1024]{1,0:T(8,128)} %a_ref.1) | copy-start | bytes 12582916
  29.7 5.0 %collective-permute-start.10 = (f32[64,1024]{1,0:T(8,128)S(1)}, f32[64,1024]{1,0:T(8,128)S(1)}, u32[]{:S(2)}, u32[]{:S(2)}) collective-permute-start(f32[64,1024]{1,0:T(8,128)S(1)} %get-tuple-element.59), channel_id=1, source_target_pairs={{0,1},{1,0},{2,3},{3,2},{4,5},{5,4},{6,7},{7,6},{8,9},{9,8},{10,11... | collective-permute-start | bytes 786440 | tf_op jit(solution)/shard_map/ppermute | solution.py:376
  34.8 5.2 %collective-permute-start.11 = (bf16[32,1024]{1,0:T(8,128)(2,1)S(1)}, bf16[32,1024]{1,0:T(8,128)(2,1)S(1)}, u32[]{:S(2)}, u32[]{:S(2)}) collective-permute-start(bf16[32,1024]{1,0:T(8,128)(2,1)S(1)} %get-tuple-element.61), channel_id=1, source_target_pairs={{0,2},{1,3},{2,0},{3,1},{4,6},{5,7},{6,4},{7,5},{8,10},{9,11},{10,... | collective-permute-start | bytes 196616 | tf_op jit(solution)/shard_map/ppermute | solution.py:376
  40.0 6.7 %collective-permute-start.14 = (bf16[32,1024]{1,0:T(8,128)(2,1)S(1)}, bf16[32,1024]{1,0:T(8,128)(2,1)S(1)}, u32[]{:S(2)}, u32[]{:S(2)}) collective-permute-start(bf16[32,1024]{1,0:T(8,128)(2,1)S(1)} %get-tuple-element.63), channel_id=1, source_target_pairs={{0,8},{1,9},{2,10},{3,11},{4,12},{5,13},{6,14},{7,15},{8,0},{9,1},... | collective-permute-start | bytes 196616 | tf_op jit(solution)/shard_map/ppermute | solution.py:387
  42.7 4.6 %collective-permute-start.13 = (bf16[32,1024]{1,0:T(8,128)(2,1)S(1)}, bf16[32,1024]{1,0:T(8,128)(2,1)S(1)}, u32[]{:S(2)}, u32[]{:S(2)}) collective-permute-start(bf16[32,1024]{1,0:T(8,128)(2,1)S(1)} %get-tuple-element.63), channel_id=1, source_target_pairs={{0,12},{1,13},{2,14},{3,15},{4,0},{5,1},{6,2},{7,3},{8,4},{9,5},{1... | collective-permute-start | bytes 196616 | tf_op jit(solution)/shard_map/ppermute | solution.py:387
  45.4 6.1 %collective-permute-start.12 = (bf16[32,1024]{1,0:T(8,128)(2,1)S(1)}, bf16[32,1024]{1,0:T(8,128)(2,1)S(1)}, u32[]{:S(2)}, u32[]{:S(2)}) collective-permute-start(bf16[32,1024]{1,0:T(8,128)(2,1)S(1)} %get-tuple-element.63), channel_id=1, source_target_pairs={{0,4},{1,5},{2,6},{3,7},{4,8},{5,9},{6,10},{7,11},{8,12},{9,13},{1... | collective-permute-start | bytes 196616 | tf_op jit(solution)/shard_map/ppermute | solution.py:387
  52.3 4.3 %collective-permute-start.15 = (bf16[32,1024]{1,0:T(8,128)(2,1)S(1)}, bf16[32,1024]{1,0:T(8,128)(2,1)S(1)}, u32[]{:S(2)}, u32[]{:S(2)}) collective-permute-start(bf16[32,1024]{1,0:T(8,128)(2,1)S(1)} %shard_map.98.own_ref), channel_id=1, source_target_pairs={{0,2},{1,3},{2,0},{3,1},{4,6},{5,7},{6,4},{7,5},{8,10},{9,11},{10,... | collective-permute-start | bytes 196616 | tf_op jit(solution)/shard_map/ppermute | solution.py:376
  55.3 1.3 %collective-permute-start.16 = (bf16[32,1024]{1,0:T(8,128)(2,1)S(1)}, bf16[32,1024]{1,0:T(8,128)(2,1)S(1)}, u32[]{:S(2)}, u32[]{:S(2)}) collective-permute-start(bf16[32,1024]{1,0:T(8,128)(2,1)S(1)} %shard_map.98.own_ref), channel_id=1, source_target_pairs={{0,1},{1,0},{2,3},{3,2},{4,5},{5,4},{6,7},{7,6},{8,9},{9,8},{10,11... | collective-permute-start | bytes 196616 | tf_op jit(solution)/shard_map/ppermute | solution.py:376
  56.6 1.3 %collective-permute-start.17 = (bf16[32,1024]{1,0:T(8,128)(2,1)S(1)}, bf16[32,1024]{1,0:T(8,128)(2,1)S(1)}, u32[]{:S(2)}, u32[]{:S(2)}) collective-permute-start(bf16[32,1024]{1,0:T(8,128)(2,1)S(1)} %collective-permute-done.15.y_ref), channel_id=1, source_target_pairs={{0,1},{1,0},{2,3},{3,2},{4,5},{5,4},{6,7},{7,6},{8,9},{9,8},{10,11... | collective-permute-start | bytes 196616 | tf_op jit(solution)/shard_map/ppermute | solution.py:376

commit v5 on v4

--- a/solution.py
+++ b/solution.py
@@ -417,22 +417,26 @@
         (shape((2 * cap + TAIL, width), BF),) * chips,
         own, got_cross,
     )
-    offsets = range(1, chips)
+    offsets = list(range(1, chips))
+    if share == 1:
+        reach = chips // 2
+        offsets.sort(key=lambda j: (-(j % 2), -min(j // 2, reach - j // 2), j))
     got = {j: turn(packed[j], j // 2, j % 2) for j in offsets}
     got[0] = packed[0]
+    arrival = [0, *offsets]
     half = chips // 2
     late_rows = half * 2 * cap
     early = call(
         functools.partial(early_kernel, cap, half),
         shape((elem_rows, width), F32),
-        *[got[j] for j in range(half)],
+        *[got[j] for j in arrival[:half]],
         scratch=(pltpu.VMEM((late_rows, width), BF),),
         flops=2 * late_rows * elem_rows * width,
     )
     far, slot_row, landed = call(
         functools.partial(far_kernel, cap, chips - half),
         (shape((halo, width), BF), shape((1, late_rows), F32), shape((late_rows, width), BF)),
-        *[got[j] for j in range(half, chips)], early,
+        *[got[j] for j in arrival[half:]], early,
         flops=16 * late_rows * halo * width,
     )
     got_far = swap_far(far)

time: 60.1 us -> 58.4 us (0.972)
  waiting for transfers between devices: 15 us -> 12.7 us
    ppermute x10, waiting for transfers between devices: 8.4 us -> 6.49 us  [turn(): return lax.ppermute(array, 'elem', pairs)]
  transfers between devices with their start and end apart: 18 -> 18, of which waited for: 10 -> 12; matrix products, arithmetic and copies ran while one was open for 0% -> 0% of each run, Pallas kernels for 16% -> 16%
where the time goes in v5:
time: 58.4 us; the launch traced here: 58.2 us
  starting transfers between devices  27.3 us (47%)
  Pallas kernels  17.2 us (29%)
  waiting for transfers between devices  12.7 us (22%)
  between operations  0.99 us (2%)
    ppermute x10, starting transfers between devices, turn(): return lax.ppermute(array, 'elem', pairs)  18.3 us
    pallas_call x15, Pallas kernels, call(): pl.pallas_call(kernel, out_shape=out_shape, in_specs=[pl.BlockSpec(memory...  17.2 us
    ppermute x7, starting transfers between devices, swap(): return lax.ppermute(array, 'elem', [(i, i ^ mask) for i in range(owners)])  8.36 us
    ppermute x10, waiting for transfers between devices, turn(): return lax.ppermute(array, 'elem', pairs)  6.49 us
    ppermute x7, waiting for transfers between devices, swap(): return lax.ppermute(array, 'elem', [(i, i ^ mask) for i in range(owners)])  6.17 us
  transfers between devices with their start and end apart: 18, of which 12 were waited for; matrix products, arithmetic and copies ran while one was open for 0% of the time, Pallas kernels for 16%

profile of v5, /device:TPU:0, one launch (start us, length us, event | category | flops | bytes accessed | tf_op | source)
XLA Modules:
  0.0 58.2 jit_solution(5866333100268855829)
XLA Ops:
  0.6 2.3 %shard_map.86 = (bf16[8,144,128]{2,1,0:T(8,128)(2,1)S(1)}, s32[1,1024]{1,0:T(1,128)S(1)}, f32[1,1024]{1,0:T(1,128)S(1)}, f32[1,32,128]{2,1,0:T(8,128)S(1)}, bf16[1024,128]{1,0:T(8,128)(2,1)S(1)}) custom-call(s32[1,1024]{1,0:T(1,128)} %bitcast.10, s32[8,128]{1,0:T(8,128)} %bitcast.11, bf16[1024,128]{1,0:T(8,128)(2,1)} %rec_hbm.1), custom_call_target="tpu_custom_call" | custom-call | flops 268435456 | bytes 270336 | tf_op jit(solution)/shard_map/pallas_call | solution.py:26
  4.7 5.0 %collective-permute-start.1 = (bf16[272,128]{1,0:T(8,128)(2,1)S(1)}, bf16[272,128]{1,0:T(8,128)(2,1)S(1)}, u32[]{:S(2)}, u32[]{:S(2)}) collective-permute-start(bf16[272,128]{1,0:T(8,128)(2,1)S(1)} %get-tuple-element.44), channel_id=1, source_target_pairs={{0,10},{1,11},{2,8},{3,9},{4,14},{5,15},{6,12},{7,13},{8,2},{9,3},... | collective-permute-start | bytes 208904 | tf_op jit(solution)/shard_map/ppermute | solution.py:387
  9.7 1.5 %collective-permute-start.2 = (bf16[272,128]{1,0:T(8,128)(2,1)S(1)}, bf16[272,128]{1,0:T(8,128)(2,1)S(1)}, u32[]{:S(2)}, u32[]{:S(2)}) collective-permute-start(bf16[272,128]{1,0:T(8,128)(2,1)S(1)} %get-tuple-element.45), channel_id=1, source_target_pairs={{0,6},{1,7},{2,4},{3,5},{4,10},{5,11},{6,8},{7,9},{8,14},{9,15},{1... | collective-permute-start | bytes 208904 | tf_op jit(solution)/shard_map/ppermute | solution.py:387
  11.2 3.2 %collective-permute-start.3 = (bf16[272,128]{1,0:T(8,128)(2,1)S(1)}, bf16[272,128]{1,0:T(8,128)(2,1)S(1)}, u32[]{:S(2)}, u32[]{:S(2)}) collective-permute-start(bf16[272,128]{1,0:T(8,128)(2,1)S(1)} %get-tuple-element.46), channel_id=1, source_target_pairs={{0,14},{1,15},{2,12},{3,13},{4,2},{5,3},{6,0},{7,1},{8,6},{9,7},{1... | collective-permute-start | bytes 208904 | tf_op jit(solution)/shard_map/ppermute | solution.py:387
  15.5 1.6 %collective-permute-done.2.refs_2_ = bf16[272,128]{1,0:T(8,128)(2,1)S(1)} collective-permute-done((bf16[272,128]{1,0:T(8,128)(2,1)S(1)}, bf16[272,128]{1,0:T(8,128)(2,1)S(1)}, u32[]{:S(2)}, u32[]{:S(2)}) %collective-permute-start.2) | collective-permute-done | bytes 69664 | tf_op jit(solution)/shard_map/ppermute | solution.py:387
  17.1 1.6 %collective-permute-start.7 = (bf16[272,128]{1,0:T(8,128)(2,1)S(1)}, bf16[272,128]{1,0:T(8,128)(2,1)S(1)}, u32[]{:S(2)}, u32[]{:S(2)}) collective-permute-start(bf16[272,128]{1,0:T(8,128)(2,1)S(1)} %get-tuple-element.50), channel_id=1, source_target_pairs={{0,12},{1,13},{2,14},{3,15},{4,0},{5,1},{6,2},{7,3},{8,4},{9,5},{1... | collective-permute-start | bytes 208904 | tf_op jit(solution)/shard_map/ppermute | solution.py:387
  18.7 1.8 %shard_map.89.refs_4_.sum_ref = f32[3072,128]{1,0:T(8,128)S(1)} custom-call(bf16[272,128]{1,0:T(8,128)(2,1)S(1)} %get-tuple-element.43.refs_0_, bf16[272,128]{1,0:T(8,128)(2,1)S(1)} %collective-permute-done.1.refs_1_, bf16[272,128]{1,0:T(8,128)(2,1)S(1)} %collective-permute-done.2.refs_2_, bf16[272,128]{1,0:T(8,128)(2,1)S(1)} %collective-permute-done.3.refs_3_), custom_call_target="tpu_custom_call" | custom-call | flops 805306368 | bytes 278528 | tf_op jit(solution)/shard_map/pallas_call | solution.py:26
  20.6 1.4 %collective-permute-done.5.refs_1_ = bf16[272,128]{1,0:T(8,128)(2,1)S(1)} collective-permute-done((bf16[272,128]{1,0:T(8,128)(2,1)S(1)}, bf16[272,128]{1,0:T(8,128)(2,1)S(1)}, u32[]{:S(2)}, u32[]{:S(2)}) %collective-permute-start.5) | collective-permute-done | bytes 69664 | tf_op jit(solution)/shard_map/ppermute | solution.py:387
  24.2 2.0 %shard_map.92 = (bf16[3072,128]{1,0:T(8,128)(2,1)S(1)}, bf16[1536,128]{1,0:T(8,128)(2,1)S(1)}) custom-call(f32[3072,128]{1,0:T(8,128)S(1)} %shard_map.89.refs_4_.sum_ref, f32[1,1024]{1,0:T(1,128)S(1)} %get-tuple-element.51.slots_ref, bf16[1024,128]{1,0:T(8,128)(2,1)S(1)} %get-tuple-element.52.records_ref, bf16[768,128]{1,0:T(8,128)(2,1)S(1)} %shard_map.91.near_ref, ...), custom_call_target="tpu_custom_call" | custom-call | flops 402653184 | bytes 4002176 | tf_op jit(solution)/shard_map/pallas_call | solution.py:26
  26.3 1.7 %shard_map.93 = (bf16[768,128]{1,0:T(8,128)(2,1)S(1)}, f32[128,1024]{1,0:T(8,128)S(1)}) custom-call(bf16[3072,128]{1,0:T(8,128)(2,1)S(1)} %get-tuple-element.54.loads_ref, bf16[768,128]{1,0:T(8,128)(2,1)S(1)} %collective-permute-done.9.got_ref, bf16[32,3,96,96]{3,2,1,0:T(8,128)(2,1)S(1)} %copy-done, s32[3,32]{1,0:T(4,128)S(1)} %bitcast.7, ...), custom_call_target="tpu_custom_call" | custom-call | flops 603979776 | bytes 9437568 | tf_op jit(solution)/shard_map/pallas_call | solution.py:26
  28.0 1.3 %shard_map.94 = (bf16[1536,128]{1,0:T(8,128)(2,1)S(1)}, f32[64,1024]{1,0:T(8,128)S(1)}, f32[64,1024]{1,0:T(8,128)S(1)}) custom-call(bf16[3072,128]{1,0:T(8,128)(2,1)S(1)} %get-tuple-element.54.loads_ref, bf16[768,128]{1,0:T(8,128)(2,1)S(1)} %collective-permute-done.8.got_ref, bf16[32,3,96,96]{3,2,1,0:T(8,128)(2,1)S(1)} %copy-done, s32[3,32]{1,0:T(4,128)S(1)} %bitcast.8, ...), custom_call_target="tpu_custom_call" | custom-call | flops 201326592 | bytes 9765248 | tf_op jit(solution)/shard_map/pallas_call | solution.py:26
  29.4 3.6 %collective-permute-start.10 = (f32[64,1024]{1,0:T(8,128)S(1)}, f32[64,1024]{1,0:T(8,128)S(1)}, u32[]{:S(2)}, u32[]{:S(2)}) collective-permute-start(f32[64,1024]{1,0:T(8,128)S(1)} %get-tuple-element.59), channel_id=1, source_target_pairs={{0,1},{1,0},{2,3},{3,2},{4,5},{5,4},{6,7},{7,6},{8,9},{9,8},{10,11... | collective-permute-start | bytes 786440 | tf_op jit(solution)/shard_map/ppermute | solution.py:376
  33.0 1.2 %collective-permute-done.10.other_ref = f32[64,1024]{1,0:T(8,128)S(1)} collective-permute-done((f32[64,1024]{1,0:T(8,128)S(1)}, f32[64,1024]{1,0:T(8,128)S(1)}, u32[]{:S(2)}, u32[]{:S(2)}) %collective-permute-start.10) | collective-permute-done | bytes 262176 | tf_op jit(solution)/shard_map/ppermute | solution.py:376
  34.2 2.8 %collective-permute-start.11 = (bf16[32,1024]{1,0:T(8,128)(2,1)S(1)}, bf16[32,1024]{1,0:T(8,128)(2,1)S(1)}, u32[]{:S(2)}, u32[]{:S(2)}) collective-permute-start(bf16[32,1024]{1,0:T(8,128)(2,1)S(1)} %get-tuple-element.61), channel_id=1, source_target_pairs={{0,2},{1,3},{2,0},{3,1},{4,6},{5,7},{6,4},{7,5},{8,10},{9,11},{10,... | collective-permute-start | bytes 196616 | tf_op jit(solution)/shard_map/ppermute | solution.py:376
  37.0 2.4 %collective-permute-done.11.other_ref = bf16[32,1024]{1,0:T(8,128)(2,1)S(1)} collective-permute-done((bf16[32,1024]{1,0:T(8,128)(2,1)S(1)}, bf16[32,1024]{1,0:T(8,128)(2,1)S(1)}, u32[]{:S(2)}, u32[]{:S(2)}) %collective-permute-start.11) | collective-permute-done | bytes 65568 | tf_op jit(solution)/shard_map/ppermute | solution.py:376
  39.4 3.8 %collective-permute-start.14 = (bf16[32,1024]{1,0:T(8,128)(2,1)S(1)}, bf16[32,1024]{1,0:T(8,128)(2,1)S(1)}, u32[]{:S(2)}, u32[]{:S(2)}) collective-permute-start(bf16[32,1024]{1,0:T(8,128)(2,1)S(1)} %get-tuple-element.63), channel_id=1, source_target_pairs={{0,8},{1,9},{2,10},{3,11},{4,12},{5,13},{6,14},{7,15},{8,0},{9,1},... | collective-permute-start | bytes 196616 | tf_op jit(solution)/shard_map/ppermute | solution.py:387
  43.7 1.6 %collective-permute-start.12 = (bf16[32,1024]{1,0:T(8,128)(2,1)S(1)}, bf16[32,1024]{1,0:T(8,128)(2,1)S(1)}, u32[]{:S(2)}, u32[]{:S(2)}) collective-permute-start(bf16[32,1024]{1,0:T(8,128)(2,1)S(1)} %get-tuple-element.63), channel_id=1, source_target_pairs={{0,4},{1,5},{2,6},{3,7},{4,8},{5,9},{6,10},{7,11},{8,12},{9,13},{1... | collective-permute-start | bytes 196616 | tf_op jit(solution)/shard_map/ppermute | solution.py:387
  45.3 1.3 %shard_map.97 = (bf16[1024,1024]{1,0:T(8,128)(2,1)S(1)}, bf16[1024,1024]{1,0:T(8,128)(2,1)S(1)}) custom-call(f32[1024,1024]{1,0:T(8,128)S(1)} %copy-done.1), custom_call_target="tpu_custom_call" | custom-call | flops 4194304 | bytes 4194304 | tf_op jit(solution)/shard_map/pallas_call | solution.py:26
  46.9 1.4 %collective-permute-done.13.refs_1_ = bf16[32,1024]{1,0:T(8,128)(2,1)S(1)} collective-permute-done((bf16[32,1024]{1,0:T(8,128)(2,1)S(1)}, bf16[32,1024]{1,0:T(8,128)(2,1)S(1)}, u32[]{:S(2)}, u32[]{:S(2)}) %collective-permute-start.13) | collective-permute-done | bytes 65568 | tf_op jit(solution)/shard_map/ppermute | solution.py:387
  48.3 1.5 %collective-permute-done.12.refs_0_ = bf16[32,1024]{1,0:T(8,128)(2,1)S(1)} collective-permute-done((bf16[32,1024]{1,0:T(8,128)(2,1)S(1)}, bf16[32,1024]{1,0:T(8,128)(2,1)S(1)}, u32[]{:S(2)}, u32[]{:S(2)}) %collective-permute-start.12) | collective-permute-done | bytes 65568 | tf_op jit(solution)/shard_map/ppermute | solution.py:387
  50.6 1.3 %collective-permute-start.15 = (bf16[32,1024]{1,0:T(8,128)(2,1)S(1)}, bf16[32,1024]{1,0:T(8,128)(2,1)S(1)}, u32[]{:S(2)}, u32[]{:S(2)}) collective-permute-start(bf16[32,1024]{1,0:T(8,128)(2,1)S(1)} %shard_map.98.own_ref), channel_id=1, source_target_pairs={{0,2},{1,3},{2,0},{3,1},{4,6},{5,7},{6,4},{7,5},{8,10},{9,11},{10,... | collective-permute-start | bytes 196616 | tf_op jit(solution)/shard_map/ppermute | solution.py:376
  51.9 2.0 %shard_map.99 = (bf16[1024,3072]{1,0:T(8,128)(2,1)S(1)}, bf16[128,3072]{1,0:T(8,128)(2,1)S(1)}) custom-call(bf16[3072,1024]{1,0:T(8,128)(2,1)S(1)} %bitcast.5, bf16[1536,128]{1,0:T(8,128)(2,1)S(1)} %get-tuple-element.55.mid_ref, bf16[1536,128]{1,0:T(8,128)(2,1)S(1)} %get-tuple-element.66.edge_ref), custom_call_target="tpu_custom_call" | custom-call | bytes 7077888 | tf_op jit(solution)/shard_map/pallas_call | solution.py:26
  55.2 0.9 %collective-permute-done.17.both_ref = bf16[32,1024]{1,0:T(8,128)(2,1)S(1)} collective-permute-done((bf16[32,1024]{1,0:T(8,128)(2,1)S(1)}, bf16[32,1024]{1,0:T(8,128)(2,1)S(1)}, u32[]{:S(2)}, u32[]{:S(2)}) %collective-permute-start.17) | collective-permute-done | bytes 65568 | tf_op jit(solution)/shard_map/ppermute | solution.py:376
  56.1 1.9 %shard_map.100 = (bf16[3072,128]{1,0:T(8,128)(2,1)}, f32[24,128]{1,0:T(8,128)}) custom-call(bf16[32,1024]{1,0:T(8,128)(2,1)S(1)} %shard_map.98.own_ref, bf16[32,1024]{1,0:T(8,128)(2,1)S(1)} %collective-permute-done.15.y_ref, bf16[32,1024]{1,0:T(8,128)(2,1)S(1)} %collective-permute-done.16.core_ref, bf16[32,1024]{1,0:T(8,128)(2,1)S(1)} %collective-permute-done.17.both_ref, ...), custom_call_target="tpu_custom_call" | custom-call | flops 805306368 | bytes 7340032 | tf_op jit(solution)/shard_map/pallas_call | solution.py:26
  (38 shorter events, 8.1 us)
Async XLA Ops:
  2.9 1.7 %collective-permute-start = (bf16[8,144,128]{2,1,0:T(8,128)(2,1)S(1)}, bf16[8,144,128]{2,1,0:T(8,128)(2,1)S(1)}, u32[]{:S(2)}, u32[]{:S(2)}) collective-permute-start(bf16[8,144,128]{2,1,0:T(8,128)(2,1)S(1)} %get-tuple-element.42), channel_id=1, source_target_pairs={{0,1},{1,0},{2,3},{3,2},{4,5},{5,4},{6,7},{7,6},{8,9},{9,8},{10,11... | collective-permute-start | bytes 884744 | tf_op jit(solution)/shard_map/ppermute | solution.py:376
  4.7 10.2 %collective-permute-start.1 = (bf16[272,128]{1,0:T(8,128)(2,1)S(1)}, bf16[272,128]{1,0:T(8,128)(2,1)S(1)}, u32[]{:S(2)}, u32[]{:S(2)}) collective-permute-start(bf16[272,128]{1,0:T(8,128)(2,1)S(1)} %get-tuple-element.44), channel_id=1, source_target_pairs={{0,10},{1,11},{2,8},{3,9},{4,14},{5,15},{6,12},{7,13},{8,2},{9,3},... | collective-permute-start | bytes 208904 | tf_op jit(solution)/shard_map/ppermute | solution.py:387
  9.7 7.5 %collective-permute-start.2 = (bf16[272,128]{1,0:T(8,128)(2,1)S(1)}, bf16[272,128]{1,0:T(8,128)(2,1)S(1)}, u32[]{:S(2)}, u32[]{:S(2)}) collective-permute-start(bf16[272,128]{1,0:T(8,128)(2,1)S(1)} %get-tuple-element.45), channel_id=1, source_target_pairs={{0,6},{1,7},{2,4},{3,5},{4,10},{5,11},{6,8},{7,9},{8,14},{9,15},{1... | collective-permute-start | bytes 208904 | tf_op jit(solution)/shard_map/ppermute | solution.py:387
  11.2 7.6 %collective-permute-start.3 = (bf16[272,128]{1,0:T(8,128)(2,1)S(1)}, bf16[272,128]{1,0:T(8,128)(2,1)S(1)}, u32[]{:S(2)}, u32[]{:S(2)}) collective-permute-start(bf16[272,128]{1,0:T(8,128)(2,1)S(1)} %get-tuple-element.46), channel_id=1, source_target_pairs={{0,14},{1,15},{2,12},{3,13},{4,2},{5,3},{6,0},{7,1},{8,6},{9,7},{1... | collective-permute-start | bytes 208904 | tf_op jit(solution)/shard_map/ppermute | solution.py:387
  14.4 6.2 %collective-permute-start.4 = (bf16[272,128]{1,0:T(8,128)(2,1)S(1)}, bf16[272,128]{1,0:T(8,128)(2,1)S(1)}, u32[]{:S(2)}, u32[]{:S(2)}) collective-permute-start(bf16[272,128]{1,0:T(8,128)(2,1)S(1)} %get-tuple-element.47), channel_id=1, source_target_pairs={{0,2},{1,3},{2,0},{3,1},{4,6},{5,7},{6,4},{7,5},{8,10},{9,11},{10,... | collective-permute-start | bytes 208904 | tf_op jit(solution)/shard_map/ppermute | solution.py:387
  14.9 7.1 %collective-permute-start.5 = (bf16[272,128]{1,0:T(8,128)(2,1)S(1)}, bf16[272,128]{1,0:T(8,128)(2,1)S(1)}, u32[]{:S(2)}, u32[]{:S(2)}) collective-permute-start(bf16[272,128]{1,0:T(8,128)(2,1)S(1)} %get-tuple-element.48), channel_id=1, source_target_pairs={{0,8},{1,9},{2,10},{3,11},{4,12},{5,13},{6,14},{7,15},{8,0},{9,1},... | collective-permute-start | bytes 208904 | tf_op jit(solution)/shard_map/ppermute | solution.py:387
  14.9 7.1 %collective-permute-start.6 = (bf16[272,128]{1,0:T(8,128)(2,1)S(1)}, bf16[272,128]{1,0:T(8,128)(2,1)S(1)}, u32[]{:S(2)}, u32[]{:S(2)}) collective-permute-start(bf16[272,128]{1,0:T(8,128)(2,1)S(1)} %get-tuple-element.49), channel_id=1, source_target_pairs={{0,4},{1,5},{2,6},{3,7},{4,8},{5,9},{6,10},{7,11},{8,12},{9,13},{1... | collective-permute-start | bytes 208904 | tf_op jit(solution)/shard_map/ppermute | solution.py:387
  17.1 5.1 %collective-permute-start.7 = (bf16[272,128]{1,0:T(8,128)(2,1)S(1)}, bf16[272,128]{1,0:T(8,128)(2,1)S(1)}, u32[]{:S(2)}, u32[]{:S(2)}) collective-permute-start(bf16[272,128]{1,0:T(8,128)(2,1)S(1)} %get-tuple-element.50), channel_id=1, source_target_pairs={{0,12},{1,13},{2,14},{3,15},{4,0},{5,1},{6,2},{7,3},{8,4},{9,5},{1... | collective-permute-start | bytes 208904 | tf_op jit(solution)/shard_map/ppermute | solution.py:387
  18.7 7.5 %slice-start = ((s8[6291456]{0:T(1024)(128)(4,1)}), s8[4194304]{0:T(1024)(128)(4,1)S(1)}, s32[]{:S(2)}) async-start(s8[6291456]{0:T(1024)(128)(4,1)} %bitcast.4), calls=%async_computation | async-start | bytes 8388608
  20.5 3.6 %copy-start.2 = (s32[32,3]{0,1:T(4,128)S(1)}, s32[32,3]{0,1:T(4,128)}, u32[]{:S(2)}) copy-start(s32[32,3]{0,1:T(4,128)} %param.11) | copy-start | bytes 1156
  20.5 5.7 %slice-start.1 = ((s8[6291456]{0:T(1024)(128)(4,1)}), s8[2097152]{0:T(1024)(128)(4,1)S(1)}, s32[]{:S(2)}) async-start(s8[6291456]{0:T(1024)(128)(4,1)} %bitcast.4), calls=%async_computation.1 | async-start | bytes 4194304
  22.3 1.9 %copy-start = (bf16[32,3,96,96]{3,2,1,0:T(8,128)(2,1)S(1)}, bf16[32,3,96,96]{3,2,1,0:T(8,128)(2,1)}, u32[]{:S(2)}) copy-start(bf16[32,3,96,96]{3,2,1,0:T(8,128)(2,1)} %stiff_ref.5) | copy-start | bytes 5308420
  23.4 2.8 %collective-permute-start.9 = (bf16[768,128]{1,0:T(8,128)(2,1)S(1)}, bf16[768,128]{1,0:T(8,128)(2,1)S(1)}, u32[]{:S(2)}, u32[]{:S(2)}) collective-permute-start(bf16[768,128]{1,0:T(8,128)(2,1)S(1)} %shard_map.91.near_ref), channel_id=1, source_target_pairs={{0,1},{1,0},{2,3},{3,2},{4,5},{5,4},{6,7},{7,6},{8,9},{9,8},{10,11... | collective-permute-start | bytes 589832 | tf_op jit(solution)/shard_map/ppermute | solution.py:376
  23.5 4.5 %collective-permute-start.8 = (bf16[768,128]{1,0:T(8,128)(2,1)S(1)}, bf16[768,128]{1,0:T(8,128)(2,1)S(1)}, u32[]{:S(2)}, u32[]{:S(2)}) collective-permute-start(bf16[768,128]{1,0:T(8,128)(2,1)S(1)} %get-tuple-element.53.far_ref), channel_id=1, source_target_pairs={{1,2},{3,4},{5,6},{7,8},{9,10},{11,12},{13,14},{2,1},{4,3},{6,5},{... | collective-permute-start | bytes 589832 | tf_op jit(solution)/shard_map/ppermute | solution.py:380
  28.0 17.3 %copy-start.1 = (f32[1024,1024]{1,0:T(8,128)S(1)}, f32[1024,1024]{1,0:T(8,128)}, u32[]{:S(2)}) copy-start(f32[1024,1024]{1,0:T(8,128)} %a_ref.1) | copy-start | bytes 12582916
  29.4 4.7 %collective-permute-start.10 = (f32[64,1024]{1,0:T(8,128)S(1)}, f32[64,1024]{1,0:T(8,128)S(1)}, u32[]{:S(2)}, u32[]{:S(2)}) collective-permute-start(f32[64,1024]{1,0:T(8,128)S(1)} %get-tuple-element.59), channel_id=1, source_target_pairs={{0,1},{1,0},{2,3},{3,2},{4,5},{5,4},{6,7},{7,6},{8,9},{9,8},{10,11... | collective-permute-start | bytes 786440 | tf_op jit(solution)/shard_map/ppermute | solution.py:376
  34.2 5.2 %collective-permute-start.11 = (bf16[32,1024]{1,0:T(8,128)(2,1)S(1)}, bf16[32,1024]{1,0:T(8,128)(2,1)S(1)}, u32[]{:S(2)}, u32[]{:S(2)}) collective-permute-start(bf16[32,1024]{1,0:T(8,128)(2,1)S(1)} %get-tuple-element.61), channel_id=1, source_target_pairs={{0,2},{1,3},{2,0},{3,1},{4,6},{5,7},{6,4},{7,5},{8,10},{9,11},{10,... | collective-permute-start | bytes 196616 | tf_op jit(solution)/shard_map/ppermute | solution.py:376
  39.4 7.5 %collective-permute-start.14 = (bf16[32,1024]{1,0:T(8,128)(2,1)S(1)}, bf16[32,1024]{1,0:T(8,128)(2,1)S(1)}, u32[]{:S(2)}, u32[]{:S(2)}) collective-permute-start(bf16[32,1024]{1,0:T(8,128)(2,1)S(1)} %get-tuple-element.63), channel_id=1, source_target_pairs={{0,8},{1,9},{2,10},{3,11},{4,12},{5,13},{6,14},{7,15},{8,0},{9,1},... | collective-permute-start | bytes 196616 | tf_op jit(solution)/shard_map/ppermute | solution.py:387
  43.2 5.0 %collective-permute-start.13 = (bf16[32,1024]{1,0:T(8,128)(2,1)S(1)}, bf16[32,1024]{1,0:T(8,128)(2,1)S(1)}, u32[]{:S(2)}, u32[]{:S(2)}) collective-permute-start(bf16[32,1024]{1,0:T(8,128)(2,1)S(1)} %get-tuple-element.63), channel_id=1, source_target_pairs={{0,12},{1,13},{2,14},{3,15},{4,0},{5,1},{6,2},{7,3},{8,4},{9,5},{1... | collective-permute-start | bytes 196616 | tf_op jit(solution)/shard_map/ppermute | solution.py:387
  43.7 6.1 %collective-permute-start.12 = (bf16[32,1024]{1,0:T(8,128)(2,1)S(1)}, bf16[32,1024]{1,0:T(8,128)(2,1)S(1)}, u32[]{:S(2)}, u32[]{:S(2)}) collective-permute-start(bf16[32,1024]{1,0:T(8,128)(2,1)S(1)} %get-tuple-element.63), channel_id=1, source_target_pairs={{0,4},{1,5},{2,6},{3,7},{4,8},{5,9},{6,10},{7,11},{8,12},{9,13},{1... | collective-permute-start | bytes 196616 | tf_op jit(solution)/shard_map/ppermute | solution.py:387
  50.6 4.3 %collective-permute-start.15 = (bf16[32,1024]{1,0:T(8,128)(2,1)S(1)}, bf16[32,1024]{1,0:T(8,128)(2,1)S(1)}, u32[]{:S(2)}, u32[]{:S(2)}) collective-permute-start(bf16[32,1024]{1,0:T(8,128)(2,1)S(1)} %shard_map.98.own_ref), channel_id=1, source_target_pairs={{0,2},{1,3},{2,0},{3,1},{4,6},{5,7},{6,4},{7,5},{8,10},{9,11},{10,... | collective-permute-start | bytes 196616 | tf_op jit(solution)/shard_map/ppermute | solution.py:376
  53.9 1.3 %collective-permute-start.16 = (bf16[32,1024]{1,0:T(8,128)(2,1)S(1)}, bf16[32,1024]{1,0:T(8,128)(2,1)S(1)}, u32[]{:S(2)}, u32[]{:S(2)}) collective-permute-start(bf16[32,1024]{1,0:T(8,128)(2,1)S(1)} %shard_map.98.own_ref), channel_id=1, source_target_pairs={{0,1},{1,0},{2,3},{3,2},{4,5},{5,4},{6,7},{7,6},{8,9},{9,8},{10,11... | collective-permute-start | bytes 196616 | tf_op jit(solution)/shard_map/ppermute | solution.py:376
  54.9 1.3 %collective-permute-start.17 = (bf16[32,1024]{1,0:T(8,128)(2,1)S(1)}, bf16[32,1024]{1,0:T(8,128)(2,1)S(1)}, u32[]{:S(2)}, u32[]{:S(2)}) collective-permute-start(bf16[32,1024]{1,0:T(8,128)(2,1)S(1)} %collective-permute-done.15.y_ref), channel_id=1, source_target_pairs={{0,1},{1,0},{2,3},{3,2},{4,5},{5,4},{6,7},{7,6},{8,9},{9,8},{10,11... | collective-permute-start | bytes 196616 | tf_op jit(solution)/shard_map/ppermute | solution.py:376

commit v6 on v5

--- a/solution.py
+++ b/solution.py
@@ -488,7 +488,7 @@
         add_kernel, (shape((quarter, mode_count), F32), piece), keep, swap(send, 2)
     )
     groups = chips // 2
-    steps = sorted(range(1, groups), key=lambda k: min(k, groups - k))
+    steps = range(groups - 1, 0, -1)
     others = [turn(send, k, 0) for k in steps]
     a_high, a_low = call(
         split_kernel,

time: 58.4 us -> 56.8 us (0.973)
  waiting for transfers between devices: 12.7 us -> 10.1 us
  starting transfers between devices: 27.3 us -> 28.4 us
    ppermute x10, waiting for transfers between devices: 6.49 us -> 4.02 us  [turn(): return lax.ppermute(array, 'elem', pairs)]
    ppermute x10, starting transfers between devices: 18.3 us -> 19.2 us  [turn(): return lax.ppermute(array, 'elem', pairs)]
  transfers between devices with their start and end apart: 18 -> 18, of which waited for: 12 -> 11; matrix products, arithmetic and copies ran while one was open for 0% -> 0% of each run, Pallas kernels for 16% -> 17%
where the time goes in v6:
time: 56.8 us; the launch traced here: 56.6 us
  starting transfers between devices  28.4 us (50%)
  Pallas kernels  17.2 us (30%)
  waiting for transfers between devices  10.1 us (18%)
  between operations  1 us (2%)
    ppermute x10, starting transfers between devices, turn(): return lax.ppermute(array, 'elem', pairs)  19.2 us
    pallas_call x15, Pallas kernels, call(): pl.pallas_call(kernel, out_shape=out_shape, in_specs=[pl.BlockSpec(memory...  17.2 us
    ppermute x7, starting transfers between devices, swap(): return lax.ppermute(array, 'elem', [(i, i ^ mask) for i in range(owners)])  8.49 us
    ppermute x7, waiting for transfers between devices, swap(): return lax.ppermute(array, 'elem', [(i, i ^ mask) for i in range(owners)])  6.05 us
    ppermute x10, waiting for transfers between devices, turn(): return lax.ppermute(array, 'elem', pairs)  4.02 us
  transfers between devices with their start and end apart: 18, of which 11 were waited for; matrix products, arithmetic and copies ran while one was open for 0% of the time, Pallas kernels for 17%

profile of v6, /device:TPU:0, one launch (start us, length us, event | category | flops | bytes accessed | tf_op | source)
XLA Modules:
  0.0 56.6 jit_solution(13738569034986973793)
XLA Ops:
  0.6 2.3 %shard_map.86 = (bf16[8,144,128]{2,1,0:T(8,128)(2,1)S(1)}, s32[1,1024]{1,0:T(1,128)S(1)}, f32[1,1024]{1,0:T(1,128)S(1)}, f32[1,32,128]{2,1,0:T(8,128)S(1)}, bf16[1024,128]{1,0:T(8,128)(2,1)S(1)}) custom-call(s32[1,1024]{1,0:T(1,128)} %bitcast.10, s32[8,128]{1,0:T(8,128)} %bitcast.11, bf16[1024,128]{1,0:T(8,128)(2,1)} %rec_hbm.1), custom_call_target="tpu_custom_call" | custom-call | flops 268435456 | bytes 270336 | tf_op jit(solution)/shard_map/pallas_call | solution.py:26
  4.7 5.0 %collective-permute-start.1 = (bf16[272,128]{1,0:T(8,128)(2,1)S(1)}, bf16[272,128]{1,0:T(8,128)(2,1)S(1)}, u32[]{:S(2)}, u32[]{:S(2)}) collective-permute-start(bf16[272,128]{1,0:T(8,128)(2,1)S(1)} %get-tuple-element.44), channel_id=1, source_target_pairs={{0,10},{1,11},{2,8},{3,9},{4,14},{5,15},{6,12},{7,13},{8,2},{9,3},... | collective-permute-start | bytes 208904 | tf_op jit(solution)/shard_map/ppermute | solution.py:387
  9.7 1.5 %collective-permute-start.2 = (bf16[272,128]{1,0:T(8,128)(2,1)S(1)}, bf16[272,128]{1,0:T(8,128)(2,1)S(1)}, u32[]{:S(2)}, u32[]{:S(2)}) collective-permute-start(bf16[272,128]{1,0:T(8,128)(2,1)S(1)} %get-tuple-element.45), channel_id=1, source_target_pairs={{0,6},{1,7},{2,4},{3,5},{4,10},{5,11},{6,8},{7,9},{8,14},{9,15},{1... | collective-permute-start | bytes 208904 | tf_op jit(solution)/shard_map/ppermute | solution.py:387
  11.2 3.2 %collective-permute-start.3 = (bf16[272,128]{1,0:T(8,128)(2,1)S(1)}, bf16[272,128]{1,0:T(8,128)(2,1)S(1)}, u32[]{:S(2)}, u32[]{:S(2)}) collective-permute-start(bf16[272,128]{1,0:T(8,128)(2,1)S(1)} %get-tuple-element.46), channel_id=1, source_target_pairs={{0,14},{1,15},{2,12},{3,13},{4,2},{5,3},{6,0},{7,1},{8,6},{9,7},{1... | collective-permute-start | bytes 208904 | tf_op jit(solution)/shard_map/ppermute | solution.py:387
  15.5 1.6 %collective-permute-done.2.refs_2_ = bf16[272,128]{1,0:T(8,128)(2,1)S(1)} collective-permute-done((bf16[272,128]{1,0:T(8,128)(2,1)S(1)}, bf16[272,128]{1,0:T(8,128)(2,1)S(1)}, u32[]{:S(2)}, u32[]{:S(2)}) %collective-permute-start.2) | collective-permute-done | bytes 69664 | tf_op jit(solution)/shard_map/ppermute | solution.py:387
  17.1 1.6 %collective-permute-start.7 = (bf16[272,128]{1,0:T(8,128)(2,1)S(1)}, bf16[272,128]{1,0:T(8,128)(2,1)S(1)}, u32[]{:S(2)}, u32[]{:S(2)}) collective-permute-start(bf16[272,128]{1,0:T(8,128)(2,1)S(1)} %get-tuple-element.50), channel_id=1, source_target_pairs={{0,12},{1,13},{2,14},{3,15},{4,0},{5,1},{6,2},{7,3},{8,4},{9,5},{1... | collective-permute-start | bytes 208904 | tf_op jit(solution)/shard_map/ppermute | solution.py:387
  18.7 1.8 %shard_map.89.refs_4_.sum_ref = f32[3072,128]{1,0:T(8,128)S(1)} custom-call(bf16[272,128]{1,0:T(8,128)(2,1)S(1)} %get-tuple-element.43.refs_0_, bf16[272,128]{1,0:T(8,128)(2,1)S(1)} %collective-permute-done.1.refs_1_, bf16[272,128]{1,0:T(8,128)(2,1)S(1)} %collective-permute-done.2.refs_2_, bf16[272,128]{1,0:T(8,128)(2,1)S(1)} %collective-permute-done.3.refs_3_), custom_call_target="tpu_custom_call" | custom-call | flops 805306368 | bytes 278528 | tf_op jit(solution)/shard_map/pallas_call | solution.py:26
  20.6 1.4 %collective-permute-done.5.refs_1_ = bf16[272,128]{1,0:T(8,128)(2,1)S(1)} collective-permute-done((bf16[272,128]{1,0:T(8,128)(2,1)S(1)}, bf16[272,128]{1,0:T(8,128)(2,1)S(1)}, u32[]{:S(2)}, u32[]{:S(2)}) %collective-permute-start.5) | collective-permute-done | bytes 69664 | tf_op jit(solution)/shard_map/ppermute | solution.py:387
  24.2 2.0 %shard_map.92 = (bf16[3072,128]{1,0:T(8,128)(2,1)S(1)}, bf16[1536,128]{1,0:T(8,128)(2,1)S(1)}) custom-call(f32[3072,128]{1,0:T(8,128)S(1)} %shard_map.89.refs_4_.sum_ref, f32[1,1024]{1,0:T(1,128)S(1)} %get-tuple-element.51.slots_ref, bf16[1024,128]{1,0:T(8,128)(2,1)S(1)} %get-tuple-element.52.records_ref, bf16[768,128]{1,0:T(8,128)(2,1)S(1)} %shard_map.91.near_ref, ...), custom_call_target="tpu_custom_call" | custom-call | flops 402653184 | bytes 4002176 | tf_op jit(solution)/shard_map/pallas_call | solution.py:26
  26.3 1.7 %shard_map.93 = (bf16[768,128]{1,0:T(8,128)(2,1)S(1)}, f32[128,1024]{1,0:T(8,128)S(1)}) custom-call(bf16[3072,128]{1,0:T(8,128)(2,1)S(1)} %get-tuple-element.54.loads_ref, bf16[768,128]{1,0:T(8,128)(2,1)S(1)} %collective-permute-done.9.got_ref, bf16[32,3,96,96]{3,2,1,0:T(8,128)(2,1)S(1)} %copy-done, s32[3,32]{1,0:T(4,128)S(1)} %bitcast.7, ...), custom_call_target="tpu_custom_call" | custom-call | flops 603979776 | bytes 9437568 | tf_op jit(solution)/shard_map/pallas_call | solution.py:26
  28.0 1.3 %shard_map.94 = (bf16[1536,128]{1,0:T(8,128)(2,1)S(1)}, f32[64,1024]{1,0:T(8,128)S(1)}, f32[64,1024]{1,0:T(8,128)S(1)}) custom-call(bf16[3072,128]{1,0:T(8,128)(2,1)S(1)} %get-tuple-element.54.loads_ref, bf16[768,128]{1,0:T(8,128)(2,1)S(1)} %collective-permute-done.8.got_ref, bf16[32,3,96,96]{3,2,1,0:T(8,128)(2,1)S(1)} %copy-done, s32[3,32]{1,0:T(4,128)S(1)} %bitcast.8, ...), custom_call_target="tpu_custom_call" | custom-call | flops 201326592 | bytes 9765248 | tf_op jit(solution)/shard_map/pallas_call | solution.py:26
  29.4 3.6 %collective-permute-start.10 = (f32[64,1024]{1,0:T(8,128)S(1)}, f32[64,1024]{1,0:T(8,128)S(1)}, u32[]{:S(2)}, u32[]{:S(2)}) collective-permute-start(f32[64,1024]{1,0:T(8,128)S(1)} %get-tuple-element.59), channel_id=1, source_target_pairs={{0,1},{1,0},{2,3},{3,2},{4,5},{5,4},{6,7},{7,6},{8,9},{9,8},{10,11... | collective-permute-start | bytes 786440 | tf_op jit(solution)/shard_map/ppermute | solution.py:376
  33.0 1.2 %collective-permute-done.10.other_ref = f32[64,1024]{1,0:T(8,128)S(1)} collective-permute-done((f32[64,1024]{1,0:T(8,128)S(1)}, f32[64,1024]{1,0:T(8,128)S(1)}, u32[]{:S(2)}, u32[]{:S(2)}) %collective-permute-start.10) | collective-permute-done | bytes 262176 | tf_op jit(solution)/shard_map/ppermute | solution.py:376
  34.2 2.8 %collective-permute-start.11 = (bf16[32,1024]{1,0:T(8,128)(2,1)S(1)}, bf16[32,1024]{1,0:T(8,128)(2,1)S(1)}, u32[]{:S(2)}, u32[]{:S(2)}) collective-permute-start(bf16[32,1024]{1,0:T(8,128)(2,1)S(1)} %get-tuple-element.61), channel_id=1, source_target_pairs={{0,2},{1,3},{2,0},{3,1},{4,6},{5,7},{6,4},{7,5},{8,10},{9,11},{10,... | collective-permute-start | bytes 196616 | tf_op jit(solution)/shard_map/ppermute | solution.py:376
  37.0 2.4 %collective-permute-done.11.other_ref = bf16[32,1024]{1,0:T(8,128)(2,1)S(1)} collective-permute-done((bf16[32,1024]{1,0:T(8,128)(2,1)S(1)}, bf16[32,1024]{1,0:T(8,128)(2,1)S(1)}, u32[]{:S(2)}, u32[]{:S(2)}) %collective-permute-start.11) | collective-permute-done | bytes 65568 | tf_op jit(solution)/shard_map/ppermute | solution.py:376
  39.4 1.9 %collective-permute-start.14 = (bf16[32,1024]{1,0:T(8,128)(2,1)S(1)}, bf16[32,1024]{1,0:T(8,128)(2,1)S(1)}, u32[]{:S(2)}, u32[]{:S(2)}) collective-permute-start(bf16[32,1024]{1,0:T(8,128)(2,1)S(1)} %get-tuple-element.63), channel_id=1, source_target_pairs={{0,4},{1,5},{2,6},{3,7},{4,8},{5,9},{6,10},{7,11},{8,12},{9,13},{1... | collective-permute-start | bytes 196616 | tf_op jit(solution)/shard_map/ppermute | solution.py:387
  41.3 2.2 %collective-permute-start.13 = (bf16[32,1024]{1,0:T(8,128)(2,1)S(1)}, bf16[32,1024]{1,0:T(8,128)(2,1)S(1)}, u32[]{:S(2)}, u32[]{:S(2)}) collective-permute-start(bf16[32,1024]{1,0:T(8,128)(2,1)S(1)} %get-tuple-element.63), channel_id=1, source_target_pairs={{0,8},{1,9},{2,10},{3,11},{4,12},{5,13},{6,14},{7,15},{8,0},{9,1},... | collective-permute-start | bytes 196616 | tf_op jit(solution)/shard_map/ppermute | solution.py:387
  43.5 2.6 %collective-permute-start.12 = (bf16[32,1024]{1,0:T(8,128)(2,1)S(1)}, bf16[32,1024]{1,0:T(8,128)(2,1)S(1)}, u32[]{:S(2)}, u32[]{:S(2)}) collective-permute-start(bf16[32,1024]{1,0:T(8,128)(2,1)S(1)} %get-tuple-element.63), channel_id=1, source_target_pairs={{0,12},{1,13},{2,14},{3,15},{4,0},{5,1},{6,2},{7,3},{8,4},{9,5},{1... | collective-permute-start | bytes 196616 | tf_op jit(solution)/shard_map/ppermute | solution.py:387
  46.2 1.3 %shard_map.97 = (bf16[1024,1024]{1,0:T(8,128)(2,1)S(1)}, bf16[1024,1024]{1,0:T(8,128)(2,1)S(1)}) custom-call(f32[1024,1024]{1,0:T(8,128)S(1)} %copy-done.1), custom_call_target="tpu_custom_call" | custom-call | flops 4194304 | bytes 4194304 | tf_op jit(solution)/shard_map/pallas_call | solution.py:26
  48.2 0.8 %shard_map.98.own_ref = bf16[32,1024]{1,0:T(8,128)(2,1)S(1)} custom-call(f32[32,1024]{1,0:T(8,128)S(1)} %get-tuple-element.62.mine_ref, bf16[32,1024]{1,0:T(8,128)(2,1)S(1)} %collective-permute-done.12.refs_0_, bf16[32,1024]{1,0:T(8,128)(2,1)S(1)} %collective-permute-done.13.refs_1_, bf16[32,1024]{1,0:T(8,128)(2,1)S(1)} %collective-permute-done.14.refs_2_, ...), custom_call_target="tpu_custom_call" | custom-call | flops 201326592 | bytes 4521984 | tf_op jit(solution)/shard_map/pallas_call | solution.py:26
  49.0 1.4 %collective-permute-start.15 = (bf16[32,1024]{1,0:T(8,128)(2,1)S(1)}, bf16[32,1024]{1,0:T(8,128)(2,1)S(1)}, u32[]{:S(2)}, u32[]{:S(2)}) collective-permute-start(bf16[32,1024]{1,0:T(8,128)(2,1)S(1)} %shard_map.98.own_ref), channel_id=1, source_target_pairs={{0,2},{1,3},{2,0},{3,1},{4,6},{5,7},{6,4},{7,5},{8,10},{9,11},{10,... | collective-permute-start | bytes 196616 | tf_op jit(solution)/shard_map/ppermute | solution.py:376
  50.5 2.0 %shard_map.99 = (bf16[1024,3072]{1,0:T(8,128)(2,1)S(1)}, bf16[128,3072]{1,0:T(8,128)(2,1)S(1)}) custom-call(bf16[3072,1024]{1,0:T(8,128)(2,1)S(1)} %bitcast.5, bf16[1536,128]{1,0:T(8,128)(2,1)S(1)} %get-tuple-element.55.mid_ref, bf16[1536,128]{1,0:T(8,128)(2,1)S(1)} %get-tuple-element.66.edge_ref), custom_call_target="tpu_custom_call" | custom-call | bytes 7077888 | tf_op jit(solution)/shard_map/pallas_call | solution.py:26
  53.8 0.8 %collective-permute-done.17.both_ref = bf16[32,1024]{1,0:T(8,128)(2,1)S(1)} collective-permute-done((bf16[32,1024]{1,0:T(8,128)(2,1)S(1)}, bf16[32,1024]{1,0:T(8,128)(2,1)S(1)}, u32[]{:S(2)}, u32[]{:S(2)}) %collective-permute-start.17) | collective-permute-done | bytes 65568 | tf_op jit(solution)/shard_map/ppermute | solution.py:376
  54.5 1.9 %shard_map.100 = (bf16[3072,128]{1,0:T(8,128)(2,1)}, f32[24,128]{1,0:T(8,128)}) custom-call(bf16[32,1024]{1,0:T(8,128)(2,1)S(1)} %shard_map.98.own_ref, bf16[32,1024]{1,0:T(8,128)(2,1)S(1)} %collective-permute-done.15.y_ref, bf16[32,1024]{1,0:T(8,128)(2,1)S(1)} %collective-permute-done.16.core_ref, bf16[32,1024]{1,0:T(8,128)(2,1)S(1)} %collective-permute-done.17.both_ref, ...), custom_call_target="tpu_custom_call" | custom-call | flops 805306368 | bytes 7340032 | tf_op jit(solution)/shard_map/pallas_call | solution.py:26
  (38 shorter events, 7.2 us)
Async XLA Ops:
  2.9 1.7 %collective-permute-start = (bf16[8,144,128]{2,1,0:T(8,128)(2,1)S(1)}, bf16[8,144,128]{2,1,0:T(8,128)(2,1)S(1)}, u32[]{:S(2)}, u32[]{:S(2)}) collective-permute-start(bf16[8,144,128]{2,1,0:T(8,128)(2,1)S(1)} %get-tuple-element.42), channel_id=1, source_target_pairs={{0,1},{1,0},{2,3},{3,2},{4,5},{5,4},{6,7},{7,6},{8,9},{9,8},{10,11... | collective-permute-start | bytes 884744 | tf_op jit(solution)/shard_map/ppermute | solution.py:376
  4.7 10.2 %collective-permute-start.1 = (bf16[272,128]{1,0:T(8,128)(2,1)S(1)}, bf16[272,128]{1,0:T(8,128)(2,1)S(1)}, u32[]{:S(2)}, u32[]{:S(2)}) collective-permute-start(bf16[272,128]{1,0:T(8,128)(2,1)S(1)} %get-tuple-element.44), channel_id=1, source_target_pairs={{0,10},{1,11},{2,8},{3,9},{4,14},{5,15},{6,12},{7,13},{8,2},{9,3},... | collective-permute-start | bytes 208904 | tf_op jit(solution)/shard_map/ppermute | solution.py:387
  9.7 7.5 %collective-permute-start.2 = (bf16[272,128]{1,0:T(8,128)(2,1)S(1)}, bf16[272,128]{1,0:T(8,128)(2,1)S(1)}, u32[]{:S(2)}, u32[]{:S(2)}) collective-permute-start(bf16[272,128]{1,0:T(8,128)(2,1)S(1)} %get-tuple-element.45), channel_id=1, source_target_pairs={{0,6},{1,7},{2,4},{3,5},{4,10},{5,11},{6,8},{7,9},{8,14},{9,15},{1... | collective-permute-start | bytes 208904 | tf_op jit(solution)/shard_map/ppermute | solution.py:387
  11.2 7.6 %collective-permute-start.3 = (bf16[272,128]{1,0:T(8,128)(2,1)S(1)}, bf16[272,128]{1,0:T(8,128)(2,1)S(1)}, u32[]{:S(2)}, u32[]{:S(2)}) collective-permute-start(bf16[272,128]{1,0:T(8,128)(2,1)S(1)} %get-tuple-element.46), channel_id=1, source_target_pairs={{0,14},{1,15},{2,12},{3,13},{4,2},{5,3},{6,0},{7,1},{8,6},{9,7},{1... | collective-permute-start | bytes 208904 | tf_op jit(solution)/shard_map/ppermute | solution.py:387
  14.4 6.2 %collective-permute-start.4 = (bf16[272,128]{1,0:T(8,128)(2,1)S(1)}, bf16[272,128]{1,0:T(8,128)(2,1)S(1)}, u32[]{:S(2)}, u32[]{:S(2)}) collective-permute-start(bf16[272,128]{1,0:T(8,128)(2,1)S(1)} %get-tuple-element.47), channel_id=1, source_target_pairs={{0,2},{1,3},{2,0},{3,1},{4,6},{5,7},{6,4},{7,5},{8,10},{9,11},{10,... | collective-permute-start | bytes 208904 | tf_op jit(solution)/shard_map/ppermute | solution.py:387
  14.9 7.1 %collective-permute-start.5 = (bf16[272,128]{1,0:T(8,128)(2,1)S(1)}, bf16[272,128]{1,0:T(8,128)(2,1)S(1)}, u32[]{:S(2)}, u32[]{:S(2)}) collective-permute-start(bf16[272,128]{1,0:T(8,128)(2,1)S(1)} %get-tuple-element.48), channel_id=1, source_target_pairs={{0,8},{1,9},{2,10},{3,11},{4,12},{5,13},{6,14},{7,15},{8,0},{9,1},... | collective-permute-start | bytes 208904 | tf_op jit(solution)/shard_map/ppermute | solution.py:387
  14.9 7.1 %collective-permute-start.6 = (bf16[272,128]{1,0:T(8,128)(2,1)S(1)}, bf16[272,128]{1,0:T(8,128)(2,1)S(1)}, u32[]{:S(2)}, u32[]{:S(2)}) collective-permute-start(bf16[272,128]{1,0:T(8,128)(2,1)S(1)} %get-tuple-element.49), channel_id=1, source_target_pairs={{0,4},{1,5},{2,6},{3,7},{4,8},{5,9},{6,10},{7,11},{8,12},{9,13},{1... | collective-permute-start | bytes 208904 | tf_op jit(solution)/shard_map/ppermute | solution.py:387
  17.1 5.1 %collective-permute-start.7 = (bf16[272,128]{1,0:T(8,128)(2,1)S(1)}, bf16[272,128]{1,0:T(8,128)(2,1)S(1)}, u32[]{:S(2)}, u32[]{:S(2)}) collective-permute-start(bf16[272,128]{1,0:T(8,128)(2,1)S(1)} %get-tuple-element.50), channel_id=1, source_target_pairs={{0,12},{1,13},{2,14},{3,15},{4,0},{5,1},{6,2},{7,3},{8,4},{9,5},{1... | collective-permute-start | bytes 208904 | tf_op jit(solution)/shard_map/ppermute | solution.py:387
  18.7 7.5 %slice-start = ((s8[6291456]{0:T(1024)(128)(4,1)}), s8[4194304]{0:T(1024)(128)(4,1)S(1)}, s32[]{:S(2)}) async-start(s8[6291456]{0:T(1024)(128)(4,1)} %bitcast.4), calls=%async_computation | async-start | bytes 8388608
  20.5 3.6 %copy-start.2 = (s32[32,3]{0,1:T(4,128)S(1)}, s32[32,3]{0,1:T(4,128)}, u32[]{:S(2)}) copy-start(s32[32,3]{0,1:T(4,128)} %param.11) | copy-start | bytes 1156
  20.5 5.7 %slice-start.1 = ((s8[6291456]{0:T(1024)(128)(4,1)}), s8[2097152]{0:T(1024)(128)(4,1)S(1)}, s32[]{:S(2)}) async-start(s8[6291456]{0:T(1024)(128)(4,1)} %bitcast.4), calls=%async_computation.1 | async-start | bytes 4194304
  22.3 1.9 %copy-start = (bf16[32,3,96,96]{3,2,1,0:T(8,128)(2,1)S(1)}, bf16[32,3,96,96]{3,2,1,0:T(8,128)(2,1)}, u32[]{:S(2)}) copy-start(bf16[32,3,96,96]{3,2,1,0:T(8,128)(2,1)} %stiff_ref.5) | copy-start | bytes 5308420
  23.4 2.8 %collective-permute-start.9 = (bf16[768,128]{1,0:T(8,128)(2,1)S(1)}, bf16[768,128]{1,0:T(8,128)(2,1)S(1)}, u32[]{:S(2)}, u32[]{:S(2)}) collective-permute-start(bf16[768,128]{1,0:T(8,128)(2,1)S(1)} %shard_map.91.near_ref), channel_id=1, source_target_pairs={{0,1},{1,0},{2,3},{3,2},{4,5},{5,4},{6,7},{7,6},{8,9},{9,8},{10,11... | collective-permute-start | bytes 589832 | tf_op jit(solution)/shard_map/ppermute | solution.py:376
  23.5 4.5 %collective-permute-start.8 = (bf16[768,128]{1,0:T(8,128)(2,1)S(1)}, bf16[768,128]{1,0:T(8,128)(2,1)S(1)}, u32[]{:S(2)}, u32[]{:S(2)}) collective-permute-start(bf16[768,128]{1,0:T(8,128)(2,1)S(1)} %get-tuple-element.53.far_ref), channel_id=1, source_target_pairs={{1,2},{3,4},{5,6},{7,8},{9,10},{11,12},{13,14},{2,1},{4,3},{6,5},{... | collective-permute-start | bytes 589832 | tf_op jit(solution)/shard_map/ppermute | solution.py:380
  28.0 18.1 %copy-start.1 = (f32[1024,1024]{1,0:T(8,128)S(1)}, f32[1024,1024]{1,0:T(8,128)}, u32[]{:S(2)}) copy-start(f32[1024,1024]{1,0:T(8,128)} %a_ref.1) | copy-start | bytes 12582916
  29.4 4.8 %collective-permute-start.10 = (f32[64,1024]{1,0:T(8,128)S(1)}, f32[64,1024]{1,0:T(8,128)S(1)}, u32[]{:S(2)}, u32[]{:S(2)}) collective-permute-start(f32[64,1024]{1,0:T(8,128)S(1)} %get-tuple-element.59), channel_id=1, source_target_pairs={{0,1},{1,0},{2,3},{3,2},{4,5},{5,4},{6,7},{7,6},{8,9},{9,8},{10,11... | collective-permute-start | bytes 786440 | tf_op jit(solution)/shard_map/ppermute | solution.py:376
  34.2 5.2 %collective-permute-start.11 = (bf16[32,1024]{1,0:T(8,128)(2,1)S(1)}, bf16[32,1024]{1,0:T(8,128)(2,1)S(1)}, u32[]{:S(2)}, u32[]{:S(2)}) collective-permute-start(bf16[32,1024]{1,0:T(8,128)(2,1)S(1)} %get-tuple-element.61), channel_id=1, source_target_pairs={{0,2},{1,3},{2,0},{3,1},{4,6},{5,7},{6,4},{7,5},{8,10},{9,11},{10,... | collective-permute-start | bytes 196616 | tf_op jit(solution)/shard_map/ppermute | solution.py:376
  39.4 8.1 %collective-permute-start.14 = (bf16[32,1024]{1,0:T(8,128)(2,1)S(1)}, bf16[32,1024]{1,0:T(8,128)(2,1)S(1)}, u32[]{:S(2)}, u32[]{:S(2)}) collective-permute-start(bf16[32,1024]{1,0:T(8,128)(2,1)S(1)} %get-tuple-element.63), channel_id=1, source_target_pairs={{0,4},{1,5},{2,6},{3,7},{4,8},{5,9},{6,10},{7,11},{8,12},{9,13},{1... | collective-permute-start | bytes 196616 | tf_op jit(solution)/shard_map/ppermute | solution.py:387
  41.3 6.5 %collective-permute-start.13 = (bf16[32,1024]{1,0:T(8,128)(2,1)S(1)}, bf16[32,1024]{1,0:T(8,128)(2,1)S(1)}, u32[]{:S(2)}, u32[]{:S(2)}) collective-permute-start(bf16[32,1024]{1,0:T(8,128)(2,1)S(1)} %get-tuple-element.63), channel_id=1, source_target_pairs={{0,8},{1,9},{2,10},{3,11},{4,12},{5,13},{6,14},{7,15},{8,0},{9,1},... | collective-permute-start | bytes 196616 | tf_op jit(solution)/shard_map/ppermute | solution.py:387
  43.5 4.7 %collective-permute-start.12 = (bf16[32,1024]{1,0:T(8,128)(2,1)S(1)}, bf16[32,1024]{1,0:T(8,128)(2,1)S(1)}, u32[]{:S(2)}, u32[]{:S(2)}) collective-permute-start(bf16[32,1024]{1,0:T(8,128)(2,1)S(1)} %get-tuple-element.63), channel_id=1, source_target_pairs={{0,12},{1,13},{2,14},{3,15},{4,0},{5,1},{6,2},{7,3},{8,4},{9,5},{1... | collective-permute-start | bytes 196616 | tf_op jit(solution)/shard_map/ppermute | solution.py:387
  49.0 4.3 %collective-permute-start.15 = (bf16[32,1024]{1,0:T(8,128)(2,1)S(1)}, bf16[32,1024]{1,0:T(8,128)(2,1)S(1)}, u32[]{:S(2)}, u32[]{:S(2)}) collective-permute-start(bf16[32,1024]{1,0:T(8,128)(2,1)S(1)} %shard_map.98.own_ref), channel_id=1, source_target_pairs={{0,2},{1,3},{2,0},{3,1},{4,6},{5,7},{6,4},{7,5},{8,10},{9,11},{10,... | collective-permute-start | bytes 196616 | tf_op jit(solution)/shard_map/ppermute | solution.py:376
  52.5 1.3 %collective-permute-start.16 = (bf16[32,1024]{1,0:T(8,128)(2,1)S(1)}, bf16[32,1024]{1,0:T(8,128)(2,1)S(1)}, u32[]{:S(2)}, u32[]{:S(2)}) collective-permute-start(bf16[32,1024]{1,0:T(8,128)(2,1)S(1)} %shard_map.98.own_ref), channel_id=1, source_target_pairs={{0,1},{1,0},{2,3},{3,2},{4,5},{5,4},{6,7},{7,6},{8,9},{9,8},{10,11... | collective-permute-start | bytes 196616 | tf_op jit(solution)/shard_map/ppermute | solution.py:376
  53.3 1.3 %collective-permute-start.17 = (bf16[32,1024]{1,0:T(8,128)(2,1)S(1)}, bf16[32,1024]{1,0:T(8,128)(2,1)S(1)}, u32[]{:S(2)}, u32[]{:S(2)}) collective-permute-start(bf16[32,1024]{1,0:T(8,128)(2,1)S(1)} %collective-permute-done.15.y_ref), channel_id=1, source_target_pairs={{0,1},{1,0},{2,3},{3,2},{4,5},{5,4},{6,7},{7,6},{8,9},{9,8},{10,11... | collective-permute-start | bytes 196616 | tf_op jit(solution)/shard_map/ppermute | solution.py:376

commit v7 on v6

--- a/solution.py
+++ b/solution.py
@@ -225,13 +225,15 @@
         )
 
 
-def outer_rows(side, loads_ref, got_ref, stiff_ref, cols_ref, st_ref, ext_ref):
+def outer_rows(side, loads_ref, got_ref, stiff_ref, cols_ref, st_ref, ext_ref, copy=None):
     halo = got_ref.shape[0]
     blocks, _, size, _ = stiff_ref.shape
     end = halo + loads_ref.shape[0]
     got_at = pl.multiple_of(side * end, 32)
     ext_ref[halo:end, :] = loads_ref[...]
     ext_ref[pl.ds(got_at, halo), :] = got_ref[...]
+    if copy is not None:
+        copy.wait()
     first_col = lax.axis_index("elem") * blocks - REACH
     for k in range(REACH):
         st_ref[k * size : (k + 1) * size, :] = stiffen(
@@ -255,11 +257,16 @@
 
 
 def far_rows_kernel(
-    loads_ref, got_ref, stiff_ref, cols_ref, modes_ref, near_ref, modal_ref,
-    edge_ref, keep_ref, send_ref, ext_ref, st_ref, total_ref,
+    loads_ref, got_ref, stiff_ref, cols_vmem, modes_ref, near_ref, modal_ref,
+    edge_ref, keep_ref, send_ref, ext_ref, st_ref, total_ref, cols_ref, sem,
 ):
+    copy = pltpu.make_async_copy(cols_vmem, cols_ref, sem)
+    copy.start()
     odd = odd_core()
-    outer_rows(odd, loads_ref, got_ref, stiff_ref, cols_ref, st_ref, ext_ref)
+    edge_ref[pl.ds(pl.multiple_of((1 - odd) * got_ref.shape[0], 32), got_ref.shape[0]), :] = (
+        near_ref[...]
+    )
+    outer_rows(odd, loads_ref, got_ref, stiff_ref, cols_ref, st_ref, ext_ref, copy)
     halo = got_ref.shape[0]
     last = modes_ref.shape[0] - halo
     at = pl.multiple_of(odd * last, 32)
@@ -270,7 +277,6 @@
     keep_ref[...] = total_ref[pl.ds(pl.multiple_of(odd * half, 8), half), :]
     send_ref[...] = total_ref[pl.ds(pl.multiple_of((1 - odd) * half, 8), half), :]
     edge_ref[pl.ds(pl.multiple_of(odd * halo, 32), halo), :] = st_ref[...]
-    edge_ref[pl.ds(pl.multiple_of((1 - odd) * halo, 32), halo), :] = near_ref[...]
 
 
 def pair_kernel(mine_ref, other_ref, keep_ref, send_ref, total_ref):
@@ -472,8 +478,13 @@
             shape((width // 2, mode_count), F32),
         ),
         loads, got_far, stiff_blocks, cols, modes, st_near, modal_near,
-        smem=(3,),
-        scratch=(extended, pltpu.VMEM((halo, width), BF), pltpu.VMEM((width, mode_count), F32)),
+        scratch=(
+            extended,
+            pltpu.VMEM((halo, width), BF),
+            pltpu.VMEM((width, mode_count), F32),
+            pltpu.SMEM(cols.shape, jnp.int32),
+            pltpu.SemaphoreType.DMA(()),
+        ),
         flops=2 * halo * width * mode_count,
     )
     quarter = width // 4

time: 56.8 us -> 56.7 us (level)
  no operation moved by 1% of the time
where the time goes in v7:
time: 56.7 us; the launch traced here: 56.6 us
  starting transfers between devices  28.4 us (50%)
  Pallas kernels  17.1 us (30%)
  waiting for transfers between devices  10 us (18%)
  between operations  1 us (2%)
    ppermute x10, starting transfers between devices, turn(): return lax.ppermute(array, 'elem', pairs)  19.2 us
    pallas_call x15, Pallas kernels, call(): pl.pallas_call(kernel, out_shape=out_shape, in_specs=[pl.BlockSpec(memory...  17.1 us
    ppermute x7, starting transfers between devices, swap(): return lax.ppermute(array, 'elem', [(i, i ^ mask) for i in range(owners)])  8.49 us
    ppermute x7, waiting for transfers between devices, swap(): return lax.ppermute(array, 'elem', [(i, i ^ mask) for i in range(owners)])  6.04 us
    ppermute x10, waiting for transfers between devices, turn(): return lax.ppermute(array, 'elem', pairs)  4.01 us
  transfers between devices with their start and end apart: 18, of which 11 were waited for; matrix products, arithmetic and copies ran while one was open for 0% of the time, Pallas kernels for 17%

profile of v7, /device:TPU:0, one launch (start us, length us, event | category | flops | bytes accessed | tf_op | source)
XLA Modules:
  0.0 56.6 jit_solution(15382136590178294147)
XLA Ops:
  0.6 2.3 %shard_map.86 = (bf16[8,144,128]{2,1,0:T(8,128)(2,1)S(1)}, s32[1,1024]{1,0:T(1,128)S(1)}, f32[1,1024]{1,0:T(1,128)S(1)}, f32[1,32,128]{2,1,0:T(8,128)S(1)}, bf16[1024,128]{1,0:T(8,128)(2,1)S(1)}) custom-call(s32[1,1024]{1,0:T(1,128)} %bitcast.10, s32[8,128]{1,0:T(8,128)} %bitcast.11, bf16[1024,128]{1,0:T(8,128)(2,1)} %rec_hbm.1), custom_call_target="tpu_custom_call" | custom-call | flops 268435456 | bytes 270336 | tf_op jit(solution)/shard_map/pallas_call | solution.py:26
  4.7 5.0 %collective-permute-start.1 = (bf16[272,128]{1,0:T(8,128)(2,1)S(1)}, bf16[272,128]{1,0:T(8,128)(2,1)S(1)}, u32[]{:S(2)}, u32[]{:S(2)}) collective-permute-start(bf16[272,128]{1,0:T(8,128)(2,1)S(1)} %get-tuple-element.44), channel_id=1, source_target_pairs={{0,10},{1,11},{2,8},{3,9},{4,14},{5,15},{6,12},{7,13},{8,2},{9,3},... | collective-permute-start | bytes 208904 | tf_op jit(solution)/shard_map/ppermute | solution.py:393
  9.7 1.5 %collective-permute-start.2 = (bf16[272,128]{1,0:T(8,128)(2,1)S(1)}, bf16[272,128]{1,0:T(8,128)(2,1)S(1)}, u32[]{:S(2)}, u32[]{:S(2)}) collective-permute-start(bf16[272,128]{1,0:T(8,128)(2,1)S(1)} %get-tuple-element.45), channel_id=1, source_target_pairs={{0,6},{1,7},{2,4},{3,5},{4,10},{5,11},{6,8},{7,9},{8,14},{9,15},{1... | collective-permute-start | bytes 208904 | tf_op jit(solution)/shard_map/ppermute | solution.py:393
  11.2 3.2 %collective-permute-start.3 = (bf16[272,128]{1,0:T(8,128)(2,1)S(1)}, bf16[272,128]{1,0:T(8,128)(2,1)S(1)}, u32[]{:S(2)}, u32[]{:S(2)}) collective-permute-start(bf16[272,128]{1,0:T(8,128)(2,1)S(1)} %get-tuple-element.46), channel_id=1, source_target_pairs={{0,14},{1,15},{2,12},{3,13},{4,2},{5,3},{6,0},{7,1},{8,6},{9,7},{1... | collective-permute-start | bytes 208904 | tf_op jit(solution)/shard_map/ppermute | solution.py:393
  15.5 1.6 %collective-permute-done.2.refs_2_ = bf16[272,128]{1,0:T(8,128)(2,1)S(1)} collective-permute-done((bf16[272,128]{1,0:T(8,128)(2,1)S(1)}, bf16[272,128]{1,0:T(8,128)(2,1)S(1)}, u32[]{:S(2)}, u32[]{:S(2)}) %collective-permute-start.2) | collective-permute-done | bytes 69664 | tf_op jit(solution)/shard_map/ppermute | solution.py:393
  17.1 1.6 %collective-permute-start.7 = (bf16[272,128]{1,0:T(8,128)(2,1)S(1)}, bf16[272,128]{1,0:T(8,128)(2,1)S(1)}, u32[]{:S(2)}, u32[]{:S(2)}) collective-permute-start(bf16[272,128]{1,0:T(8,128)(2,1)S(1)} %get-tuple-element.50), channel_id=1, source_target_pairs={{0,12},{1,13},{2,14},{3,15},{4,0},{5,1},{6,2},{7,3},{8,4},{9,5},{1... | collective-permute-start | bytes 208904 | tf_op jit(solution)/shard_map/ppermute | solution.py:393
  18.7 1.8 %shard_map.89.refs_4_.sum_ref = f32[3072,128]{1,0:T(8,128)S(1)} custom-call(bf16[272,128]{1,0:T(8,128)(2,1)S(1)} %get-tuple-element.43.refs_0_, bf16[272,128]{1,0:T(8,128)(2,1)S(1)} %collective-permute-done.1.refs_1_, bf16[272,128]{1,0:T(8,128)(2,1)S(1)} %collective-permute-done.2.refs_2_, bf16[272,128]{1,0:T(8,128)(2,1)S(1)} %collective-permute-done.3.refs_3_), custom_call_target="tpu_custom_call" | custom-call | flops 805306368 | bytes 278528 | tf_op jit(solution)/shard_map/pallas_call | solution.py:26
  20.6 1.4 %collective-permute-done.5.refs_1_ = bf16[272,128]{1,0:T(8,128)(2,1)S(1)} collective-permute-done((bf16[272,128]{1,0:T(8,128)(2,1)S(1)}, bf16[272,128]{1,0:T(8,128)(2,1)S(1)}, u32[]{:S(2)}, u32[]{:S(2)}) %collective-permute-start.5) | collective-permute-done | bytes 69664 | tf_op jit(solution)/shard_map/ppermute | solution.py:393
  24.2 2.0 %shard_map.92 = (bf16[3072,128]{1,0:T(8,128)(2,1)S(1)}, bf16[1536,128]{1,0:T(8,128)(2,1)S(1)}) custom-call(f32[3072,128]{1,0:T(8,128)S(1)} %shard_map.89.refs_4_.sum_ref, f32[1,1024]{1,0:T(1,128)S(1)} %get-tuple-element.51.slots_ref, bf16[1024,128]{1,0:T(8,128)(2,1)S(1)} %get-tuple-element.52.records_ref, bf16[768,128]{1,0:T(8,128)(2,1)S(1)} %shard_map.91.near_ref, ...), custom_call_target="tpu_custom_call" | custom-call | flops 402653184 | bytes 4002176 | tf_op jit(solution)/shard_map/pallas_call | solution.py:26
  26.3 1.7 %shard_map.93 = (bf16[768,128]{1,0:T(8,128)(2,1)S(1)}, f32[128,1024]{1,0:T(8,128)S(1)}) custom-call(bf16[3072,128]{1,0:T(8,128)(2,1)S(1)} %get-tuple-element.54.loads_ref, bf16[768,128]{1,0:T(8,128)(2,1)S(1)} %collective-permute-done.9.got_ref, bf16[32,3,96,96]{3,2,1,0:T(8,128)(2,1)S(1)} %copy-done, s32[3,32]{1,0:T(4,128)S(1)} %bitcast.7, ...), custom_call_target="tpu_custom_call" | custom-call | flops 603979776 | bytes 9437568 | tf_op jit(solution)/shard_map/pallas_call | solution.py:26
  28.0 1.3 %shard_map.94 = (bf16[1536,128]{1,0:T(8,128)(2,1)S(1)}, f32[64,1024]{1,0:T(8,128)S(1)}, f32[64,1024]{1,0:T(8,128)S(1)}) custom-call(bf16[3072,128]{1,0:T(8,128)(2,1)S(1)} %get-tuple-element.54.loads_ref, bf16[768,128]{1,0:T(8,128)(2,1)S(1)} %collective-permute-done.8.got_ref, bf16[32,3,96,96]{3,2,1,0:T(8,128)(2,1)S(1)} %copy-done, s32[3,32]{1,0:T(4,128)S(1)} %bitcast.8, ...), custom_call_target="tpu_custom_call" | custom-call | flops 201326592 | bytes 9765248 | tf_op jit(solution)/shard_map/pallas_call | solution.py:26
  29.3 3.6 %collective-permute-start.10 = (f32[64,1024]{1,0:T(8,128)S(1)}, f32[64,1024]{1,0:T(8,128)S(1)}, u32[]{:S(2)}, u32[]{:S(2)}) collective-permute-start(f32[64,1024]{1,0:T(8,128)S(1)} %get-tuple-element.59), channel_id=1, source_target_pairs={{0,1},{1,0},{2,3},{3,2},{4,5},{5,4},{6,7},{7,6},{8,9},{9,8},{10,11... | collective-permute-start | bytes 786440 | tf_op jit(solution)/shard_map/ppermute | solution.py:382
  32.9 1.2 %collective-permute-done.10.other_ref = f32[64,1024]{1,0:T(8,128)S(1)} collective-permute-done((f32[64,1024]{1,0:T(8,128)S(1)}, f32[64,1024]{1,0:T(8,128)S(1)}, u32[]{:S(2)}, u32[]{:S(2)}) %collective-permute-start.10) | collective-permute-done | bytes 262176 | tf_op jit(solution)/shard_map/ppermute | solution.py:382
  34.1 2.8 %collective-permute-start.11 = (bf16[32,1024]{1,0:T(8,128)(2,1)S(1)}, bf16[32,1024]{1,0:T(8,128)(2,1)S(1)}, u32[]{:S(2)}, u32[]{:S(2)}) collective-permute-start(bf16[32,1024]{1,0:T(8,128)(2,1)S(1)} %get-tuple-element.61), channel_id=1, source_target_pairs={{0,2},{1,3},{2,0},{3,1},{4,6},{5,7},{6,4},{7,5},{8,10},{9,11},{10,... | collective-permute-start | bytes 196616 | tf_op jit(solution)/shard_map/ppermute | solution.py:382
  36.9 2.4 %collective-permute-done.11.other_ref = bf16[32,1024]{1,0:T(8,128)(2,1)S(1)} collective-permute-done((bf16[32,1024]{1,0:T(8,128)(2,1)S(1)}, bf16[32,1024]{1,0:T(8,128)(2,1)S(1)}, u32[]{:S(2)}, u32[]{:S(2)}) %collective-permute-start.11) | collective-permute-done | bytes 65568 | tf_op jit(solution)/shard_map/ppermute | solution.py:382
  39.3 1.9 %collective-permute-start.14 = (bf16[32,1024]{1,0:T(8,128)(2,1)S(1)}, bf16[32,1024]{1,0:T(8,128)(2,1)S(1)}, u32[]{:S(2)}, u32[]{:S(2)}) collective-permute-start(bf16[32,1024]{1,0:T(8,128)(2,1)S(1)} %get-tuple-element.63), channel_id=1, source_target_pairs={{0,4},{1,5},{2,6},{3,7},{4,8},{5,9},{6,10},{7,11},{8,12},{9,13},{1... | collective-permute-start | bytes 196616 | tf_op jit(solution)/shard_map/ppermute | solution.py:393
  41.3 2.2 %collective-permute-start.13 = (bf16[32,1024]{1,0:T(8,128)(2,1)S(1)}, bf16[32,1024]{1,0:T(8,128)(2,1)S(1)}, u32[]{:S(2)}, u32[]{:S(2)}) collective-permute-start(bf16[32,1024]{1,0:T(8,128)(2,1)S(1)} %get-tuple-element.63), channel_id=1, source_target_pairs={{0,8},{1,9},{2,10},{3,11},{4,12},{5,13},{6,14},{7,15},{8,0},{9,1},... | collective-permute-start | bytes 196616 | tf_op jit(solution)/shard_map/ppermute | solution.py:393
  43.4 2.6 %collective-permute-start.12 = (bf16[32,1024]{1,0:T(8,128)(2,1)S(1)}, bf16[32,1024]{1,0:T(8,128)(2,1)S(1)}, u32[]{:S(2)}, u32[]{:S(2)}) collective-permute-start(bf16[32,1024]{1,0:T(8,128)(2,1)S(1)} %get-tuple-element.63), channel_id=1, source_target_pairs={{0,12},{1,13},{2,14},{3,15},{4,0},{5,1},{6,2},{7,3},{8,4},{9,5},{1... | collective-permute-start | bytes 196616 | tf_op jit(solution)/shard_map/ppermute | solution.py:393
  46.1 1.3 %shard_map.97 = (bf16[1024,1024]{1,0:T(8,128)(2,1)S(1)}, bf16[1024,1024]{1,0:T(8,128)(2,1)S(1)}) custom-call(f32[1024,1024]{1,0:T(8,128)S(1)} %copy-done.1), custom_call_target="tpu_custom_call" | custom-call | flops 4194304 | bytes 4194304 | tf_op jit(solution)/shard_map/pallas_call | solution.py:26
  48.1 0.8 %shard_map.98.own_ref = bf16[32,1024]{1,0:T(8,128)(2,1)S(1)} custom-call(f32[32,1024]{1,0:T(8,128)S(1)} %get-tuple-element.62.mine_ref, bf16[32,1024]{1,0:T(8,128)(2,1)S(1)} %collective-permute-done.12.refs_0_, bf16[32,1024]{1,0:T(8,128)(2,1)S(1)} %collective-permute-done.13.refs_1_, bf16[32,1024]{1,0:T(8,128)(2,1)S(1)} %collective-permute-done.14.refs_2_, ...), custom_call_target="tpu_custom_call" | custom-call | flops 201326592 | bytes 4521984 | tf_op jit(solution)/shard_map/pallas_call | solution.py:26
  48.9 1.4 %collective-permute-start.15 = (bf16[32,1024]{1,0:T(8,128)(2,1)S(1)}, bf16[32,1024]{1,0:T(8,128)(2,1)S(1)}, u32[]{:S(2)}, u32[]{:S(2)}) collective-permute-start(bf16[32,1024]{1,0:T(8,128)(2,1)S(1)} %shard_map.98.own_ref), channel_id=1, source_target_pairs={{0,2},{1,3},{2,0},{3,1},{4,6},{5,7},{6,4},{7,5},{8,10},{9,11},{10,... | collective-permute-start | bytes 196616 | tf_op jit(solution)/shard_map/ppermute | solution.py:382
  50.4 2.0 %shard_map.99 = (bf16[1024,3072]{1,0:T(8,128)(2,1)S(1)}, bf16[128,3072]{1,0:T(8,128)(2,1)S(1)}) custom-call(bf16[3072,1024]{1,0:T(8,128)(2,1)S(1)} %bitcast.5, bf16[1536,128]{1,0:T(8,128)(2,1)S(1)} %get-tuple-element.55.mid_ref, bf16[1536,128]{1,0:T(8,128)(2,1)S(1)} %get-tuple-element.66.edge_ref), custom_call_target="tpu_custom_call" | custom-call | bytes 7077888 | tf_op jit(solution)/shard_map/pallas_call | solution.py:26
  53.7 0.7 %collective-permute-done.17.both_ref = bf16[32,1024]{1,0:T(8,128)(2,1)S(1)} collective-permute-done((bf16[32,1024]{1,0:T(8,128)(2,1)S(1)}, bf16[32,1024]{1,0:T(8,128)(2,1)S(1)}, u32[]{:S(2)}, u32[]{:S(2)}) %collective-permute-start.17) | collective-permute-done | bytes 65568 | tf_op jit(solution)/shard_map/ppermute | solution.py:382
  54.5 1.9 %shard_map.100 = (bf16[3072,128]{1,0:T(8,128)(2,1)}, f32[24,128]{1,0:T(8,128)}) custom-call(bf16[32,1024]{1,0:T(8,128)(2,1)S(1)} %shard_map.98.own_ref, bf16[32,1024]{1,0:T(8,128)(2,1)S(1)} %collective-permute-done.15.y_ref, bf16[32,1024]{1,0:T(8,128)(2,1)S(1)} %collective-permute-done.16.core_ref, bf16[32,1024]{1,0:T(8,128)(2,1)S(1)} %collective-permute-done.17.both_ref, ...), custom_call_target="tpu_custom_call" | custom-call | flops 805306368 | bytes 7340032 | tf_op jit(solution)/shard_map/pallas_call | solution.py:26
  (38 shorter events, 7.2 us)
Async XLA Ops:
  2.9 1.7 %collective-permute-start = (bf16[8,144,128]{2,1,0:T(8,128)(2,1)S(1)}, bf16[8,144,128]{2,1,0:T(8,128)(2,1)S(1)}, u32[]{:S(2)}, u32[]{:S(2)}) collective-permute-start(bf16[8,144,128]{2,1,0:T(8,128)(2,1)S(1)} %get-tuple-element.42), channel_id=1, source_target_pairs={{0,1},{1,0},{2,3},{3,2},{4,5},{5,4},{6,7},{7,6},{8,9},{9,8},{10,11... | collective-permute-start | bytes 884744 | tf_op jit(solution)/shard_map/ppermute | solution.py:382
  4.7 10.2 %collective-permute-start.1 = (bf16[272,128]{1,0:T(8,128)(2,1)S(1)}, bf16[272,128]{1,0:T(8,128)(2,1)S(1)}, u32[]{:S(2)}, u32[]{:S(2)}) collective-permute-start(bf16[272,128]{1,0:T(8,128)(2,1)S(1)} %get-tuple-element.44), channel_id=1, source_target_pairs={{0,10},{1,11},{2,8},{3,9},{4,14},{5,15},{6,12},{7,13},{8,2},{9,3},... | collective-permute-start | bytes 208904 | tf_op jit(solution)/shard_map/ppermute | solution.py:393
  9.7 7.5 %collective-permute-start.2 = (bf16[272,128]{1,0:T(8,128)(2,1)S(1)}, bf16[272,128]{1,0:T(8,128)(2,1)S(1)}, u32[]{:S(2)}, u32[]{:S(2)}) collective-permute-start(bf16[272,128]{1,0:T(8,128)(2,1)S(1)} %get-tuple-element.45), channel_id=1, source_target_pairs={{0,6},{1,7},{2,4},{3,5},{4,10},{5,11},{6,8},{7,9},{8,14},{9,15},{1... | collective-permute-start | bytes 208904 | tf_op jit(solution)/shard_map/ppermute | solution.py:393
  11.2 7.6 %collective-permute-start.3 = (bf16[272,128]{1,0:T(8,128)(2,1)S(1)}, bf16[272,128]{1,0:T(8,128)(2,1)S(1)}, u32[]{:S(2)}, u32[]{:S(2)}) collective-permute-start(bf16[272,128]{1,0:T(8,128)(2,1)S(1)} %get-tuple-element.46), channel_id=1, source_target_pairs={{0,14},{1,15},{2,12},{3,13},{4,2},{5,3},{6,0},{7,1},{8,6},{9,7},{1... | collective-permute-start | bytes 208904 | tf_op jit(solution)/shard_map/ppermute | solution.py:393
  14.4 6.2 %collective-permute-start.4 = (bf16[272,128]{1,0:T(8,128)(2,1)S(1)}, bf16[272,128]{1,0:T(8,128)(2,1)S(1)}, u32[]{:S(2)}, u32[]{:S(2)}) collective-permute-start(bf16[272,128]{1,0:T(8,128)(2,1)S(1)} %get-tuple-element.47), channel_id=1, source_target_pairs={{0,2},{1,3},{2,0},{3,1},{4,6},{5,7},{6,4},{7,5},{8,10},{9,11},{10,... | collective-permute-start | bytes 208904 | tf_op jit(solution)/shard_map/ppermute | solution.py:393
  14.9 7.1 %collective-permute-start.5 = (bf16[272,128]{1,0:T(8,128)(2,1)S(1)}, bf16[272,128]{1,0:T(8,128)(2,1)S(1)}, u32[]{:S(2)}, u32[]{:S(2)}) collective-permute-start(bf16[272,128]{1,0:T(8,128)(2,1)S(1)} %get-tuple-element.48), channel_id=1, source_target_pairs={{0,8},{1,9},{2,10},{3,11},{4,12},{5,13},{6,14},{7,15},{8,0},{9,1},... | collective-permute-start | bytes 208904 | tf_op jit(solution)/shard_map/ppermute | solution.py:393
  14.9 7.1 %collective-permute-start.6 = (bf16[272,128]{1,0:T(8,128)(2,1)S(1)}, bf16[272,128]{1,0:T(8,128)(2,1)S(1)}, u32[]{:S(2)}, u32[]{:S(2)}) collective-permute-start(bf16[272,128]{1,0:T(8,128)(2,1)S(1)} %get-tuple-element.49), channel_id=1, source_target_pairs={{0,4},{1,5},{2,6},{3,7},{4,8},{5,9},{6,10},{7,11},{8,12},{9,13},{1... | collective-permute-start | bytes 208904 | tf_op jit(solution)/shard_map/ppermute | solution.py:393
  17.1 5.1 %collective-permute-start.7 = (bf16[272,128]{1,0:T(8,128)(2,1)S(1)}, bf16[272,128]{1,0:T(8,128)(2,1)S(1)}, u32[]{:S(2)}, u32[]{:S(2)}) collective-permute-start(bf16[272,128]{1,0:T(8,128)(2,1)S(1)} %get-tuple-element.50), channel_id=1, source_target_pairs={{0,12},{1,13},{2,14},{3,15},{4,0},{5,1},{6,2},{7,3},{8,4},{9,5},{1... | collective-permute-start | bytes 208904 | tf_op jit(solution)/shard_map/ppermute | solution.py:393
  18.7 7.5 %slice-start = ((s8[6291456]{0:T(1024)(128)(4,1)}), s8[4194304]{0:T(1024)(128)(4,1)S(1)}, s32[]{:S(2)}) async-start(s8[6291456]{0:T(1024)(128)(4,1)} %bitcast.4), calls=%async_computation | async-start | bytes 8388608
  20.5 3.6 %copy-start.2 = (s32[32,3]{0,1:T(4,128)S(1)}, s32[32,3]{0,1:T(4,128)}, u32[]{:S(2)}) copy-start(s32[32,3]{0,1:T(4,128)} %param.11) | copy-start | bytes 1156
  20.5 5.7 %slice-start.1 = ((s8[6291456]{0:T(1024)(128)(4,1)}), s8[2097152]{0:T(1024)(128)(4,1)S(1)}, s32[]{:S(2)}) async-start(s8[6291456]{0:T(1024)(128)(4,1)} %bitcast.4), calls=%async_computation.1 | async-start | bytes 4194304
  22.3 1.9 %copy-start = (bf16[32,3,96,96]{3,2,1,0:T(8,128)(2,1)S(1)}, bf16[32,3,96,96]{3,2,1,0:T(8,128)(2,1)}, u32[]{:S(2)}) copy-start(bf16[32,3,96,96]{3,2,1,0:T(8,128)(2,1)} %stiff_ref.5) | copy-start | bytes 5308420
  23.4 2.8 %collective-permute-start.9 = (bf16[768,128]{1,0:T(8,128)(2,1)S(1)}, bf16[768,128]{1,0:T(8,128)(2,1)S(1)}, u32[]{:S(2)}, u32[]{:S(2)}) collective-permute-start(bf16[768,128]{1,0:T(8,128)(2,1)S(1)} %shard_map.91.near_ref), channel_id=1, source_target_pairs={{0,1},{1,0},{2,3},{3,2},{4,5},{5,4},{6,7},{7,6},{8,9},{9,8},{10,11... | collective-permute-start | bytes 589832 | tf_op jit(solution)/shard_map/ppermute | solution.py:382
  23.5 4.5 %collective-permute-start.8 = (bf16[768,128]{1,0:T(8,128)(2,1)S(1)}, bf16[768,128]{1,0:T(8,128)(2,1)S(1)}, u32[]{:S(2)}, u32[]{:S(2)}) collective-permute-start(bf16[768,128]{1,0:T(8,128)(2,1)S(1)} %get-tuple-element.53.far_ref), channel_id=1, source_target_pairs={{1,2},{3,4},{5,6},{7,8},{9,10},{11,12},{13,14},{2,1},{4,3},{6,5},{... | collective-permute-start | bytes 589832 | tf_op jit(solution)/shard_map/ppermute | solution.py:386
  28.0 18.1 %copy-start.1 = (f32[1024,1024]{1,0:T(8,128)S(1)}, f32[1024,1024]{1,0:T(8,128)}, u32[]{:S(2)}) copy-start(f32[1024,1024]{1,0:T(8,128)} %a_ref.1) | copy-start | bytes 12582916
  29.3 4.7 %collective-permute-start.10 = (f32[64,1024]{1,0:T(8,128)S(1)}, f32[64,1024]{1,0:T(8,128)S(1)}, u32[]{:S(2)}, u32[]{:S(2)}) collective-permute-start(f32[64,1024]{1,0:T(8,128)S(1)} %get-tuple-element.59), channel_id=1, source_target_pairs={{0,1},{1,0},{2,3},{3,2},{4,5},{5,4},{6,7},{7,6},{8,9},{9,8},{10,11... | collective-permute-start | bytes 786440 | tf_op jit(solution)/shard_map/ppermute | solution.py:382
  34.1 5.2 %collective-permute-start.11 = (bf16[32,1024]{1,0:T(8,128)(2,1)S(1)}, bf16[32,1024]{1,0:T(8,128)(2,1)S(1)}, u32[]{:S(2)}, u32[]{:S(2)}) collective-permute-start(bf16[32,1024]{1,0:T(8,128)(2,1)S(1)} %get-tuple-element.61), channel_id=1, source_target_pairs={{0,2},{1,3},{2,0},{3,1},{4,6},{5,7},{6,4},{7,5},{8,10},{9,11},{10,... | collective-permute-start | bytes 196616 | tf_op jit(solution)/shard_map/ppermute | solution.py:382
  39.3 8.1 %collective-permute-start.14 = (bf16[32,1024]{1,0:T(8,128)(2,1)S(1)}, bf16[32,1024]{1,0:T(8,128)(2,1)S(1)}, u32[]{:S(2)}, u32[]{:S(2)}) collective-permute-start(bf16[32,1024]{1,0:T(8,128)(2,1)S(1)} %get-tuple-element.63), channel_id=1, source_target_pairs={{0,4},{1,5},{2,6},{3,7},{4,8},{5,9},{6,10},{7,11},{8,12},{9,13},{1... | collective-permute-start | bytes 196616 | tf_op jit(solution)/shard_map/ppermute | solution.py:393
  41.3 6.5 %collective-permute-start.13 = (bf16[32,1024]{1,0:T(8,128)(2,1)S(1)}, bf16[32,1024]{1,0:T(8,128)(2,1)S(1)}, u32[]{:S(2)}, u32[]{:S(2)}) collective-permute-start(bf16[32,1024]{1,0:T(8,128)(2,1)S(1)} %get-tuple-element.63), channel_id=1, source_target_pairs={{0,8},{1,9},{2,10},{3,11},{4,12},{5,13},{6,14},{7,15},{8,0},{9,1},... | collective-permute-start | bytes 196616 | tf_op jit(solution)/shard_map/ppermute | solution.py:393
  43.4 4.7 %collective-permute-start.12 = (bf16[32,1024]{1,0:T(8,128)(2,1)S(1)}, bf16[32,1024]{1,0:T(8,128)(2,1)S(1)}, u32[]{:S(2)}, u32[]{:S(2)}) collective-permute-start(bf16[32,1024]{1,0:T(8,128)(2,1)S(1)} %get-tuple-element.63), channel_id=1, source_target_pairs={{0,12},{1,13},{2,14},{3,15},{4,0},{5,1},{6,2},{7,3},{8,4},{9,5},{1... | collective-permute-start | bytes 196616 | tf_op jit(solution)/shard_map/ppermute | solution.py:393
  48.9 4.3 %collective-permute-start.15 = (bf16[32,1024]{1,0:T(8,128)(2,1)S(1)}, bf16[32,1024]{1,0:T(8,128)(2,1)S(1)}, u32[]{:S(2)}, u32[]{:S(2)}) collective-permute-start(bf16[32,1024]{1,0:T(8,128)(2,1)S(1)} %shard_map.98.own_ref), channel_id=1, source_target_pairs={{0,2},{1,3},{2,0},{3,1},{4,6},{5,7},{6,4},{7,5},{8,10},{9,11},{10,... | collective-permute-start | bytes 196616 | tf_op jit(solution)/shard_map/ppermute | solution.py:382
  52.4 1.3 %collective-permute-start.16 = (bf16[32,1024]{1,0:T(8,128)(2,1)S(1)}, bf16[32,1024]{1,0:T(8,128)(2,1)S(1)}, u32[]{:S(2)}, u32[]{:S(2)}) collective-permute-start(bf16[32,1024]{1,0:T(8,128)(2,1)S(1)} %shard_map.98.own_ref), channel_id=1, source_target_pairs={{0,1},{1,0},{2,3},{3,2},{4,5},{5,4},{6,7},{7,6},{8,9},{9,8},{10,11... | collective-permute-start | bytes 196616 | tf_op jit(solution)/shard_map/ppermute | solution.py:382
  53.2 1.3 %collective-permute-start.17 = (bf16[32,1024]{1,0:T(8,128)(2,1)S(1)}, bf16[32,1024]{1,0:T(8,128)(2,1)S(1)}, u32[]{:S(2)}, u32[]{:S(2)}) collective-permute-start(bf16[32,1024]{1,0:T(8,128)(2,1)S(1)} %collective-permute-done.15.y_ref), channel_id=1, source_target_pairs={{0,1},{1,0},{2,3},{3,2},{4,5},{5,4},{6,7},{7,6},{8,9},{9,8},{10,11... | collective-permute-start | bytes 196616 | tf_op jit(solution)/shard_map/ppermute | solution.py:382

commit v8 on v7

--- a/solution.py
+++ b/solution.py
@@ -258,7 +258,7 @@
 
 def far_rows_kernel(
     loads_ref, got_ref, stiff_ref, cols_vmem, modes_ref, near_ref, modal_ref,
-    edge_ref, keep_ref, send_ref, ext_ref, st_ref, total_ref, cols_ref, sem,
+    edge_ref, keep_ref, one_ref, two_ref, three_ref, ext_ref, st_ref, total_ref, cols_ref, sem,
 ):
     copy = pltpu.make_async_copy(cols_vmem, cols_ref, sem)
     copy.start()
@@ -273,22 +273,18 @@
     total_ref[...] = modal_ref[...] + lax.dot_general(
         st_ref[...], modes_ref[pl.ds(at, halo), :], TN, preferred_element_type=F32
     )
-    half = total_ref.shape[0] // 2
-    keep_ref[...] = total_ref[pl.ds(pl.multiple_of(odd * half, 8), half), :]
-    send_ref[...] = total_ref[pl.ds(pl.multiple_of((1 - odd) * half, 8), half), :]
+    quarter = keep_ref.shape[0]
+    part = lax.rem(lax.axis_index("elem"), 4)
+    for k, ref in enumerate((keep_ref, one_ref, two_ref, three_ref)):
+        to = lax.rem(part + k, 4)
+        at = pl.multiple_of((lax.rem(to, 2) * 2 + to // 2) * quarter, 16)
+        ref[...] = total_ref[pl.ds(at, quarter), :].astype(ref.dtype)
     edge_ref[pl.ds(pl.multiple_of(odd * halo, 32), halo), :] = st_ref[...]
 
 
-def pair_kernel(mine_ref, other_ref, keep_ref, send_ref, total_ref):
-    bit = lax.rem(lax.axis_index("elem") // 2, 2)
-    total_ref[...] = mine_ref[...] + other_ref[...]
-    half = total_ref.shape[0] // 2
-    keep_ref[...] = total_ref[pl.ds(pl.multiple_of(bit * half, 8), half), :]
-    send_ref[...] = total_ref[pl.ds(pl.multiple_of((1 - bit) * half, 8), half), :].astype(BF)
-
-
-def add_kernel(mine_ref, other_ref, total_ref, send_ref):
-    total = mine_ref[...] + other_ref[...].astype(F32)
+def add_kernel(mine_ref, one_ref, two_ref, three_ref, total_ref, send_ref):
+    total = mine_ref[...] + one_ref[...].astype(F32)
+    total += two_ref[...].astype(F32) + three_ref[...].astype(F32)
     total_ref[...] = total
     send_ref[...] = total.astype(BF)
 
@@ -381,6 +377,11 @@
     def swap(array, mask):
         return lax.ppermute(array, "elem", [(i, i ^ mask) for i in range(owners)])
 
+    def around(array, k):
+        return lax.ppermute(
+            array, "elem", [(i, i // 4 * 4 + (i + k) % 4) for i in range(owners)]
+        )
+
     def swap_far(array):
         pairs = [(i, i + 1) for i in range(1, owners - 1, 2)]
         return lax.ppermute(array, "elem", pairs + [(j, i) for i, j in pairs])
@@ -470,12 +471,16 @@
         scratch=(extended,),
         flops=2 * (elem_rows - halo) * width * mode_count,
     )
-    st_edge, keep, send = call(
+    quarter = width // 4
+    piece = shape((quarter, mode_count), BF)
+    st_edge, keep, *sends = call(
         far_rows_kernel,
         (
             shape((2 * halo, width), BF),
-            shape((width // 2, mode_count), F32),
-            shape((width // 2, mode_count), F32),
+            shape((quarter, mode_count), F32),
+            piece,
+            piece,
+            piece,
         ),
         loads, got_far, stiff_blocks, cols, modes, st_near, modal_near,
         scratch=(
@@ -487,16 +492,11 @@
         ),
         flops=2 * halo * width * mode_count,
     )
-    quarter = width // 4
-    piece = shape((quarter, mode_count), BF)
-    keep, send = call(
-        pair_kernel,
+    shares = {k: around(sends[k - 1], k) for k in (1, 3, 2)}
+    total, send = call(
+        add_kernel,
         (shape((quarter, mode_count), F32), piece),
-        keep, swap(send, 1),
-        scratch=(pltpu.VMEM((width // 2, mode_count), F32),),
-    )
-    total, send = call(
-        add_kernel, (shape((quarter, mode_count), F32), piece), keep, swap(send, 2)
+        keep, shares[1], shares[2], shares[3],
     )
     groups = chips // 2
     steps = range(groups - 1, 0, -1)

time: 56.7 us -> 56.5 us (level)
  waiting for transfers between devices: 10 us -> 9.27 us
  starting transfers between devices: 28.4 us -> 29 us
    ppermute x0 -> x3, starting transfers between devices: none -> 7.42 us  [around(): lax.ppermute(array, 'elem', [(i, i // 4 * 4 + (i + k) % 4) for i in range...]
    ppermute x7 -> x5, starting transfers between devices: 8.49 us -> 2.4 us  [swap(): return lax.ppermute(array, 'elem', [(i, i ^ mask) for i in range(owners)])]
    ppermute x7 -> x5, waiting for transfers between devices: 6.04 us -> 2.19 us  [swap(): return lax.ppermute(array, 'elem', [(i, i ^ mask) for i in range(owners)])]
    ppermute x0 -> x3, waiting for transfers between devices: none -> 1.9 us  [around(): lax.ppermute(array, 'elem', [(i, i // 4 * 4 + (i + k) % 4) for i in range...]
    ppermute x10, waiting for transfers between devices: 4.01 us -> 5.17 us  [turn(): return lax.ppermute(array, 'elem', pairs)]
    ppermute x10, starting transfers between devices: 19.2 us -> 18.5 us  [turn(): return lax.ppermute(array, 'elem', pairs)]
    pallas_call x15 -> x14, Pallas kernels: 17.1 us -> 17.1 us  [call(): pl.pallas_call(kernel, out_shape=out_shape, in_specs=[pl.BlockSpec(memory...]
  transfers between devices with their start and end apart: 18 -> 19, of which waited for: 11 -> 10; matrix products, arithmetic and copies ran while one was open for 0% -> 0% of each run, Pallas kernels for 17% -> 17%
where the time goes in v8:
time: 56.5 us; the launch traced here: 56.4 us
  starting transfers between devices  29 us (51%)
  Pallas kernels  17.1 us (30%)
  waiting for transfers between devices  9.27 us (16%)
  between operations  1 us (2%)
    ppermute x10, starting transfers between devices, turn(): return lax.ppermute(array, 'elem', pairs)  18.5 us
    pallas_call x14, Pallas kernels, call(): pl.pallas_call(kernel, out_shape=out_shape, in_specs=[pl.BlockSpec(memory...  17.1 us
    ppermute x3, starting transfers between devices, around(): lax.ppermute(array, 'elem', [(i, i // 4 * 4 + (i + k) % 4) for i in range...  7.42 us
    ppermute x10, waiting for transfers between devices, turn(): return lax.ppermute(array, 'elem', pairs)  5.17 us
    ppermute x5, starting transfers between devices, swap(): return lax.ppermute(array, 'elem', [(i, i ^ mask) for i in range(owners)])  2.4 us
    ppermute x5, waiting for transfers between devices, swap(): return lax.ppermute(array, 'elem', [(i, i ^ mask) for i in range(owners)])  2.19 us
    ppermute x3, waiting for transfers between devices, around(): lax.ppermute(array, 'elem', [(i, i // 4 * 4 + (i + k) % 4) for i in range...  1.9 us
  transfers between devices with their start and end apart: 19, of which 10 were waited for; matrix products, arithmetic and copies ran while one was open for 0% of the time, Pallas kernels for 17%

profile of v8, /device:TPU:0, one launch (start us, length us, event | category | flops | bytes accessed | tf_op | source)
XLA Modules:
  0.0 56.4 jit_solution(1081186149372665818)
XLA Ops:
  0.6 2.3 %shard_map.86 = (bf16[8,144,128]{2,1,0:T(8,128)(2,1)S(1)}, s32[1,1024]{1,0:T(1,128)S(1)}, f32[1,1024]{1,0:T(1,128)S(1)}, f32[1,32,128]{2,1,0:T(8,128)S(1)}, bf16[1024,128]{1,0:T(8,128)(2,1)S(1)}) custom-call(s32[1,1024]{1,0:T(1,128)} %bitcast.10, s32[8,128]{1,0:T(8,128)} %bitcast.11, bf16[1024,128]{1,0:T(8,128)(2,1)} %rec_hbm.1), custom_call_target="tpu_custom_call" | custom-call | flops 268435456 | bytes 270336 | tf_op jit(solution)/shard_map/pallas_call | solution.py:26
  4.7 5.0 %collective-permute-start.1 = (bf16[272,128]{1,0:T(8,128)(2,1)S(1)}, bf16[272,128]{1,0:T(8,128)(2,1)S(1)}, u32[]{:S(2)}, u32[]{:S(2)}) collective-permute-start(bf16[272,128]{1,0:T(8,128)(2,1)S(1)} %get-tuple-element.44), channel_id=1, source_target_pairs={{0,10},{1,11},{2,8},{3,9},{4,14},{5,15},{6,12},{7,13},{8,2},{9,3},... | collective-permute-start | bytes 208904 | tf_op jit(solution)/shard_map/ppermute | solution.py:394
  9.7 1.5 %collective-permute-start.2 = (bf16[272,128]{1,0:T(8,128)(2,1)S(1)}, bf16[272,128]{1,0:T(8,128)(2,1)S(1)}, u32[]{:S(2)}, u32[]{:S(2)}) collective-permute-start(bf16[272,128]{1,0:T(8,128)(2,1)S(1)} %get-tuple-element.45), channel_id=1, source_target_pairs={{0,6},{1,7},{2,4},{3,5},{4,10},{5,11},{6,8},{7,9},{8,14},{9,15},{1... | collective-permute-start | bytes 208904 | tf_op jit(solution)/shard_map/ppermute | solution.py:394
  11.2 3.2 %collective-permute-start.3 = (bf16[272,128]{1,0:T(8,128)(2,1)S(1)}, bf16[272,128]{1,0:T(8,128)(2,1)S(1)}, u32[]{:S(2)}, u32[]{:S(2)}) collective-permute-start(bf16[272,128]{1,0:T(8,128)(2,1)S(1)} %get-tuple-element.46), channel_id=1, source_target_pairs={{0,14},{1,15},{2,12},{3,13},{4,2},{5,3},{6,0},{7,1},{8,6},{9,7},{1... | collective-permute-start | bytes 208904 | tf_op jit(solution)/shard_map/ppermute | solution.py:394
  15.5 1.6 %collective-permute-done.2.refs_2_ = bf16[272,128]{1,0:T(8,128)(2,1)S(1)} collective-permute-done((bf16[272,128]{1,0:T(8,128)(2,1)S(1)}, bf16[272,128]{1,0:T(8,128)(2,1)S(1)}, u32[]{:S(2)}, u32[]{:S(2)}) %collective-permute-start.2) | collective-permute-done | bytes 69664 | tf_op jit(solution)/shard_map/ppermute | solution.py:394
  17.1 1.6 %collective-permute-start.7 = (bf16[272,128]{1,0:T(8,128)(2,1)S(1)}, bf16[272,128]{1,0:T(8,128)(2,1)S(1)}, u32[]{:S(2)}, u32[]{:S(2)}) collective-permute-start(bf16[272,128]{1,0:T(8,128)(2,1)S(1)} %get-tuple-element.50), channel_id=1, source_target_pairs={{0,12},{1,13},{2,14},{3,15},{4,0},{5,1},{6,2},{7,3},{8,4},{9,5},{1... | collective-permute-start | bytes 208904 | tf_op jit(solution)/shard_map/ppermute | solution.py:394
  18.7 1.8 %shard_map.89.refs_4_.sum_ref = f32[3072,128]{1,0:T(8,128)S(1)} custom-call(bf16[272,128]{1,0:T(8,128)(2,1)S(1)} %get-tuple-element.43.refs_0_, bf16[272,128]{1,0:T(8,128)(2,1)S(1)} %collective-permute-done.1.refs_1_, bf16[272,128]{1,0:T(8,128)(2,1)S(1)} %collective-permute-done.2.refs_2_, bf16[272,128]{1,0:T(8,128)(2,1)S(1)} %collective-permute-done.3.refs_3_), custom_call_target="tpu_custom_call" | custom-call | flops 805306368 | bytes 278528 | tf_op jit(solution)/shard_map/pallas_call | solution.py:26
  20.6 1.4 %collective-permute-done.5.refs_1_ = bf16[272,128]{1,0:T(8,128)(2,1)S(1)} collective-permute-done((bf16[272,128]{1,0:T(8,128)(2,1)S(1)}, bf16[272,128]{1,0:T(8,128)(2,1)S(1)}, u32[]{:S(2)}, u32[]{:S(2)}) %collective-permute-start.5) | collective-permute-done | bytes 69664 | tf_op jit(solution)/shard_map/ppermute | solution.py:394
  24.2 2.0 %shard_map.92 = (bf16[3072,128]{1,0:T(8,128)(2,1)S(1)}, bf16[1536,128]{1,0:T(8,128)(2,1)S(1)}) custom-call(f32[3072,128]{1,0:T(8,128)S(1)} %shard_map.89.refs_4_.sum_ref, f32[1,1024]{1,0:T(1,128)S(1)} %get-tuple-element.51.slots_ref, bf16[1024,128]{1,0:T(8,128)(2,1)S(1)} %get-tuple-element.52.records_ref, bf16[768,128]{1,0:T(8,128)(2,1)S(1)} %shard_map.91.near_ref, ...), custom_call_target="tpu_custom_call" | custom-call | flops 402653184 | bytes 4002176 | tf_op jit(solution)/shard_map/pallas_call | solution.py:26
  26.3 1.7 %shard_map.93 = (bf16[768,128]{1,0:T(8,128)(2,1)S(1)}, f32[128,1024]{1,0:T(8,128)S(1)}) custom-call(bf16[3072,128]{1,0:T(8,128)(2,1)S(1)} %get-tuple-element.54.loads_ref, bf16[768,128]{1,0:T(8,128)(2,1)S(1)} %collective-permute-done.9.got_ref, bf16[32,3,96,96]{3,2,1,0:T(8,128)(2,1)S(1)} %copy-done, s32[3,32]{1,0:T(4,128)S(1)} %bitcast.7, ...), custom_call_target="tpu_custom_call" | custom-call | flops 603979776 | bytes 9437568 | tf_op jit(solution)/shard_map/pallas_call | solution.py:26
  28.0 1.3 %shard_map.94 = (bf16[1536,128]{1,0:T(8,128)(2,1)S(1)}, f32[32,1024]{1,0:T(8,128)S(1)}, bf16[32,1024]{1,0:T(8,128)(2,1)S(1)}, bf16[32,1024]{1,0:T(8,128)(2,1)S(1)}, bf16[32,1024]{1,0:T(8,128)(2,1)S(1)}) custom-call(bf16[3072,128]{1,0:T(8,128)(2,1)S(1)} %get-tuple-element.54.loads_ref, bf16[768,128]{1,0:T(8,128)(2,1)S(1)} %collective-permute-done.8.got_ref, ...), custom_call_target="tpu_custom_call" | custom-call | flops 201326592 | bytes 9765248 | tf_op jit(solution)/shard_map/pallas_call | solution.py:26
  29.3 3.6 %collective-permute-start.10 = (bf16[32,1024]{1,0:T(8,128)(2,1)S(1)}, bf16[32,1024]{1,0:T(8,128)(2,1)S(1)}, u32[]{:S(2)}, u32[]{:S(2)}) collective-permute-start(bf16[32,1024]{1,0:T(8,128)(2,1)S(1)} %get-tuple-element.59), channel_id=1, source_target_pairs={{0,1},{1,2},{2,3},{3,0},{4,5},{5,6},{6,7},{7,4},{8,9},{9,10},{10,1... | collective-permute-start | bytes 196616 | tf_op jit(solution)/shard_map/ppermute | solution.py:381
  32.9 2.4 %collective-permute-start.11 = (bf16[32,1024]{1,0:T(8,128)(2,1)S(1)}, bf16[32,1024]{1,0:T(8,128)(2,1)S(1)}, u32[]{:S(2)}, u32[]{:S(2)}) collective-permute-start(bf16[32,1024]{1,0:T(8,128)(2,1)S(1)} %get-tuple-element.60), channel_id=1, source_target_pairs={{0,2},{1,3},{2,0},{3,1},{4,6},{5,7},{6,4},{7,5},{8,10},{9,11},{10,... | collective-permute-start | bytes 196616 | tf_op jit(solution)/shard_map/ppermute | solution.py:381
  35.3 1.4 %collective-permute-start.12 = (bf16[32,1024]{1,0:T(8,128)(2,1)S(1)}, bf16[32,1024]{1,0:T(8,128)(2,1)S(1)}, u32[]{:S(2)}, u32[]{:S(2)}) collective-permute-start(bf16[32,1024]{1,0:T(8,128)(2,1)S(1)} %get-tuple-element.61), channel_id=1, source_target_pairs={{0,3},{1,0},{2,1},{3,2},{4,7},{5,4},{6,5},{7,6},{8,11},{9,8},{10,9... | collective-permute-start | bytes 196616 | tf_op jit(solution)/shard_map/ppermute | solution.py:381
  36.7 1.0 %collective-permute-done.11.two_ref = bf16[32,1024]{1,0:T(8,128)(2,1)S(1)} collective-permute-done((bf16[32,1024]{1,0:T(8,128)(2,1)S(1)}, bf16[32,1024]{1,0:T(8,128)(2,1)S(1)}, u32[]{:S(2)}, u32[]{:S(2)}) %collective-permute-start.11) | collective-permute-done | bytes 65568 | tf_op jit(solution)/shard_map/ppermute | solution.py:381
  37.8 0.9 %collective-permute-done.12.three_ref = bf16[32,1024]{1,0:T(8,128)(2,1)S(1)} collective-permute-done((bf16[32,1024]{1,0:T(8,128)(2,1)S(1)}, bf16[32,1024]{1,0:T(8,128)(2,1)S(1)}, u32[]{:S(2)}, u32[]{:S(2)}) %collective-permute-start.12) | collective-permute-done | bytes 65568 | tf_op jit(solution)/shard_map/ppermute | solution.py:381
  38.6 1.8 %collective-permute-start.15 = (bf16[32,1024]{1,0:T(8,128)(2,1)S(1)}, bf16[32,1024]{1,0:T(8,128)(2,1)S(1)}, u32[]{:S(2)}, u32[]{:S(2)}) collective-permute-start(bf16[32,1024]{1,0:T(8,128)(2,1)S(1)} %get-tuple-element.63), channel_id=1, source_target_pairs={{0,4},{1,5},{2,6},{3,7},{4,8},{5,9},{6,10},{7,11},{8,12},{9,13},{1... | collective-permute-start | bytes 196616 | tf_op jit(solution)/shard_map/ppermute | solution.py:394
  40.4 1.7 %collective-permute-start.14 = (bf16[32,1024]{1,0:T(8,128)(2,1)S(1)}, bf16[32,1024]{1,0:T(8,128)(2,1)S(1)}, u32[]{:S(2)}, u32[]{:S(2)}) collective-permute-start(bf16[32,1024]{1,0:T(8,128)(2,1)S(1)} %get-tuple-element.63), channel_id=1, source_target_pairs={{0,8},{1,9},{2,10},{3,11},{4,12},{5,13},{6,14},{7,15},{8,0},{9,1},... | collective-permute-start | bytes 196616 | tf_op jit(solution)/shard_map/ppermute | solution.py:394
  42.1 2.6 %collective-permute-start.13 = (bf16[32,1024]{1,0:T(8,128)(2,1)S(1)}, bf16[32,1024]{1,0:T(8,128)(2,1)S(1)}, u32[]{:S(2)}, u32[]{:S(2)}) collective-permute-start(bf16[32,1024]{1,0:T(8,128)(2,1)S(1)} %get-tuple-element.63), channel_id=1, source_target_pairs={{0,12},{1,13},{2,14},{3,15},{4,0},{5,1},{6,2},{7,3},{8,4},{9,5},{1... | collective-permute-start | bytes 196616 | tf_op jit(solution)/shard_map/ppermute | solution.py:394
  44.7 1.3 %shard_map.96 = (bf16[1024,1024]{1,0:T(8,128)(2,1)S(1)}, bf16[1024,1024]{1,0:T(8,128)(2,1)S(1)}) custom-call(f32[1024,1024]{1,0:T(8,128)S(1)} %copy-done.1), custom_call_target="tpu_custom_call" | custom-call | flops 4194304 | bytes 4194304 | tf_op jit(solution)/shard_map/pallas_call | solution.py:26
  46.0 1.9 %collective-permute-done.14.refs_1_ = bf16[32,1024]{1,0:T(8,128)(2,1)S(1)} collective-permute-done((bf16[32,1024]{1,0:T(8,128)(2,1)S(1)}, bf16[32,1024]{1,0:T(8,128)(2,1)S(1)}, u32[]{:S(2)}, u32[]{:S(2)}) %collective-permute-start.14) | collective-permute-done | bytes 65568 | tf_op jit(solution)/shard_map/ppermute | solution.py:394
  48.7 1.7 %collective-permute-start.16 = (bf16[32,1024]{1,0:T(8,128)(2,1)S(1)}, bf16[32,1024]{1,0:T(8,128)(2,1)S(1)}, u32[]{:S(2)}, u32[]{:S(2)}) collective-permute-start(bf16[32,1024]{1,0:T(8,128)(2,1)S(1)} %shard_map.97.own_ref), channel_id=1, source_target_pairs={{0,2},{1,3},{2,0},{3,1},{4,6},{5,7},{6,4},{7,5},{8,10},{9,11},{10,... | collective-permute-start | bytes 196616 | tf_op jit(solution)/shard_map/ppermute | solution.py:378
  50.4 2.0 %shard_map.98 = (bf16[1024,3072]{1,0:T(8,128)(2,1)S(1)}, bf16[128,3072]{1,0:T(8,128)(2,1)S(1)}) custom-call(bf16[3072,1024]{1,0:T(8,128)(2,1)S(1)} %bitcast.5, bf16[1536,128]{1,0:T(8,128)(2,1)S(1)} %get-tuple-element.55.mid_ref, bf16[1536,128]{1,0:T(8,128)(2,1)S(1)} %get-tuple-element.66.edge_ref), custom_call_target="tpu_custom_call" | custom-call | bytes 7077888 | tf_op jit(solution)/shard_map/pallas_call | solution.py:26
  54.3 1.9 %shard_map.99 = (bf16[3072,128]{1,0:T(8,128)(2,1)}, f32[24,128]{1,0:T(8,128)}) custom-call(bf16[32,1024]{1,0:T(8,128)(2,1)S(1)} %shard_map.97.own_ref, bf16[32,1024]{1,0:T(8,128)(2,1)S(1)} %collective-permute-done.16.y_ref, bf16[32,1024]{1,0:T(8,128)(2,1)S(1)} %collective-permute-done.17.core_ref, bf16[32,1024]{1,0:T(8,128)(2,1)S(1)} %collective-permute-done.18.both_ref, ...), custom_call_target="tpu_custom_call" | custom-call | flops 805306368 | bytes 7340032 | tf_op jit(solution)/shard_map/pallas_call | solution.py:26
  (39 shorter events, 7.7 us)
Async XLA Ops:
  2.9 1.7 %collective-permute-start = (bf16[8,144,128]{2,1,0:T(8,128)(2,1)S(1)}, bf16[8,144,128]{2,1,0:T(8,128)(2,1)S(1)}, u32[]{:S(2)}, u32[]{:S(2)}) collective-permute-start(bf16[8,144,128]{2,1,0:T(8,128)(2,1)S(1)} %get-tuple-element.42), channel_id=1, source_target_pairs={{0,1},{1,0},{2,3},{3,2},{4,5},{5,4},{6,7},{7,6},{8,9},{9,8},{10,11... | collective-permute-start | bytes 884744 | tf_op jit(solution)/shard_map/ppermute | solution.py:378
  4.7 10.2 %collective-permute-start.1 = (bf16[272,128]{1,0:T(8,128)(2,1)S(1)}, bf16[272,128]{1,0:T(8,128)(2,1)S(1)}, u32[]{:S(2)}, u32[]{:S(2)}) collective-permute-start(bf16[272,128]{1,0:T(8,128)(2,1)S(1)} %get-tuple-element.44), channel_id=1, source_target_pairs={{0,10},{1,11},{2,8},{3,9},{4,14},{5,15},{6,12},{7,13},{8,2},{9,3},... | collective-permute-start | bytes 208904 | tf_op jit(solution)/shard_map/ppermute | solution.py:394
  9.7 7.5 %collective-permute-start.2 = (bf16[272,128]{1,0:T(8,128)(2,1)S(1)}, bf16[272,128]{1,0:T(8,128)(2,1)S(1)}, u32[]{:S(2)}, u32[]{:S(2)}) collective-permute-start(bf16[272,128]{1,0:T(8,128)(2,1)S(1)} %get-tuple-element.45), channel_id=1, source_target_pairs={{0,6},{1,7},{2,4},{3,5},{4,10},{5,11},{6,8},{7,9},{8,14},{9,15},{1... | collective-permute-start | bytes 208904 | tf_op jit(solution)/shard_map/ppermute | solution.py:394
  11.2 7.6 %collective-permute-start.3 = (bf16[272,128]{1,0:T(8,128)(2,1)S(1)}, bf16[272,128]{1,0:T(8,128)(2,1)S(1)}, u32[]{:S(2)}, u32[]{:S(2)}) collective-permute-start(bf16[272,128]{1,0:T(8,128)(2,1)S(1)} %get-tuple-element.46), channel_id=1, source_target_pairs={{0,14},{1,15},{2,12},{3,13},{4,2},{5,3},{6,0},{7,1},{8,6},{9,7},{1... | collective-permute-start | bytes 208904 | tf_op jit(solution)/shard_map/ppermute | solution.py:394
  14.4 6.2 %collective-permute-start.4 = (bf16[272,128]{1,0:T(8,128)(2,1)S(1)}, bf16[272,128]{1,0:T(8,128)(2,1)S(1)}, u32[]{:S(2)}, u32[]{:S(2)}) collective-permute-start(bf16[272,128]{1,0:T(8,128)(2,1)S(1)} %get-tuple-element.47), channel_id=1, source_target_pairs={{0,2},{1,3},{2,0},{3,1},{4,6},{5,7},{6,4},{7,5},{8,10},{9,11},{10,... | collective-permute-start | bytes 208904 | tf_op jit(solution)/shard_map/ppermute | solution.py:394
  14.9 7.1 %collective-permute-start.5 = (bf16[272,128]{1,0:T(8,128)(2,1)S(1)}, bf16[272,128]{1,0:T(8,128)(2,1)S(1)}, u32[]{:S(2)}, u32[]{:S(2)}) collective-permute-start(bf16[272,128]{1,0:T(8,128)(2,1)S(1)} %get-tuple-element.48), channel_id=1, source_target_pairs={{0,8},{1,9},{2,10},{3,11},{4,12},{5,13},{6,14},{7,15},{8,0},{9,1},... | collective-permute-start | bytes 208904 | tf_op jit(solution)/shard_map/ppermute | solution.py:394
  14.9 7.1 %collective-permute-start.6 = (bf16[272,128]{1,0:T(8,128)(2,1)S(1)}, bf16[272,128]{1,0:T(8,128)(2,1)S(1)}, u32[]{:S(2)}, u32[]{:S(2)}) collective-permute-start(bf16[272,128]{1,0:T(8,128)(2,1)S(1)} %get-tuple-element.49), channel_id=1, source_target_pairs={{0,4},{1,5},{2,6},{3,7},{4,8},{5,9},{6,10},{7,11},{8,12},{9,13},{1... | collective-permute-start | bytes 208904 | tf_op jit(solution)/shard_map/ppermute | solution.py:394
  17.1 5.1 %collective-permute-start.7 = (bf16[272,128]{1,0:T(8,128)(2,1)S(1)}, bf16[272,128]{1,0:T(8,128)(2,1)S(1)}, u32[]{:S(2)}, u32[]{:S(2)}) collective-permute-start(bf16[272,128]{1,0:T(8,128)(2,1)S(1)} %get-tuple-element.50), channel_id=1, source_target_pairs={{0,12},{1,13},{2,14},{3,15},{4,0},{5,1},{6,2},{7,3},{8,4},{9,5},{1... | collective-permute-start | bytes 208904 | tf_op jit(solution)/shard_map/ppermute | solution.py:394
  18.7 7.5 %slice-start = ((s8[6291456]{0:T(1024)(128)(4,1)}), s8[4194304]{0:T(1024)(128)(4,1)S(1)}, s32[]{:S(2)}) async-start(s8[6291456]{0:T(1024)(128)(4,1)} %bitcast.4), calls=%async_computation | async-start | bytes 8388608
  20.5 3.6 %copy-start.2 = (s32[32,3]{0,1:T(4,128)S(1)}, s32[32,3]{0,1:T(4,128)}, u32[]{:S(2)}) copy-start(s32[32,3]{0,1:T(4,128)} %param.11) | copy-start | bytes 1156
  20.5 5.7 %slice-start.1 = ((s8[6291456]{0:T(1024)(128)(4,1)}), s8[2097152]{0:T(1024)(128)(4,1)S(1)}, s32[]{:S(2)}) async-start(s8[6291456]{0:T(1024)(128)(4,1)} %bitcast.4), calls=%async_computation.1 | async-start | bytes 4194304
  22.3 1.9 %copy-start = (bf16[32,3,96,96]{3,2,1,0:T(8,128)(2,1)S(1)}, bf16[32,3,96,96]{3,2,1,0:T(8,128)(2,1)}, u32[]{:S(2)}) copy-start(bf16[32,3,96,96]{3,2,1,0:T(8,128)(2,1)} %stiff_ref.5) | copy-start | bytes 5308420
  23.4 2.8 %collective-permute-start.9 = (bf16[768,128]{1,0:T(8,128)(2,1)S(1)}, bf16[768,128]{1,0:T(8,128)(2,1)S(1)}, u32[]{:S(2)}, u32[]{:S(2)}) collective-permute-start(bf16[768,128]{1,0:T(8,128)(2,1)S(1)} %shard_map.91.near_ref), channel_id=1, source_target_pairs={{0,1},{1,0},{2,3},{3,2},{4,5},{5,4},{6,7},{7,6},{8,9},{9,8},{10,11... | collective-permute-start | bytes 589832 | tf_op jit(solution)/shard_map/ppermute | solution.py:378
  23.5 4.5 %collective-permute-start.8 = (bf16[768,128]{1,0:T(8,128)(2,1)S(1)}, bf16[768,128]{1,0:T(8,128)(2,1)S(1)}, u32[]{:S(2)}, u32[]{:S(2)}) collective-permute-start(bf16[768,128]{1,0:T(8,128)(2,1)S(1)} %get-tuple-element.53.far_ref), channel_id=1, source_target_pairs={{1,2},{3,4},{5,6},{7,8},{9,10},{11,12},{13,14},{2,1},{4,3},{6,5},{... | collective-permute-start | bytes 589832 | tf_op jit(solution)/shard_map/ppermute | solution.py:387
  28.0 16.7 %copy-start.1 = (f32[1024,1024]{1,0:T(8,128)S(1)}, f32[1024,1024]{1,0:T(8,128)}, u32[]{:S(2)}) copy-start(f32[1024,1024]{1,0:T(8,128)} %a_ref.1) | copy-start | bytes 12582916
  29.3 7.4 %collective-permute-start.10 = (bf16[32,1024]{1,0:T(8,128)(2,1)S(1)}, bf16[32,1024]{1,0:T(8,128)(2,1)S(1)}, u32[]{:S(2)}, u32[]{:S(2)}) collective-permute-start(bf16[32,1024]{1,0:T(8,128)(2,1)S(1)} %get-tuple-element.59), channel_id=1, source_target_pairs={{0,1},{1,2},{2,3},{3,0},{4,5},{5,6},{6,7},{7,4},{8,9},{9,10},{10,1... | collective-permute-start | bytes 196616 | tf_op jit(solution)/shard_map/ppermute | solution.py:381
  32.9 4.9 %collective-permute-start.11 = (bf16[32,1024]{1,0:T(8,128)(2,1)S(1)}, bf16[32,1024]{1,0:T(8,128)(2,1)S(1)}, u32[]{:S(2)}, u32[]{:S(2)}) collective-permute-start(bf16[32,1024]{1,0:T(8,128)(2,1)S(1)} %get-tuple-element.60), channel_id=1, source_target_pairs={{0,2},{1,3},{2,0},{3,1},{4,6},{5,7},{6,4},{7,5},{8,10},{9,11},{10,... | collective-permute-start | bytes 196616 | tf_op jit(solution)/shard_map/ppermute | solution.py:381
  35.3 3.3 %collective-permute-start.12 = (bf16[32,1024]{1,0:T(8,128)(2,1)S(1)}, bf16[32,1024]{1,0:T(8,128)(2,1)S(1)}, u32[]{:S(2)}, u32[]{:S(2)}) collective-permute-start(bf16[32,1024]{1,0:T(8,128)(2,1)S(1)} %get-tuple-element.61), channel_id=1, source_target_pairs={{0,3},{1,0},{2,1},{3,2},{4,7},{5,4},{6,5},{7,6},{8,11},{9,8},{10,9... | collective-permute-start | bytes 196616 | tf_op jit(solution)/shard_map/ppermute | solution.py:381
  38.6 7.4 %collective-permute-start.15 = (bf16[32,1024]{1,0:T(8,128)(2,1)S(1)}, bf16[32,1024]{1,0:T(8,128)(2,1)S(1)}, u32[]{:S(2)}, u32[]{:S(2)}) collective-permute-start(bf16[32,1024]{1,0:T(8,128)(2,1)S(1)} %get-tuple-element.63), channel_id=1, source_target_pairs={{0,4},{1,5},{2,6},{3,7},{4,8},{5,9},{6,10},{7,11},{8,12},{9,13},{1... | collective-permute-start | bytes 196616 | tf_op jit(solution)/shard_map/ppermute | solution.py:394
  40.4 7.5 %collective-permute-start.14 = (bf16[32,1024]{1,0:T(8,128)(2,1)S(1)}, bf16[32,1024]{1,0:T(8,128)(2,1)S(1)}, u32[]{:S(2)}, u32[]{:S(2)}) collective-permute-start(bf16[32,1024]{1,0:T(8,128)(2,1)S(1)} %get-tuple-element.63), channel_id=1, source_target_pairs={{0,8},{1,9},{2,10},{3,11},{4,12},{5,13},{6,14},{7,15},{8,0},{9,1},... | collective-permute-start | bytes 196616 | tf_op jit(solution)/shard_map/ppermute | solution.py:394
  42.1 5.8 %collective-permute-start.13 = (bf16[32,1024]{1,0:T(8,128)(2,1)S(1)}, bf16[32,1024]{1,0:T(8,128)(2,1)S(1)}, u32[]{:S(2)}, u32[]{:S(2)}) collective-permute-start(bf16[32,1024]{1,0:T(8,128)(2,1)S(1)} %get-tuple-element.63), channel_id=1, source_target_pairs={{0,12},{1,13},{2,14},{3,15},{4,0},{5,1},{6,2},{7,3},{8,4},{9,5},{1... | collective-permute-start | bytes 196616 | tf_op jit(solution)/shard_map/ppermute | solution.py:394
  48.7 4.3 %collective-permute-start.16 = (bf16[32,1024]{1,0:T(8,128)(2,1)S(1)}, bf16[32,1024]{1,0:T(8,128)(2,1)S(1)}, u32[]{:S(2)}, u32[]{:S(2)}) collective-permute-start(bf16[32,1024]{1,0:T(8,128)(2,1)S(1)} %shard_map.97.own_ref), channel_id=1, source_target_pairs={{0,2},{1,3},{2,0},{3,1},{4,6},{5,7},{6,4},{7,5},{8,10},{9,11},{10,... | collective-permute-start | bytes 196616 | tf_op jit(solution)/shard_map/ppermute | solution.py:378
  52.5 1.3 %collective-permute-start.17 = (bf16[32,1024]{1,0:T(8,128)(2,1)S(1)}, bf16[32,1024]{1,0:T(8,128)(2,1)S(1)}, u32[]{:S(2)}, u32[]{:S(2)}) collective-permute-start(bf16[32,1024]{1,0:T(8,128)(2,1)S(1)} %shard_map.97.own_ref), channel_id=1, source_target_pairs={{0,1},{1,0},{2,3},{3,2},{4,5},{5,4},{6,7},{7,6},{8,9},{9,8},{10,11... | collective-permute-start | bytes 196616 | tf_op jit(solution)/shard_map/ppermute | solution.py:378
  53.0 1.3 %collective-permute-start.18 = (bf16[32,1024]{1,0:T(8,128)(2,1)S(1)}, bf16[32,1024]{1,0:T(8,128)(2,1)S(1)}, u32[]{:S(2)}, u32[]{:S(2)}) collective-permute-start(bf16[32,1024]{1,0:T(8,128)(2,1)S(1)} %collective-permute-done.16.y_ref), channel_id=1, source_target_pairs={{0,1},{1,0},{2,3},{3,2},{4,5},{5,4},{6,7},{7,6},{8,9},{9,8},{10,11... | collective-permute-start | bytes 196616 | tf_op jit(solution)/shard_map/ppermute | solution.py:378
